TPU v7x, 1024 devices: a whole 8x8x8 slice. The times are simulated.
1024 devices in a mesh: grp: 2 (over y_lo), dp: 32 (over y_hi, z), blk: 16 (over x, core).
Axes of the slice: x: 8, y: 8 (y_hi: 4, y_lo: 2; y = y_hi * 2 + y_lo), z: 8, core: 2. Of those that a mesh axis runs over, the one named last changes fastest.
Arguments:
- layer_input: bfloat16 [64, 2048, 3584], P(('grp', 'dp'), 'blk'), may hold values from -16 to 16
- queries: bfloat16 [64, 2048, 1792], P(('grp', 'dp'), 'blk'), may hold values from -8 to 8
- keys: bfloat16 [64, 2048, 256], P(('grp', 'dp'), 'blk'), may hold values from -8 to 8
- d_out: bfloat16 [64, 2048, 1792], P(('grp', 'dp'), 'blk'), may hold values from -6 to 6
- doc_start: int32 [64, 2048], P(('grp', 'dp'), 'blk'), may hold values from 0 to 2047, as said below
- moment_m: float32 [3584, 256], P(('grp', 'dp'), 'blk'), may hold values from -0.3 to 0.3
- moment_v: float32 [3584, 256], P(('grp', 'dp'), 'blk'), may hold values from 0.001 to 0.01
Outputs:
- new_m: float32 [3584, 256], P(('grp', 'dp'), 'blk')
- new_v: float32 [3584, 256], P(('grp', 'dp'), 'blk')
- update: float32 [3584, 256], P(('grp', 'dp'), 'blk')
Inputs may be any that keep to these rules, and one draw needn't show every extreme that they name: `doc_start`: the first 32 slots hold one document each; each other slot holds 16 sequences of 128 tokens, positions k * 128 to (k + 1) * 128 - 1, in which documents are consecutive runs of 1 to 64 tokens, the first exactly 64 long, the last a single token.
All inputs are finite; a program needn't handle non-finite values.
Results may differ from a plain program's by a relative error of at most 0.0071.
Values may be sent and summed in bfloat16 or wider, within the bound.
No kernel may reach another device: no remote copies, remote signals or barrier semaphores. Data moves between devices by JAX's collectives and lax.ppermute only.
A program may use at most 32 MiB of HBM per device.

v0:
```python
import math

import jax
import jax.numpy as jnp
from jax import lax
from jax.sharding import PartitionSpec as P

KV_HEADS = 2
HD = 128
STEP = 10
GROUP = 7


masked_score = -1e30


def block_scores(q_heads, key_block, key_start, doc_begin, query_pos):
    span_rows = key_block.shape[0]
    key_mat = key_block.reshape(span_rows, KV_HEADS, HD)
    scores = jnp.einsum(
        "rgph,kgh->gprk", q_heads, key_mat, preferred_element_type=jnp.float32
    ) * HD ** (-0.5)
    key_pos = key_start + jnp.arange(span_rows, dtype=jnp.int32)
    visible = (key_pos[None, :] >= doc_begin[:, None]) & (key_pos[None, :] <= query_pos[:, None])
    return (scores, visible)


def body(layer_input, queries, keys, d_out, doc_start, moment_m, moment_v):
    local_rows = queries.shape[1]
    cycle_size = lax.axis_size("blk")
    cycle_index = lax.axis_index("blk")
    query_pos = cycle_index * local_rows + jnp.arange(local_rows, dtype=jnp.int32)
    doc_begin = doc_start[0]
    q_heads = queries[0].reshape(local_rows, KV_HEADS, GROUP, HD)
    d_heads = d_out[0].reshape(local_rows, KV_HEADS, GROUP, HD)
    all_keys = lax.all_gather(keys[0], "blk", axis=0, tiled=True)
    seq_rows = all_keys.shape[0]
    block_rows = math.gcd(seq_rows, 512)

    def merge_block(running, block_index):
        key_start = block_index * block_rows
        key_block = lax.dynamic_slice_in_dim(all_keys, key_start, block_rows, 0)
        scores, visible = block_scores(q_heads, key_block, key_start, doc_begin, query_pos)
        scores = jnp.where(visible, scores, masked_score)
        new_max = jnp.maximum(running[0], jnp.max(scores, axis=-1))
        weights = jnp.where(visible, jnp.exp(scores - new_max[..., None]), 0.0)
        running = (new_max, running[1] * jnp.exp(running[0] - new_max) + jnp.sum(weights, axis=-1))
        return (running, None)

    start_state = (
        jnp.full((KV_HEADS, GROUP, local_rows), masked_score, jnp.float32),
        jnp.zeros((KV_HEADS, GROUP, local_rows), jnp.float32),
    )
    running, unused = lax.scan(
        merge_block, start_state, jnp.arange(seq_rows // block_rows, dtype=jnp.int32)
    )
    log_total = running[0] + jnp.log(running[1])
    step_rows = math.gcd(local_rows * lax.axis_size("blk"), 512)

    def one_block(block_index):
        key_start = block_index * step_rows
        key_block = lax.dynamic_slice_in_dim(all_keys, key_start, step_rows, 0)
        scores, visible = block_scores(q_heads, key_block, key_start, doc_begin, query_pos)
        shifted = jnp.where(visible, scores - log_total[..., None], masked_score)
        probs = jnp.where(visible, jnp.exp(shifted), 0.0).astype(jnp.bfloat16)
        summed = jnp.einsum("gprk,rgph->kgh", probs, d_heads, preferred_element_type=jnp.float32)
        return summed.reshape(step_rows, KV_HEADS * HD)

    pieces = lax.map(
        one_block, jnp.arange(local_rows * lax.axis_size("blk") // step_rows, dtype=jnp.int32)
    )
    value_grad = lax.psum_scatter(
        pieces.reshape(local_rows * lax.axis_size("blk"), KV_HEADS * HD),
        "blk",
        scatter_dimension=0,
        tiled=True,
    ).astype(jnp.bfloat16)
    token_mat = layer_input[0]
    owner_count = lax.axis_size("grp") * lax.axis_size("dp")
    scale_all = 1.0 / math.sqrt(owner_count * cycle_size * local_rows)
    partial_grad = jnp.einsum(
        "rd,rc->dc", token_mat, value_grad, preferred_element_type=jnp.float32
    )
    gradient = lax.psum_scatter(partial_grad, "blk", scatter_dimension=1, tiled=True)
    gradient = lax.psum_scatter(gradient, ("grp", "dp"), scatter_dimension=0, tiled=True)
    gradient = gradient * scale_all
    new_m = 0.9 * moment_m + 0.1 * gradient
    new_v = 0.95 * moment_v + 0.05 * gradient * gradient
    update = new_m / (1.0 - 0.9**STEP) / (jnp.sqrt(new_v / (1.0 - 0.95**STEP)) + 1e-08)
    return (new_m, new_v, update)


def solution(mesh):
    in_specs = (
        P(("grp", "dp"), "blk", None),
        P(("grp", "dp"), "blk", None),
        P(("grp", "dp"), "blk", None),
        P(("grp", "dp"), "blk", None),
        P(("grp", "dp"), "blk"),
        P(("grp", "dp"), "blk"),
        P(("grp", "dp"), "blk"),
    )
    out_specs = (P(("grp", "dp"), "blk"), P(("grp", "dp"), "blk"), P(("grp", "dp"), "blk"))
    return jax.shard_map(body, mesh=mesh, in_specs=in_specs, out_specs=out_specs, check_vma=False)
```

profile of v0, /device:TPU:2, one launch (start us, length us, event | category | flops | bytes accessed | tf_op | source)
XLA Modules:
  0.0 433.3 jit_solution(3919169673212003597)
XLA Ops:
  7.2 1.6 copy.32
  9.0 1.3 copy.33
  10.5 1.3 copy.35
  11.8 53.3 %all-gather.3.cloned.1.call-done = bf16[1,2048,256]{1,2,0:T(8,128)(2,1)} async-done(((bf16[1,128,256]{1,2,0:T(8,128)(2,1)}), bf16[1,2048,256]{1,2,0:T(8,128)(2,1)}) %all-gather.3.cloned.1.call-update) | async-done | bytes 1048592 | tf_op jit(solution)/shard_map/all_gather | solution.py:36
  65.1 34.2 %while.25 = (s32[]{:T(128)}, f32[2,7,128]{2,1,0:T(8,128)S(1)}, f32[2,7,128]{2,1,0:T(8,128)S(1)}, s32[4]{0:T(128)S(1)}, s32[1,128]{1,0:T(1,128)}, /*index=5*/bf16...) while((s32[]{:T(128)}, f32[2,7,128]{2,1,0:T(8,128)S(1)}, ...), condition=%wide.region_3.4_spmd.clone, body=%wide.region_0.3_spmd.clone.sunk | while | flops 242427264 | bytes 8880838 | solution.py:54
  65.1 0.6 dynamic_slice.26
  66.3 1.0 constant_dynamic-slice_fusion.5
  67.3 0.8 compare_and_fusion.5
  68.1 2.6 fusion.35
  70.7 2.9 select_reduce_fusion.2
  73.6 0.6 dynamic_slice.26
  74.8 1.0 constant_dynamic-slice_fusion.5
  75.8 0.8 compare_and_fusion.5
  76.6 2.6 fusion.35
  79.2 2.9 select_reduce_fusion.2
  82.2 0.6 dynamic_slice.26
  83.4 1.0 constant_dynamic-slice_fusion.5
  84.4 0.8 compare_and_fusion.5
  85.2 2.6 fusion.35
  87.8 2.9 select_reduce_fusion.2
  90.7 0.6 dynamic_slice.26
  91.9 1.0 constant_dynamic-slice_fusion.5
  92.9 0.8 compare_and_fusion.5
  93.7 2.6 fusion.35
  96.3 2.9 select_reduce_fusion.2
  99.3 22.8 %while.24 = (s32[]{:T(128)}, f32[4,512,256]{2,1,0:T(8,128)}, s32[4]{0:T(128)S(1)}, s32[1,128]{1,0:T(1,128)}, bf16[2048,256]{0,1:T(8,128)(2,1)}, /*index=5*/bf16[...) while((s32[]{:T(128)}, f32[4,512,256]{2,1,0:T(8,128)}, ...), condition=%wide.region_5.6_spmd.clone, body=%wide.region_4.5_spmd.clone.sunk | while | flops 474546816 | bytes 4469955 | solution.py:69
  100.5 1.0 constant_dynamic-slice_fusion.4
  101.5 0.8 compare_and_fusion.4
  102.3 1.6 fusion.32
  104.1 0.8 constant_dynamic-update-slice_fusion.2
  106.2 1.0 constant_dynamic-slice_fusion.4
  107.2 0.8 compare_and_fusion.4
  108.0 1.6 fusion.32
  109.8 0.9 constant_dynamic-update-slice_fusion.2
  111.9 1.0 constant_dynamic-slice_fusion.4
  112.9 0.8 compare_and_fusion.4
  113.7 1.6 fusion.32
  115.5 0.9 constant_dynamic-update-slice_fusion.2
  117.6 1.0 constant_dynamic-slice_fusion.4
  118.6 0.8 compare_and_fusion.4
  119.4 1.6 fusion.32
  121.2 0.9 constant_dynamic-update-slice_fusion.2
  122.2 60.7 %reduce-scatter.4.cloned.1.call-done = f32[128,256]{1,0:T(8,128)} async-done(((f32[2048,256]{1,0:T(8,128)}), f32[128,256]{1,0:T(8,128)}) %reduce-scatter.4.cloned.1.call-update) | async-done | bytes 131088 | tf_op jit(solution)/shard_map/reduce_scatter | solution.py:72
  182.9 3.4 convolution_bitcast_fusion
  186.3 66.5 %reduce-scatter.6.cloned.1.call-done = f32[3584,16]{0,1:T(8,128)} async-done(((f32[3584,256]{0,1:T(8,128)}), f32[3584,16]{0,1:T(8,128)}) %reduce-scatter.6.cloned.1.call-update) | async-done | bytes 229392 | tf_op jit(solution)/shard_map/reduce_scatter | solution.py:84
  252.9 1.3 dynamic-slice
  254.8 170.5 %all-reduce.3.cloned.1.call-done = f32[3584,16]{0,1:T(8,128)} async-done(((f32[3584,16]{0,1:T(8,128)}), f32[3584,16]{0,1:T(8,128)}) %all-reduce.3.cloned.1.call-update) | async-done | bytes 229392
  425.4 1.4 add_divide_fusion
  (57 shorter events, 3.8 us)
Async XLA Ops:
  7.2 175.7 %copy-start = (bf16[1,128,3584]{2,1,0:T(8,128)(2,1)S(1)}, bf16[1,128,3584]{2,1,0:T(8,128)(2,1)}, u32[]{:S(2)}) copy-start(bf16[1,128,3584]{2,1,0:T(8,128)(2,1)} %param.11) | copy-start | bytes 2752516
  7.2 57.9 %all-gather.3.cloned.1.call-start = ((), (), s32[]{:S(2)}) async-start(), calls=%async_computation.4 | async-start | bytes 1114112 | tf_op jit(solution)/shard_map/all_gather | solution.py:36
  8.9 174.0 %reduce-scatter.4.cloned.1.call-start = ((), (), s32[]{:S(2)}) async-start(), calls=%async_computation.2 | async-start | bytes 2228224 | tf_op jit(solution)/shard_map/reduce_scatter | solution.py:72
  122.1 303.3 %copy-start.1 = (f32[56,16]{0,1:T(8,128)S(1)}, f32[56,16]{0,1:T(8,128)}, u32[]{:S(2)}) copy-start(f32[56,16]{0,1:T(8,128)} %param.17) | copy-start | bytes 10756
  122.1 303.3 %copy-start.2 = (f32[56,16]{0,1:T(8,128)S(1)}, f32[56,16]{0,1:T(8,128)}, u32[]{:S(2)}) copy-start(f32[56,16]{0,1:T(8,128)} %param.16) | copy-start | bytes 10756
  122.1 130.8 %reduce-scatter.6.cloned.1.call-start = ((), (), s32[]{:S(2)}) async-start(), calls=%async_computation.3 | async-start | bytes 3899392 | tf_op jit(solution)/shard_map/reduce_scatter | solution.py:84
  186.3 239.1 %all-reduce.3.cloned.1.call-start = ((), (), s32[]{:S(2)}) async-start(), calls=%async_computation.5 | async-start | bytes 458752
Sparse Core Ops, SparseCore 0:
  10.6 54.3 all-gather.2
  122.2 60.6 reduce-scatter.3
  186.4 66.4 reduce-scatter.5
  255.9 169.3 all-reduce.2
where the time goes:
time: 434 us; the launch traced here: 433 us
  waiting for transfers between devices  351 us (81%)
  local copies, waits for them, and re-layouts  22.4 us (5%)
  matrix products  20 us (5%)
  other arithmetic  19.5 us (4%)
  between operations  14.5 us (3%)
  loops' own time  5.53 us (1%)
    unnamed x5, waiting for transfers between devices  171 us
    reduce_scatter x1, waiting for transfers between devices, body(): lax.psum_scatter(partial_grad, 'blk', scatter_dimension=1, tiled=True)  66.5 us
    reduce_scatter x1, waiting for transfers between devices, body(): lax.psum_scatter(pieces.reshape(local_rows * lax.axis_size('blk'), KV_HEA...  60.7 us
    all_gather x1, waiting for transfers between devices, body(): all_keys = lax.all_gather(keys[0], 'blk', axis=0, tiled=True)  53.3 us
    reduce_sum x4, other arithmetic, merge_block(): jnp.sum(weights, axis=-1)  11.6 us
    dot_general x4, matrix products, block_scores(): jnp.einsum('rgph,kgh->gprk', q_heads, key_mat, preferred_element_type=jnp...  10.3 us
  transfers between devices with their start and end apart: 4, of which 4 were waited for; matrix products, arithmetic and copies ran while one was open for 1% of the time, Pallas kernels for 0%

commit v1 on v0

v1 whole, which is shorter than its diff:
```python
import functools
import math

import jax
import jax.numpy as jnp
from jax import lax
from jax.experimental import pallas as pl
from jax.experimental.pallas import tpu as pltpu
from jax.sharding import PartitionSpec as P

KV_HEADS = 2
HD = 128
STEP = 10
GROUP = 7
CHUNK = 512
TILE = 512
masked_score = -1e30
WHOLE = pl.BlockSpec(memory_space=pltpu.VMEM)
SCALARS = pl.BlockSpec(memory_space=pltpu.SMEM)
PARAMS = pltpu.CompilerParams(vmem_limit_bytes=48 * 1024 * 1024)


def attention_kernel(place, begin, q, d, k0, k1, out, own, qs, ds, s):
    seq, rows_here = k0.shape[0], q.shape[0]
    width = GROUP * rows_here
    low, high, first_row = place[0], place[1], place[2]
    gain = HD ** (-0.5) * math.log2(math.e)
    for h in range(KV_HEADS * GROUP):
        g, r = divmod(h, GROUP)
        qs[g, r * rows_here : (r + 1) * rows_here, :] = q[:, h * HD : (h + 1) * HD]
        ds[g, r * rows_here : (r + 1) * rows_here, :] = d[:, h * HD : (h + 1) * HD]

    def chunk_rows(c):
        return pl.ds(pl.multiple_of(c * CHUNK, CHUNK), CHUNK)

    def clear(c, carry):
        @pl.when((c < low) | (c > high))
        def _():
            out[chunk_rows(c), :] = jnp.zeros((CHUNK, KV_HEADS * HD), out.dtype)

        return carry

    lax.fori_loop(0, seq // CHUNK, clear, 0)
    begin_all = jnp.concatenate([begin[...]] * GROUP, axis=1)
    query_pos = first_row + jnp.concatenate(
        [lax.broadcasted_iota(jnp.int32, (1, rows_here), 1)] * GROUP, axis=1
    )
    for g, k in enumerate((k0, k1)):
        cols = slice(g * HD, (g + 1) * HD)

        def scores(c):
            return gain * lax.dot_general(
                k[chunk_rows(c), :],
                qs[g],
                (((1,), (1,)), ((), ())),
                preferred_element_type=jnp.float32,
            )

        def larger(x, top):
            return jnp.maximum(top, jnp.max(x.reshape(CHUNK // 8, 8, width), axis=0))

        def inner(c, top):
            x = scores(c)
            s[chunk_rows(c), :] = x
            return larger(x, top)

        top = lax.fori_loop(low, high, inner, jnp.full((8, width), masked_score, jnp.float32))
        x = scores(high)
        key_pos = high * CHUNK + lax.broadcasted_iota(jnp.int32, (CHUNK, width), 0)
        x = jnp.where((key_pos >= begin_all) & (key_pos <= query_pos), x, masked_score)
        s[chunk_rows(high), :] = x
        top = jnp.max(larger(x, top), axis=0, keepdims=True)

        def weigh(c, total):
            p = jnp.exp2(s[chunk_rows(c), :] - top)
            return total + jnp.sum(p.reshape(CHUNK // 8, 8, width), axis=0)

        total = lax.fori_loop(low, high + 1, weigh, jnp.zeros((8, width), jnp.float32))
        shift = top + jnp.log2(jnp.sum(total, axis=0, keepdims=True))

        def collect(c):
            p = jnp.exp2(s[chunk_rows(c), :] - shift).astype(ds.dtype)
            block = jnp.dot(p, ds[g], preferred_element_type=jnp.float32)
            out[chunk_rows(c), cols] = block.astype(out.dtype)
            return block

        def inner_collect(c, carry):
            collect(c)
            return carry

        lax.fori_loop(low, high, inner_collect, 0)
        block = collect(high)
        for i in range(CHUNK // rows_here):

            @pl.when(first_row == high * CHUNK + i * rows_here)
            def _():
                own[:, cols] = block[i * rows_here : (i + 1) * rows_here]


def project_kernel(place, own, pieces, x, keep, send, vg):
    n, rows, cols = pieces.shape
    total = own[...]
    for i in range(n):
        total = total + jnp.where(place[1] == i, 0.0, pieces[i].astype(jnp.float32))
    vg[...] = jnp.transpose(total).astype(vg.dtype)

    def emit(even, odd):
        for t in range(x.shape[1] // TILE):
            part = slice(t * TILE, (t + 1) * TILE)
            block = jnp.dot(vg[...], x[:, part], preferred_element_type=jnp.float32)
            block = block.reshape(n // 2, 2, cols // n, TILE)
            even[:, :, part] = block[:, 0]
            odd[:, :, part] = block[:, 1]

    @pl.when(place[0] == 0)
    def _():
        emit(keep, send)

    @pl.when(place[0] == 1)
    def _():
        emit(send, keep)


def add_kernel(a, b, out):
    out[...] = (a[...] + b[...]).astype(out.dtype)


def fold_kernel(owners, pieces, out, total):
    acc = pieces[0].astype(jnp.float32)
    for i in range(1, pieces.shape[0]):
        acc = acc + pieces[i].astype(jnp.float32)
    total[...] = acc
    span = total.shape[1] // owners
    out[...] = jnp.zeros(out.shape, out.dtype)
    for r in range(owners):
        block = total[:, r * span : (r + 1) * span]
        out[r, :, :span] = block[:8]
        out[r, :, 64 : 64 + span] = block[8:]


def adam_kernel(scale, pieces, m, v, new_m, new_v, update):
    acc = pieces[0]
    for i in range(1, pieces.shape[0]):
        acc = acc + pieces[i]
    span = m.shape[1]
    gradient = jnp.concatenate([acc[:, :span], acc[:, 64 : 64 + span]], axis=0) * scale
    first = 0.9 * m[...] + 0.1 * gradient
    second = 0.95 * v[...] + 0.05 * gradient * gradient
    new_m[...] = first
    new_v[...] = second
    update[...] = first / (1.0 - 0.9**STEP) / (jnp.sqrt(second / (1.0 - 0.95**STEP)) + 1e-08)


def body(layer_input, queries, keys, d_out, doc_start, moment_m, moment_v):
    local_rows = queries.shape[1]
    cycle_size = lax.axis_size("blk")
    cycle_index = lax.axis_index("blk")
    owners = lax.axis_size("grp") * lax.axis_size("dp")
    seq = cycle_size * local_rows
    width, cols = layer_input.shape[2], KV_HEADS * HD
    bf16, f32 = jnp.bfloat16, jnp.float32

    k0 = lax.all_gather(keys[0, :, :HD], "blk", axis=0, tiled=True)
    k1 = lax.all_gather(keys[0, :, HD:], "blk", axis=0, tiled=True)
    high = cycle_index * local_rows // CHUNK
    low = jnp.where(lax.axis_index("grp") == 0, 0, high)
    place = jnp.stack([low, high, cycle_index * local_rows]).astype(jnp.int32)
    partial, own = pl.pallas_call(
        attention_kernel,
        out_shape=(
            jax.ShapeDtypeStruct((seq, cols), bf16),
            jax.ShapeDtypeStruct((local_rows, cols), f32),
        ),
        in_specs=[SCALARS] + [WHOLE] * 5,
        out_specs=(WHOLE, WHOLE),
        scratch_shapes=[
            pltpu.VMEM((KV_HEADS, GROUP * local_rows, HD), bf16),
            pltpu.VMEM((KV_HEADS, GROUP * local_rows, HD), bf16),
            pltpu.VMEM((seq, GROUP * local_rows), f32),
        ],
        compiler_params=PARAMS,
    )(place, doc_start, queries[0], d_out[0], k0, k1)
    pieces = lax.all_to_all(
        partial.reshape(cycle_size, local_rows, cols), "blk", 0, 0, tiled=True
    )

    chips, share = cycle_size // 2, cols // cycle_size
    seat = jnp.stack([lax.rem(cycle_index, 2), cycle_index]).astype(jnp.int32)
    half = jax.ShapeDtypeStruct((chips, share, width), f32)
    keep, send = pl.pallas_call(
        project_kernel,
        out_shape=(half, half),
        in_specs=[SCALARS, WHOLE, WHOLE, WHOLE],
        out_specs=(WHOLE, WHOLE),
        scratch_shapes=[pltpu.VMEM((cols, local_rows), bf16)],
        compiler_params=PARAMS,
    )(seat, own, pieces, layer_input[0])
    other = lax.ppermute(send, "blk", [(i, i ^ 1) for i in range(cycle_size)])
    both = pl.pallas_call(
        add_kernel,
        out_shape=jax.ShapeDtypeStruct((chips, share, width), bf16),
        in_specs=[WHOLE, WHOLE],
        out_specs=WHOLE,
        compiler_params=PARAMS,
    )(keep, other)
    lines = [[c + 2 * i for i in range(chips)] for c in range(2)]
    terms = lax.all_to_all(both, "blk", 0, 0, tiled=True, axis_index_groups=lines)
    sent = pl.pallas_call(
        functools.partial(fold_kernel, owners),
        out_shape=jax.ShapeDtypeStruct((owners, 8, 128), f32),
        in_specs=[WHOLE],
        out_specs=WHOLE,
        scratch_shapes=[pltpu.VMEM((share, width), f32)],
        compiler_params=PARAMS,
    )(terms)
    landed = lax.all_to_all(sent, ("grp", "dp"), 0, 0, tiled=True)
    result = jax.ShapeDtypeStruct(moment_m.shape[::-1], f32)
    outs = pl.pallas_call(
        functools.partial(adam_kernel, 1.0 / math.sqrt(owners * seq)),
        out_shape=(result,) * 3,
        in_specs=[WHOLE] * 3,
        out_specs=(WHOLE,) * 3,
        compiler_params=PARAMS,
    )(landed, moment_m.T, moment_v.T)
    return tuple(o.T for o in outs)


def solution(mesh):
    in_specs = (
        P(("grp", "dp"), "blk", None),
        P(("grp", "dp"), "blk", None),
        P(("grp", "dp"), "blk", None),
        P(("grp", "dp"), "blk", None),
        P(("grp", "dp"), "blk"),
        P(("grp", "dp"), "blk"),
        P(("grp", "dp"), "blk"),
    )
    out_specs = (P(("grp", "dp"), "blk"), P(("grp", "dp"), "blk"), P(("grp", "dp"), "blk"))
    return jax.shard_map(body, mesh=mesh, in_specs=in_specs, out_specs=out_specs, check_vma=False)
```

time: 434 us -> 156 us (0.36)
  the two profiles are of different devices: /device:TPU:2 before, /device:TPU:16 now
where the time goes in v1:
time: 156 us; the launch traced here: 155 us
  blocking collectives  106 us (68%)
  waiting for transfers between devices  30 us (19%)
  starting transfers between devices  8.57 us (5%)
  Pallas kernels  6.61 us (4%)
  local copies, waits for them, and re-layouts  3.49 us (2%)
    all_to_all x1, blocking collectives, body(): landed = lax.all_to_all(sent, ('grp', 'dp'), 0, 0, tiled=True)  41.2 us
    all_to_all x1, blocking collectives, body(): lax.all_to_all(both, 'blk', 0, 0, tiled=True, axis_index_groups=lines)  29.4 us
    all_to_all x1, waiting for transfers between devices, body(): lax.all_to_all(partial.reshape(cycle_size, local_rows, cols), 'blk', 0, 0...  26.6 us
    all_gather x1, blocking collectives, body(): k1 = lax.all_gather(keys[0, :, HD:], 'blk', axis=0, tiled=True)  18.4 us
    all_gather x1, blocking collectives, body(): k0 = lax.all_gather(keys[0, :, :HD], 'blk', axis=0, tiled=True)  16.6 us
    all_to_all x1, starting transfers between devices, body(): lax.all_to_all(partial.reshape(cycle_size, local_rows, cols), 'blk', 0, 0...  4.96 us
    pallas_call x1, Pallas kernels, body(): pl.pallas_call(attention_kernel, out_shape=(jax.ShapeDtypeStruct((seq, co...  4.02 us
    ppermute x1, starting transfers between devices, body(): other = lax.ppermute(send, 'blk', [(i, i ^ 1) for i in range(cycle_size)])  3.61 us
  transfers between devices with their start and end apart: 2, of which 2 were waited for; matrix products, arithmetic and copies ran while one was open for 0% of the time, Pallas kernels for 0%

profile of v1, /device:TPU:16, one launch (start us, length us, event | category | flops | bytes accessed | tf_op | source)
XLA Modules:
  0.0 155.1 jit_solution(12732842902563355050)
XLA Ops:
  0.6 0.8 fusion
  1.4 18.4 %all-gather.1 = bf16[1,2048,128]{2,1,0:T(8,128)(2,1)S(1)} all-gather(bf16[1,128,128]{2,1,0:T(8,128)(2,1)S(1)} %get-tuple-element.17), channel_id=3, replica_groups=mesh['grp'=2,'dp'=32,'blk'=16] {'blk'}, dimensions={1}, use_global_device_ids=true | all-gather | bytes 557056 | tf_op jit(solution)/shard_map/all_gather | solution.py:164
  19.8 16.6 %all-gather = bf16[1,2048,128]{2,1,0:T(8,128)(2,1)S(1)} all-gather(bf16[1,128,128]{2,1,0:T(8,128)(2,1)S(1)} %get-tuple-element.18), channel_id=2, replica_groups=mesh['grp'=2,'dp'=32,'blk'=16] {'blk'}, dimensions={1}, use_global_device_ids=true | all-gather | bytes 557056 | tf_op jit(solution)/shard_map/all_gather | solution.py:163
  36.4 0.1 pad_add_fusion.1.place
  36.5 0.0 copy-start.1
  36.5 1.0 copy-done.1
  37.5 0.0 copy-start.2
  37.5 1.0 copy-done.2
  38.5 0.0 copy-start.5
  38.5 0.7 copy-done.5
  39.2 0.0 copy-start
  39.2 4.0 %shard_map.94 = (bf16[2048,256]{1,0:T(8,128)(2,1)}, f32[128,256]{1,0:T(8,128)S(1)}) custom-call(s32[3]{0:T(128)S(1)} %pad_add_fusion.1.place, s32[1,128]{1,0:T(1,128)S(1)} %copy-done.5, bf16[128,1792]{1,0:T(8,128)(2,1)S(1)} %bitcast.19, bf16[128,1792]{1,0:T(8,128)(2,1)S(1)} %bitcast.20, bf16[2048,128]{1,0:T(8,128)(2,1)S(1)} %bitcast.17, ...), custom_call_target="tpu_custom_call" | custom-call | tf_op jit(solution)/shard_map/pallas_call | solution.py:168
  43.2 5.0 %all-to-all-start = ((bf16[16,128,256]{2,1,0:T(8,128)(2,1)}), bf16[16,128,256]{2,1,0:T(8,128)(2,1)S(1)}, u32[]{:S(2)}, u32[]{:S(2)}) async-start(bf16[16,128,256]{2,1,0:T(8,128)(2,1)} %bitcast.9), calls=%async_computation | async-start | bytes 2097152 | tf_op jit(solution)/shard_map/all_to_all | solution.py:183
  48.2 0.1 pad_add_fusion.place
  48.3 26.6 %all-to-all-done.pieces = bf16[16,128,256]{2,1,0:T(8,128)(2,1)S(1)} async-done(((bf16[16,128,256]{2,1,0:T(8,128)(2,1)}), bf16[16,128,256]{2,1,0:T(8,128)(2,1)S(1)}, u32[]{:S(2)}, u32[]{:S(2)}) %all-to-all-start) | async-done | bytes 1048608 | tf_op jit(solution)/shard_map/all_to_all | solution.py:183
  74.8 0.0 copy-done
  74.9 1.4 shard_map.95
  76.3 3.6 %collective-permute-start = (f32[8,16,3584]{2,1,0:T(8,128)S(1)}, f32[8,16,3584]{2,1,0:T(8,128)S(1)}, u32[]{:S(2)}, u32[]{:S(2)}) collective-permute-start(f32[8,16,3584]{2,1,0:T(8,128)S(1)} %get-tuple-element.13), channel_id=1, source_target_pairs={{0,1},{1,0},{2,3},{3,2},{4,5},{5,4},{6,7},{7,6},{8,9},{9,8},{10,11... | collective-permute-start | bytes 5505032 | tf_op jit(solution)/shard_map/ppermute | solution.py:198
  79.9 3.4 %collective-permute-done.b = f32[8,16,3584]{2,1,0:T(8,128)S(1)} collective-permute-done((f32[8,16,3584]{2,1,0:T(8,128)S(1)}, f32[8,16,3584]{2,1,0:T(8,128)S(1)}, u32[]{:S(2)}, u32[]{:S(2)}) %collective-permute-start) | collective-permute-done | bytes 1835040 | tf_op jit(solution)/shard_map/ppermute | solution.py:198
  83.3 0.2 shard_map.96
  83.5 0.0 copy-start.3
  83.5 0.0 copy-start.4
  83.5 29.4 %all_to_all.15.pieces = bf16[8,16,3584]{2,1,0:T(8,128)(2,1)S(1)} all-to-all(bf16[8,16,3584]{2,1,0:T(8,128)(2,1)S(1)} %shard_map.96), channel_id=1, replica_groups={{0,2,4,6,8,10,12,14},{1,3,5,7,9,11,13,15},{16,18,20,22,24,26,28,30},{17..., dimensions={0} | all-to-all | bytes 1835008 | tf_op jit(solution)/shard_map/all_to_all | solution.py:207
  112.9 0.3 shard_map.97
  113.1 41.2 %all_to_all.16.pieces = f32[64,8,128]{2,1,0:T(8,128)S(1)} all-to-all(f32[64,8,128]{2,1,0:T(8,128)S(1)} %shard_map.97), channel_id=1, replica_groups=mesh['grp'=2,'dp'=32,'blk'=16] {'grp','dp'}, dimensions={0} | all-to-all | bytes 524288 | tf_op jit(solution)/shard_map/all_to_all | solution.py:216
  154.3 0.0 copy-done.3
  154.3 0.0 copy-done.4
  154.3 0.8 shard_map.98
Async XLA Ops:
  36.5 1.0 copy-start.1
  37.5 1.0 copy-start.2
  38.5 0.7 copy-start.5
  39.2 35.6 %copy-start = (bf16[1,128,3584]{2,1,0:T(8,128)(2,1)S(1)}, bf16[1,128,3584]{2,1,0:T(8,128)(2,1)}, u32[]{:S(2)}) copy-start(bf16[1,128,3584]{2,1,0:T(8,128)(2,1)} %param.7) | copy-start | bytes 2752516
  43.2 31.6 %all-to-all-start = ((bf16[16,128,256]{2,1,0:T(8,128)(2,1)}), bf16[16,128,256]{2,1,0:T(8,128)(2,1)S(1)}, u32[]{:S(2)}, u32[]{:S(2)}) async-start(bf16[16,128,256]{2,1,0:T(8,128)(2,1)} %bitcast.9), calls=%async_computation | async-start | bytes 2097152 | tf_op jit(solution)/shard_map/all_to_all | solution.py:183
  76.3 7.0 %collective-permute-start = (f32[8,16,3584]{2,1,0:T(8,128)S(1)}, f32[8,16,3584]{2,1,0:T(8,128)S(1)}, u32[]{:S(2)}, u32[]{:S(2)}) collective-permute-start(f32[8,16,3584]{2,1,0:T(8,128)S(1)} %get-tuple-element.13), channel_id=1, source_target_pairs={{0,1},{1,0},{2,3},{3,2},{4,5},{5,4},{6,7},{7,6},{8,9},{9,8},{10,11... | collective-permute-start | bytes 5505032 | tf_op jit(solution)/shard_map/ppermute | solution.py:198
  83.5 70.8 %copy-start.3 = (f32[56,16]{0,1:T(8,128)S(1)}, f32[56,16]{0,1:T(8,128)}, u32[]{:S(2)}) copy-start(f32[56,16]{0,1:T(8,128)} %param.12) | copy-start | bytes 10756
  83.5 70.8 %copy-start.4 = (f32[56,16]{0,1:T(8,128)S(1)}, f32[56,16]{0,1:T(8,128)}, u32[]{:S(2)}) copy-start(f32[56,16]{0,1:T(8,128)} %param.13) | copy-start | bytes 10756

commit v2 on v0

v2 whole, which is shorter than its diff:
```python
import functools
import math

import jax
import jax.numpy as jnp
from jax import lax
from jax.experimental import pallas as pl
from jax.experimental.pallas import tpu as pltpu
from jax.sharding import Mesh
from jax.sharding import PartitionSpec as P

KV_HEADS = 2
HD = 128
STEP = 10
GROUP = 7
CHUNK = 512
TILE = 256
masked_score = -1e30
GAIN = HD ** (-0.5) * math.log2(math.e)
WHOLE = pl.BlockSpec(memory_space=pltpu.VMEM)
SCALARS = pl.BlockSpec(memory_space=pltpu.SMEM)
PARAMS = pltpu.CompilerParams(vmem_limit_bytes=24 * 1024 * 1024)


def product(a, b, axis):
    return lax.dot_general(
        a, b, (((1,), (axis,)), ((), ())), preferred_element_type=jnp.float32
    )


def lanes_of_queries(row):
    return jnp.concatenate([row] * GROUP, axis=1)


def local_kernel(place, begin, q, d, k, out, qs, ds):
    rows = q.shape[0]
    width = GROUP * rows

    @pl.when(place[0] == 0)
    def _():
        out[...] = jnp.zeros(out.shape, out.dtype)

    @pl.when(place[0] == 1)
    def _():
        first = lanes_of_queries(begin[...] - place[1])
        query_pos = lanes_of_queries(lax.broadcasted_iota(jnp.int32, (1, rows), 1))
        key_pos = lax.broadcasted_iota(jnp.int32, (rows, width), 0)
        visible = (key_pos >= first) & (key_pos <= query_pos)
        for g in range(KV_HEADS):
            for r in range(GROUP):
                h = g * GROUP + r
                qs[r * rows : (r + 1) * rows, :] = q[:, h * HD : (h + 1) * HD]
                ds[r * rows : (r + 1) * rows, :] = d[:, h * HD : (h + 1) * HD]
            cols = slice(g * HD, (g + 1) * HD)
            x = jnp.where(visible, product(k[:, cols], qs[...], 1) * GAIN, masked_score)
            top = jnp.max(x, axis=0, keepdims=True)
            shift = top + jnp.log2(jnp.sum(jnp.exp2(x - top), axis=0, keepdims=True))
            p = jnp.exp2(x - shift).astype(ds.dtype)
            out[:, cols] = product(p, ds[...], 0).astype(out.dtype)


def long_kernel(place, q, d, other, k, out, own, qs, ds, s):
    seq, rows = k.shape[0], q.shape[0]
    width = GROUP * rows
    first_row, high = place[1], place[2]

    @pl.when(place[0] == 0)
    def _():
        for r in range(GROUP):
            qs[r * rows : (r + 1) * rows, :] = q[:, r * HD : (r + 1) * HD]
            ds[r * rows : (r + 1) * rows, :] = d[:, r * HD : (r + 1) * HD]

    @pl.when(place[0] == 1)
    def _():
        for r in range(GROUP):
            h = GROUP + r
            qs[r * rows : (r + 1) * rows, :] = other[:, r * HD : (r + 1) * HD]
            ds[r * rows : (r + 1) * rows, :] = other[:, h * HD : (h + 1) * HD]

    def chunk_rows(c):
        return pl.ds(pl.multiple_of(c * CHUNK, CHUNK), CHUNK)

    def clear(c, carry):
        out[chunk_rows(c), :] = jnp.zeros((CHUNK, HD), out.dtype)
        return carry

    lax.fori_loop(high + 1, seq // CHUNK, clear, 0)

    def larger(x, top):
        return jnp.maximum(top, jnp.max(x.reshape(CHUNK // 8, 8, width), axis=0))

    def inner(c, top):
        x = product(k[chunk_rows(c), :], qs[...], 1) * GAIN
        s[chunk_rows(c), :] = x
        return larger(x, top)

    top = lax.fori_loop(0, high, inner, jnp.full((8, width), masked_score, jnp.float32))
    query_pos = first_row + lanes_of_queries(lax.broadcasted_iota(jnp.int32, (1, rows), 1))
    key_pos = high * CHUNK + lax.broadcasted_iota(jnp.int32, (CHUNK, width), 0)
    x = product(k[chunk_rows(high), :], qs[...], 1) * GAIN
    x = jnp.where(key_pos <= query_pos, x, masked_score)
    s[chunk_rows(high), :] = x
    top = jnp.max(larger(x, top), axis=0, keepdims=True)

    def weigh(c, total):
        p = jnp.exp2(s[chunk_rows(c), :] - top)
        return total + jnp.sum(p.reshape(CHUNK // 8, 8, width), axis=0)

    total = lax.fori_loop(0, high + 1, weigh, jnp.zeros((8, width), jnp.float32))
    shift = top + jnp.log2(jnp.sum(total, axis=0, keepdims=True))

    def collect(c):
        p = jnp.exp2(s[chunk_rows(c), :] - shift).astype(ds.dtype)
        block = product(p, ds[...], 0)
        out[chunk_rows(c), :] = block.astype(out.dtype)
        return block

    def inner_collect(c, carry):
        collect(c)
        return carry

    lax.fori_loop(0, high, inner_collect, 0)
    block = collect(high)
    for i in range(CHUNK // rows):

        @pl.when(first_row == high * CHUNK + i * rows)
        def _():
            own[...] = block[i * rows : (i + 1) * rows]


def value_kernel(place, own, pieces, short, out):
    total = own[...]
    for i in range(pieces.shape[0]):
        total = total + jnp.where(place[3] == i, 0.0, pieces[i].astype(jnp.float32))
    out[:, :HD] = total.astype(out.dtype)
    out[:, HD:] = short[...]


def project_kernel(place, values, mine, across, beside, corner, out, turned, vg):
    share = out.shape[1]
    rows = values.shape[1]
    group, core = place[0], place[4]
    for c in range(2):
        for g in range(KV_HEADS):
            heads = slice(g * HD, (g + 1) * HD)
            part = values[2 * g + c, :, :HD].astype(jnp.float32)
            turned[c, heads, :] = jnp.transpose(part)
            part = values[2 + c, :, (1 + g) * HD : (2 + g) * HD].astype(jnp.float32)
            turned[2 + c, heads, :] = jnp.transpose(part)
    for j in range(4):
        g = jnp.where(j % 2 == 0, group, 1 - group)
        c = jnp.where(j // 2 == 0, core, 1 - core)
        for i in range(out.shape[0]):
            chunk = pl.ds(pl.multiple_of((2 * i + core) * share, share), share)
            block = turned[2 * g + c, chunk, :].astype(vg.dtype)
            vg[i * share : (i + 1) * share, j * rows : (j + 1) * rows] = block
    for t in range(mine.shape[1] // TILE):
        part = slice(t * TILE, (t + 1) * TILE)
        x = jnp.concatenate(
            [mine[:, part], across[:, part], beside[:, part], corner[:, part]], axis=0
        )
        block = product(vg[...], x, 0)
        out[:, :, part] = block.astype(out.dtype).reshape(out.shape[0], share, TILE)


def fold_kernel(owners, pieces, out, total):
    acc = pieces[0].astype(jnp.float32)
    for i in range(1, pieces.shape[0]):
        acc = acc + pieces[i].astype(jnp.float32)
    total[...] = acc
    span = total.shape[1] // owners
    out[...] = jnp.zeros(out.shape, out.dtype)
    for r in range(owners):
        block = total[:, r * span : (r + 1) * span]
        out[r, :, :span] = block[:8]
        out[r, :, 64 : 64 + span] = block[8:]


def adam_kernel(scale, pieces, m, v, new_m, new_v, update):
    acc = pieces[0]
    for i in range(1, pieces.shape[0]):
        acc = acc + pieces[i]
    span = m.shape[1]
    gradient = jnp.concatenate([acc[:, :span], acc[:, 64 : 64 + span]], axis=0) * scale
    first = 0.9 * m[...] + 0.1 * gradient
    second = 0.95 * v[...] + 0.05 * gradient * gradient
    new_m[...] = first
    new_v[...] = second
    update[...] = first / (1.0 - 0.9**STEP) / (jnp.sqrt(second / (1.0 - 0.95**STEP)) + 1e-08)


def call(kernel, out, scalars, arrays, scratch=(), flops=0):
    many = isinstance(out, tuple)
    return pl.pallas_call(
        kernel,
        out_shape=out,
        in_specs=[SCALARS] * len(scalars) + [WHOLE] * len(arrays),
        out_specs=(WHOLE,) * len(out) if many else WHOLE,
        scratch_shapes=list(scratch),
        compiler_params=PARAMS,
        cost_estimate=pl.CostEstimate(flops=flops, bytes_accessed=0, transcendentals=0),
    )(*scalars, *arrays)


def body(layer_input, queries, keys, d_out, doc_start, moment_m, moment_v):
    rows = queries.shape[1]
    chips, cores = lax.axis_size("x"), lax.axis_size("core")
    owners = lax.axis_size("dp")
    blocks = chips * cores
    seq = blocks * rows
    width, cols = layer_input.shape[2], KV_HEADS * HD
    half, share = width // 2, cols // blocks
    heads = GROUP * HD
    bf16, f32 = jnp.bfloat16, jnp.float32
    shape = jax.ShapeDtypeStruct

    group, core = lax.axis_index("grp"), lax.axis_index("core")
    index = lax.axis_index("x") * cores + core
    first_row = index * rows
    place = jnp.stack([group, first_row, first_row // CHUNK, index, core]).astype(jnp.int32)
    q, d, k = queries[0], d_out[0], keys[0]

    down = [(0, 1)]
    other_k = lax.ppermute(k[:, HD:], "grp", down)
    other = lax.ppermute(jnp.concatenate([q[:, heads:], d[:, heads:]], axis=1), "grp", down)
    short = call(
        local_kernel,
        shape((rows, cols), bf16),
        [place],
        [doc_start, q, d, k],
        [pltpu.VMEM((heads, HD), bf16), pltpu.VMEM((heads, HD), bf16)],
        flops=3 * 10**9,
    )
    lower, upper = layer_input[0, :, :half], layer_input[0, :, half:]
    mine = jnp.where(group == 0, lower, upper)
    theirs = jnp.where(group == 0, upper, lower)
    theirs, other_k, short = lax.optimization_barrier((theirs, other_k, short))
    swap = [(0, 1), (1, 0)]
    across = lax.ppermute(theirs, "grp", swap)
    chosen = jnp.where(group == 0, k[:, :HD], other_k)
    all_keys = lax.all_gather(chosen, ("x", "core"), axis=0, tiled=True)
    partial, own = call(
        long_kernel,
        (shape((seq, HD), bf16), shape((rows, HD), f32)),
        [place],
        [q, d, other, all_keys],
        [
            pltpu.VMEM((heads, HD), bf16),
            pltpu.VMEM((heads, HD), bf16),
            pltpu.VMEM((seq, GROUP * rows), f32),
        ],
        flops=6 * 10**9,
    )
    mine, across, own = lax.optimization_barrier((mine, across, own))
    beside = lax.ppermute(mine, "core", swap)
    corner = lax.ppermute(across, "core", swap)
    pieces = lax.all_to_all(
        partial.reshape(blocks, rows, HD), ("x", "core"), 0, 0, tiled=True
    )
    values = call(value_kernel, shape((rows, HD + cols), bf16), [place], [own, pieces, short])
    values = lax.all_gather(values, ("grp", "core"), axis=0)
    gradient = call(
        project_kernel,
        shape((chips, share, half), bf16),
        [place],
        [values, mine, across, beside, corner],
        [pltpu.VMEM((4, cols, rows), f32), pltpu.VMEM((cols // 2, 4 * rows), bf16)],
    )
    terms = lax.all_to_all(gradient, "x", 0, 0, tiled=True)
    sent = call(
        functools.partial(fold_kernel, owners),
        shape((owners, 8, 128), f32),
        [],
        [terms],
        [pltpu.VMEM((share, half), f32)],
    )
    landed = lax.all_to_all(sent, "dp", 0, 0, tiled=True)
    result = shape(moment_m.shape[::-1], f32)
    total_tokens = 2 * owners * seq
    outs = call(
        functools.partial(adam_kernel, 1.0 / math.sqrt(total_tokens)),
        (result,) * 3,
        [],
        [landed, moment_m.T, moment_v.T],
    )
    return tuple(o.T for o in outs)


def solution(mesh):
    split = mesh.devices.reshape(*mesh.devices.shape[:2], -1, 2)
    mesh = Mesh(split, ("grp", "dp", "x", "core"))
    slots, tokens = ("grp", "dp"), ("x", "core")
    wide, flat = P(slots, tokens, None), P(slots, tokens)
    in_specs = (wide, wide, wide, wide, flat, flat, flat)
    return jax.shard_map(
        body, mesh=mesh, in_specs=in_specs, out_specs=(flat,) * 3, check_vma=False
    )
```

time: 434 us -> 123 us (0.28)
  the two profiles are of different devices: /device:TPU:2 before, /device:TPU:1 now
where the time goes in v2:
time: 123 us
  blocking collectives  81.8 us (67%)
  starting transfers between devices  18.7 us (15%)
  waiting for transfers between devices  12.1 us (10%)
  Pallas kernels  5.79 us (5%)
  local copies, waits for them, and re-layouts  2.6 us (2%)
    all_gather x1, blocking collectives, body(): all_keys = lax.all_gather(chosen, ('x', 'core'), axis=0, tiled=True)  26.9 us
    all_to_all x1, blocking collectives, body(): landed = lax.all_to_all(sent, 'dp', 0, 0, tiled=True)  25.5 us
    all_to_all x1, blocking collectives, body(): terms = lax.all_to_all(gradient, 'x', 0, 0, tiled=True)  22.8 us
    ppermute x1, waiting for transfers between devices, body(): across = lax.ppermute(theirs, 'grp', swap)  12.1 us
    all_to_all x1, starting transfers between devices, body(): lax.all_to_all(partial.reshape(blocks, rows, HD), ('x', 'core'), 0, 0, ti...  6.59 us
    all_gather x1, blocking collectives, body(): values = lax.all_gather(values, ('grp', 'core'), axis=0)  6.58 us
    pallas_call x6, Pallas kernels, call(): pl.pallas_call(kernel, out_shape=out, in_specs=[SCALARS] * len(scalars) +...  5.79 us
    ppermute x1, starting transfers between devices, body(): other_k = lax.ppermute(k[:, HD:], 'grp', down)  4.13 us
  transfers between devices with their start and end apart: 6, of which 1 were waited for; matrix products, arithmetic and copies ran while one was open for 2% of the time, Pallas kernels for 1%

profile of v2, /device:TPU:1, one launch (start us, length us, event | category | flops | bytes accessed | tf_op | source)
XLA Modules:
  0.0 122.6 jit_solution(9264134973499206658)
XLA Ops:
  0.6 0.0 copy-start.1
  0.6 0.8 slice.24
  1.5 4.1 %collective-permute-start = (bf16[128,128]{1,0:T(8,128)(2,1)S(1)}, bf16[128,128]{1,0:T(8,128)(2,1)S(1)}, u32[]{:S(2)}, u32[]{:S(2)}) collective-permute-start(bf16[128,128]{1,0:T(8,128)(2,1)S(1)} %slice.24), channel_id=1, source_target_pairs={{0,512},{1,513},{2,514},{3,515},{4,516},{5,517},{6,518},{7,519},{8... | collective-permute-start | bytes 98312 | tf_op jit(solution)/shard_map/ppermute | solution.py:224
  5.6 0.0 copy-start.6
  5.6 1.0 slice.25
  6.7 0.0 copy-done.1
  6.7 1.3 %collective-permute-start.2 = (bf16[128,1792]{1,0:T(8,128)(2,1)S(1)}, bf16[128,1792]{1,0:T(8,128)(2,1)S(1)}, u32[]{:S(2)}, u32[]{:S(2)}) collective-permute-start(bf16[128,1792]{1,0:T(8,128)(2,1)S(1)} %pad_maximum_fusion), channel_id=1, source_target_pairs={{0,512},{1,513},{2,514},{3,515},{4,516},{5,517},{6,518},{7,519},{8... | collective-permute-start | bytes 1376264 | tf_op jit(solution)/shard_map/ppermute | solution.py:225
  8.1 0.0 copy-done.6
  8.1 0.0 copy-start
  8.1 0.0 copy-start.2
  8.1 0.8 select_bitcast_fusion
  9.0 0.0 copy-start.5
  9.0 0.1 stack.23.place
  9.0 0.2 copy-done
  9.2 0.0 copy-done.2
  9.2 0.4 copy-done.5
  9.7 0.6 shard_map.94.short
  10.2 0.0 collective-permute-done
  10.2 26.9 %all_gather.9.k = bf16[2048,128]{1,0:T(8,128)(2,1)S(1)} all-gather(bf16[128,128]{1,0:T(8,128)(2,1)S(1)} %slice_select_fusion), channel_id=1, replica_groups=mesh['grp'=2,'dp'=32,'x'=8,'core'=2] {'x','core'}, dimensions={0}, use_global_device_ids=true | all-gather | bytes 557056 | tf_op jit(solution)/shard_map/all_gather | solution.py:241
  37.1 0.0 collective-permute-done.2.other
  37.1 2.6 %shard_map.95 = (bf16[2048,128]{1,0:T(8,128)(2,1)}, f32[128,128]{1,0:T(8,128)S(1)}) custom-call(s32[5]{0:T(128)S(1)} %stack.23.place, bf16[128,1792]{1,0:T(8,128)(2,1)S(1)} %bitcast.22, bf16[128,1792]{1,0:T(8,128)(2,1)S(1)} %bitcast.25, bf16[128,1792]{1,0:T(8,128)(2,1)S(1)} %collective-permute-done.2.other, bf16[2048,128]{1,0:T(8,128)(2,1)S(1)} %all_gather.9.k), custom_call_target="tpu_custom_call" | custom-call | flops 6000000000 | tf_op jit(solution)/shard_map/pallas_call | solution.py:194
  39.7 0.0 copy-start.7
  39.7 6.6 %all-to-all-start = ((bf16[16,128,128]{2,1,0:T(8,128)(2,1)}), bf16[16,128,128]{2,1,0:T(8,128)(2,1)S(1)}, u32[]{:S(2)}, u32[]{:S(2)}) async-start(bf16[16,128,128]{2,1,0:T(8,128)(2,1)} %bitcast.10), calls=%async_computation | async-start | bytes 1048576 | tf_op jit(solution)/shard_map/all_to_all | solution.py:257
  46.3 0.0 copy-done.7
  46.3 1.9 %collective-permute-start.1 = (bf16[128,1792]{1,0:T(8,128)(2,1)S(1)}, bf16[128,1792]{1,0:T(8,128)(2,1)S(1)}, u32[]{:S(2)}, u32[]{:S(2)}) collective-permute-start(bf16[128,1792]{1,0:T(8,128)(2,1)S(1)} %copy-done.7), channel_id=1, source_target_pairs={{0,512},{512,0},{1,513},{513,1},{2,514},{514,2},{3,515},{515,3},{4... | collective-permute-start | bytes 1376264 | tf_op jit(solution)/shard_map/ppermute | solution.py:239
  48.3 12.1 %collective-permute-done.1.across = bf16[128,1792]{1,0:T(8,128)(2,1)S(1)} collective-permute-done((bf16[128,1792]{1,0:T(8,128)(2,1)S(1)}, bf16[128,1792]{1,0:T(8,128)(2,1)S(1)}, u32[]{:S(2)}, u32[]{:S(2)}) %collective-permute-start.1) | collective-permute-done | bytes 458784 | tf_op jit(solution)/shard_map/ppermute | solution.py:239
  60.3 2.8 %collective-permute-start.3 = (bf16[128,1792]{1,0:T(8,128)(2,1)S(1)}, bf16[128,1792]{1,0:T(8,128)(2,1)S(1)}, u32[]{:S(2)}, u32[]{:S(2)}) collective-permute-start(bf16[128,1792]{1,0:T(8,128)(2,1)S(1)} %get-tuple-element.20.mine), channel_id=1, source_target_pairs={{0,1},{1,0},{2,3},{3,2},{4,5},{5,4},{6,7},{7,6},{8,9},{9,8},{10,11... | collective-permute-start | bytes 1376264 | tf_op jit(solution)/shard_map/ppermute | solution.py:255
  63.1 1.9 %collective-permute-start.4 = (bf16[128,1792]{1,0:T(8,128)(2,1)S(1)}, bf16[128,1792]{1,0:T(8,128)(2,1)S(1)}, u32[]{:S(2)}, u32[]{:S(2)}) collective-permute-start(bf16[128,1792]{1,0:T(8,128)(2,1)S(1)} %collective-permute-done.1.across), channel_id=1, source_target_pairs={{0,1},{1,0},{2,3},{3,2},{4,5},{5,4},{6,7},{7,6},{8,9},{9,8},{10,11... | collective-permute-start | bytes 1376264 | tf_op jit(solution)/shard_map/ppermute | solution.py:256
  65.0 0.0 all-to-all-done.pieces
  65.0 0.7 shard_map.96
  65.7 6.6 %all-gather = bf16[512,384]{1,0:T(8,128)(2,1)S(1)} all-gather(bf16[128,384]{1,0:T(8,128)(2,1)S(1)} %shard_map.96), channel_id=2, replica_groups=mesh['grp'=2,'dp'=32,'x'=8,'core'=2] {'grp','core'}, dimensions={0}, use_global_device_ids=true | all-gather | bytes 491520 | tf_op jit(solution)/shard_map/all_gather | solution.py:261
  72.3 0.0 collective-permute-done.3.beside
  72.3 0.0 collective-permute-done.4.corner
  72.3 1.1 shard_map.97
  73.4 22.8 %all_to_all.15.pieces = bf16[8,16,1792]{2,1,0:T(8,128)(2,1)S(1)} all-to-all(bf16[8,16,1792]{2,1,0:T(8,128)(2,1)S(1)} %shard_map.97), channel_id=1, replica_groups=mesh['grp'=2,'dp'=32,'x'=8,'core'=2] {'x'}, dimensions={0} | all-to-all | bytes 917504 | tf_op jit(solution)/shard_map/all_to_all | solution.py:269
  96.2 0.0 copy-start.3
  96.2 0.0 copy-start.4
  96.2 0.2 shard_map.98
  96.3 25.5 %all_to_all.16.pieces = f32[32,8,128]{2,1,0:T(8,128)S(1)} all-to-all(f32[32,8,128]{2,1,0:T(8,128)S(1)} %shard_map.98), channel_id=1, replica_groups=mesh['grp'=2,'dp'=32,'x'=8,'core'=2] {'dp'}, dimensions={0} | all-to-all | bytes 262144 | tf_op jit(solution)/shard_map/all_to_all | solution.py:277
  121.9 0.0 copy-done.3
  121.9 0.0 copy-done.4
  121.9 0.7 shard_map.99
  (3 shorter events, 0.1 us)
Async XLA Ops:
  0.6 6.0 %copy-start.1 = (bf16[1,128,1792]{2,1,0:T(8,128)(2,1)S(1)}, bf16[1,128,1792]{2,1,0:T(8,128)(2,1)}, u32[]{:S(2)}) copy-start(bf16[1,128,1792]{2,1,0:T(8,128)(2,1)} %param.10) | copy-start | bytes 1376260
  1.5 8.8 %collective-permute-start = (bf16[128,128]{1,0:T(8,128)(2,1)S(1)}, bf16[128,128]{1,0:T(8,128)(2,1)S(1)}, u32[]{:S(2)}, u32[]{:S(2)}) collective-permute-start(bf16[128,128]{1,0:T(8,128)(2,1)S(1)} %slice.24), channel_id=1, source_target_pairs={{0,512},{1,513},{2,514},{3,515},{4,516},{5,517},{6,518},{7,519},{8... | collective-permute-start | bytes 98312 | tf_op jit(solution)/shard_map/ppermute | solution.py:224
  5.6 2.5 %copy-start.6 = (bf16[1,128,3584]{2,1,0:T(8,128)(2,1)S(1)}, bf16[1,128,3584]{2,1,0:T(8,128)(2,1)}, u32[]{:S(2)}) copy-start(bf16[1,128,3584]{2,1,0:T(8,128)(2,1)} %param.7) | copy-start | bytes 2752516
  6.7 30.4 %collective-permute-start.2 = (bf16[128,1792]{1,0:T(8,128)(2,1)S(1)}, bf16[128,1792]{1,0:T(8,128)(2,1)S(1)}, u32[]{:S(2)}, u32[]{:S(2)}) collective-permute-start(bf16[128,1792]{1,0:T(8,128)(2,1)S(1)} %pad_maximum_fusion), channel_id=1, source_target_pairs={{0,512},{1,513},{2,514},{3,515},{4,516},{5,517},{6,518},{7,519},{8... | collective-permute-start | bytes 1376264 | tf_op jit(solution)/shard_map/ppermute | solution.py:225
  8.1 1.1 copy-start
  8.1 1.1 copy-start.2
  9.0 0.7 copy-start.5
  39.7 6.6 %copy-start.7 = (bf16[128,1792]{1,0:T(8,128)(2,1)S(1)}, bf16[128,1792]{1,0:T(8,128)(2,1)}, u32[]{:S(2)}) copy-start(bf16[128,1792]{1,0:T(8,128)(2,1)} %get-tuple-element.14) | copy-start | bytes 1376260
  39.7 25.3 %all-to-all-start = ((bf16[16,128,128]{2,1,0:T(8,128)(2,1)}), bf16[16,128,128]{2,1,0:T(8,128)(2,1)S(1)}, u32[]{:S(2)}, u32[]{:S(2)}) async-start(bf16[16,128,128]{2,1,0:T(8,128)(2,1)} %bitcast.10), calls=%async_computation | async-start | bytes 1048576 | tf_op jit(solution)/shard_map/all_to_all | solution.py:257
  46.3 14.0 %collective-permute-start.1 = (bf16[128,1792]{1,0:T(8,128)(2,1)S(1)}, bf16[128,1792]{1,0:T(8,128)(2,1)S(1)}, u32[]{:S(2)}, u32[]{:S(2)}) collective-permute-start(bf16[128,1792]{1,0:T(8,128)(2,1)S(1)} %copy-done.7), channel_id=1, source_target_pairs={{0,512},{512,0},{1,513},{513,1},{2,514},{514,2},{3,515},{515,3},{4... | collective-permute-start | bytes 1376264 | tf_op jit(solution)/shard_map/ppermute | solution.py:239
  60.3 12.0 %collective-permute-start.3 = (bf16[128,1792]{1,0:T(8,128)(2,1)S(1)}, bf16[128,1792]{1,0:T(8,128)(2,1)S(1)}, u32[]{:S(2)}, u32[]{:S(2)}) collective-permute-start(bf16[128,1792]{1,0:T(8,128)(2,1)S(1)} %get-tuple-element.20.mine), channel_id=1, source_target_pairs={{0,1},{1,0},{2,3},{3,2},{4,5},{5,4},{6,7},{7,6},{8,9},{9,8},{10,11... | collective-permute-start | bytes 1376264 | tf_op jit(solution)/shard_map/ppermute | solution.py:255
  63.1 9.2 %collective-permute-start.4 = (bf16[128,1792]{1,0:T(8,128)(2,1)S(1)}, bf16[128,1792]{1,0:T(8,128)(2,1)S(1)}, u32[]{:S(2)}, u32[]{:S(2)}) collective-permute-start(bf16[128,1792]{1,0:T(8,128)(2,1)S(1)} %collective-permute-done.1.across), channel_id=1, source_target_pairs={{0,1},{1,0},{2,3},{3,2},{4,5},{5,4},{6,7},{7,6},{8,9},{9,8},{10,11... | collective-permute-start | bytes 1376264 | tf_op jit(solution)/shard_map/ppermute | solution.py:256
  96.2 25.7 %copy-start.3 = (f32[56,16]{0,1:T(8,128)S(1)}, f32[56,16]{0,1:T(8,128)}, u32[]{:S(2)}) copy-start(f32[56,16]{0,1:T(8,128)} %param.12) | copy-start | bytes 10756
  96.2 25.7 %copy-start.4 = (f32[56,16]{0,1:T(8,128)S(1)}, f32[56,16]{0,1:T(8,128)}, u32[]{:S(2)}) copy-start(f32[56,16]{0,1:T(8,128)} %param.13) | copy-start | bytes 10756

commit v3 on v2

--- a/solution.py
+++ b/solution.py
@@ -14,7 +14,6 @@
 STEP = 10
 GROUP = 7
 CHUNK = 512
-TILE = 256
 masked_score = -1e30
 GAIN = HD ** (-0.5) * math.log2(math.e)
 WHOLE = pl.BlockSpec(memory_space=pltpu.VMEM)
@@ -32,9 +31,31 @@
     return jnp.concatenate([row] * GROUP, axis=1)
 
 
-def local_kernel(place, begin, q, d, k, out, qs, ds):
+def regroup_rows(owners, x, group, mine, theirs):
+    rows = x.shape[0]
+    half = x.shape[1] // 2
+    span = half // owners
+    for g in range(2):
+        at = slice(0, rows) if g == group else slice(rows, 2 * rows)
+        for p in range(owners // 2):
+            for parity, out in enumerate((mine, theirs)):
+                start = g * half + (2 * p + parity) * span
+                out[at, p * span : (p + 1) * span] = x[:, start : start + span]
+
+
+def pack_kernel(owners, place, begin, q, d, k, x, out, packed, keep, send, qs, ds):
     rows = q.shape[0]
     width = GROUP * rows
+    heads = GROUP * HD
+    packed[:, :heads] = q[:, heads:]
+    packed[:, heads:] = d[:, heads:]
+    for group in range(2):
+        for low in range(2):
+
+            @pl.when((place[0] == group) & (place[5] == low))
+            def _():
+                refs = (send, keep) if low else (keep, send)
+                regroup_rows(owners, x, group, *refs)
 
     @pl.when(place[0] == 0)
     def _():
@@ -128,39 +149,43 @@
             own[...] = block[i * rows : (i + 1) * rows]
 
 
-def value_kernel(place, own, pieces, short, out):
+def regroup_kernel(keep, got, short, pair, onward, up):
+    rows = short.shape[0]
+    pair[:rows], pair[rows:] = keep[:rows], got[:rows]
+    onward[:rows], onward[rows:] = keep[rows:], got[rows:]
+    up[...] = short[:, :HD]
+
+
+def value_kernel(place, own, pieces, short, got, out):
     total = own[...]
     for i in range(pieces.shape[0]):
         total = total + jnp.where(place[3] == i, 0.0, pieces[i].astype(jnp.float32))
     out[:, :HD] = total.astype(out.dtype)
-    out[:, HD:] = short[...]
-
-
-def project_kernel(place, values, mine, across, beside, corner, out, turned, vg):
+    out[:, HD:] = jnp.where(place[0] == 0, got[...], short[:, HD:])
+
+
+def project_kernel(place, values, pair, across, beside, corner, out, turned, vg):
     share = out.shape[1]
     rows = values.shape[1]
-    group, core = place[0], place[4]
-    for c in range(2):
-        for g in range(KV_HEADS):
-            heads = slice(g * HD, (g + 1) * HD)
-            part = values[2 * g + c, :, :HD].astype(jnp.float32)
-            turned[c, heads, :] = jnp.transpose(part)
-            part = values[2 + c, :, (1 + g) * HD : (2 + g) * HD].astype(jnp.float32)
-            turned[2 + c, heads, :] = jnp.transpose(part)
-    for j in range(4):
-        g = jnp.where(j % 2 == 0, group, 1 - group)
-        c = jnp.where(j // 2 == 0, core, 1 - core)
-        for i in range(out.shape[0]):
-            chunk = pl.ds(pl.multiple_of((2 * i + core) * share, share), share)
-            block = turned[2 * g + c, chunk, :].astype(vg.dtype)
-            vg[i * share : (i + 1) * share, j * rows : (j + 1) * rows] = block
-    for t in range(mine.shape[1] // TILE):
-        part = slice(t * TILE, (t + 1) * TILE)
-        x = jnp.concatenate(
-            [mine[:, part], across[:, part], beside[:, part], corner[:, part]], axis=0
-        )
-        block = product(vg[...], x, 0)
-        out[:, :, part] = block.astype(out.dtype).reshape(out.shape[0], share, TILE)
+    group, core, low = place[0], place[4], place[5]
+    for n in range(8):
+        g, z, c = n // 4, n // 2 % 2, n % 2
+        both = jnp.transpose(values[n].astype(jnp.float32))
+        turned[2 * z + c, g * HD : (g + 1) * HD, :] = both[:HD]
+        turned[4 + 2 * z + c, g * HD : (g + 1) * HD, :] = both[HD:]
+    total = None
+    for j, x in enumerate((pair, across, beside, corner)):
+        g = group if j % 2 == 0 else 1 - group
+        c = core if j // 2 == 0 else 1 - core
+        for k in range(2):
+            z = low if k == 0 else 1 - low
+            for i in range(out.shape[0]):
+                chunk = pl.ds(pl.multiple_of((2 * i + core) * share, share), share)
+                block = turned[4 * g + 2 * z + c, chunk, :].astype(vg.dtype)
+                vg[j, i * share : (i + 1) * share, k * rows : (k + 1) * rows] = block
+        part = product(vg[j], x[...], 0)
+        total = part if total is None else total + part
+    out[...] = total.astype(out.dtype).reshape(out.shape)
 
 
 def fold_kernel(owners, pieces, out, total):
@@ -209,36 +234,33 @@
     blocks = chips * cores
     seq = blocks * rows
     width, cols = layer_input.shape[2], KV_HEADS * HD
-    half, share = width // 2, cols // blocks
+    quarter, share = width // 4, cols // blocks
     heads = GROUP * HD
     bf16, f32 = jnp.bfloat16, jnp.float32
     shape = jax.ShapeDtypeStruct
 
-    group, core = lax.axis_index("grp"), lax.axis_index("core")
+    group, low, core = lax.axis_index("grp"), lax.axis_index("zl"), lax.axis_index("core")
     index = lax.axis_index("x") * cores + core
     first_row = index * rows
-    place = jnp.stack([group, first_row, first_row // CHUNK, index, core]).astype(jnp.int32)
+    place = jnp.stack([group, first_row, first_row // CHUNK, index, core, low]).astype(jnp.int32)
     q, d, k = queries[0], d_out[0], keys[0]
 
-    down = [(0, 1)]
-    other_k = lax.ppermute(k[:, HD:], "grp", down)
-    other = lax.ppermute(jnp.concatenate([q[:, heads:], d[:, heads:]], axis=1), "grp", down)
-    short = call(
-        local_kernel,
-        shape((rows, cols), bf16),
+    down, up, swap = [(0, 1)], [(1, 0)], [(0, 1), (1, 0)]
+    other_k = lax.ppermute(k, "grp", down)
+    block = shape((2 * rows, quarter), bf16)
+    short, packed, keep, send = call(
+        functools.partial(pack_kernel, 2 * owners),
+        (shape((rows, cols), bf16), shape((rows, 2 * heads), bf16), block, block),
         [place],
-        [doc_start, q, d, k],
+        [doc_start, q, d, k, layer_input[0]],
         [pltpu.VMEM((heads, HD), bf16), pltpu.VMEM((heads, HD), bf16)],
         flops=3 * 10**9,
     )
-    lower, upper = layer_input[0, :, :half], layer_input[0, :, half:]
-    mine = jnp.where(group == 0, lower, upper)
-    theirs = jnp.where(group == 0, upper, lower)
-    theirs, other_k, short = lax.optimization_barrier((theirs, other_k, short))
-    swap = [(0, 1), (1, 0)]
-    across = lax.ppermute(theirs, "grp", swap)
-    chosen = jnp.where(group == 0, k[:, :HD], other_k)
+    other = lax.ppermute(packed, "grp", down)
+    got = lax.ppermute(send, "zl", swap)
+    chosen = jnp.where(group == 0, k[:, :HD], other_k[:, HD:])
     all_keys = lax.all_gather(chosen, ("x", "core"), axis=0, tiled=True)
+    all_keys, got = lax.optimization_barrier((all_keys, got))
     partial, own = call(
         long_kernel,
         (shape((seq, HD), bf16), shape((rows, HD), f32)),
@@ -251,20 +273,27 @@
         ],
         flops=6 * 10**9,
     )
-    mine, across, own = lax.optimization_barrier((mine, across, own))
-    beside = lax.ppermute(mine, "core", swap)
+    got, own = lax.optimization_barrier((got, own))
+    pair, onward, upward = call(
+        regroup_kernel, (block, block, shape((rows, HD), bf16)), [], [keep, got, short]
+    )
+    across = lax.ppermute(onward, "grp", swap)
+    beside = lax.ppermute(pair, "core", swap)
+    from_short = lax.ppermute(upward, "grp", up)
     corner = lax.ppermute(across, "core", swap)
     pieces = lax.all_to_all(
         partial.reshape(blocks, rows, HD), ("x", "core"), 0, 0, tiled=True
     )
-    values = call(value_kernel, shape((rows, HD + cols), bf16), [place], [own, pieces, short])
-    values = lax.all_gather(values, ("grp", "core"), axis=0)
+    values = call(
+        value_kernel, shape((rows, 2 * HD), bf16), [place], [own, pieces, short, from_short]
+    )
+    values = lax.all_gather(values, ("grp", "zl", "core"), axis=0)
     gradient = call(
         project_kernel,
-        shape((chips, share, half), bf16),
+        shape((chips, share, quarter), bf16),
         [place],
-        [values, mine, across, beside, corner],
-        [pltpu.VMEM((4, cols, rows), f32), pltpu.VMEM((cols // 2, 4 * rows), bf16)],
+        [values, pair, across, beside, corner],
+        [pltpu.VMEM((8, cols, rows), f32), pltpu.VMEM((4, cols // 2, 2 * rows), bf16)],
     )
     terms = lax.all_to_all(gradient, "x", 0, 0, tiled=True)
     sent = call(
@@ -272,11 +301,11 @@
         shape((owners, 8, 128), f32),
         [],
         [terms],
-        [pltpu.VMEM((share, half), f32)],
+        [pltpu.VMEM((share, quarter), f32)],
     )
     landed = lax.all_to_all(sent, "dp", 0, 0, tiled=True)
     result = shape(moment_m.shape[::-1], f32)
-    total_tokens = 2 * owners * seq
+    total_tokens = 4 * owners * seq
     outs = call(
         functools.partial(adam_kernel, 1.0 / math.sqrt(total_tokens)),
         (result,) * 3,
@@ -287,9 +316,10 @@
 
 
 def solution(mesh):
-    split = mesh.devices.reshape(*mesh.devices.shape[:2], -1, 2)
-    mesh = Mesh(split, ("grp", "dp", "x", "core"))
-    slots, tokens = ("grp", "dp"), ("x", "core")
+    groups, copies, blocks = mesh.devices.shape
+    split = mesh.devices.reshape(groups, copies // 2, 2, blocks // 2, 2)
+    mesh = Mesh(split, ("grp", "dp", "zl", "x", "core"))
+    slots, tokens = ("grp", "dp", "zl"), ("x", "core")
     wide, flat = P(slots, tokens, None), P(slots, tokens)
     in_specs = (wide, wide, wide, wide, flat, flat, flat)
     return jax.shard_map(

time: 123 us -> 134 us (1.089)
  starting transfers between devices: 18.7 us -> 26 us
  local copies, waits for them, and re-layouts: 2.6 us -> 3.97 us
    all_gather x1, blocking collectives: 6.58 us -> 13.6 us  [body(): values = lax.all_gather(values, ('grp', 'zl', 'core'), axis=0)]
    ppermute x4 -> x6, starting transfers between devices: 10.1 us -> 16.8 us  [the longest x1 5.04 us: body(): got = lax.ppermute(send, 'zl', swap)]
    all_to_all x1, blocking collectives: 22.8 us -> 17.6 us  [body(): terms = lax.all_to_all(gradient, 'x', 0, 0, tiled=True)]
    all_gather x1, blocking collectives: 26.9 us -> 22.9 us  [body(): all_keys = lax.all_gather(chosen, ('x', 'core'), axis=0, tiled=True)]
    unnamed x16 -> x18, local copies, waits for them, and re-layouts: 0.64 us -> 3.89 us
    all_to_all x1, blocking collectives: 25.5 us -> 27.9 us  [body(): landed = lax.all_to_all(sent, 'dp', 0, 0, tiled=True)]
    slice x3 -> x0, local copies, waits for them, and re-layouts: 1.88 us -> none  [the longest x1 1.04 us: body(): q[:, heads:]]
    ppermute x4 -> x6, waiting for transfers between devices: 12.1 us -> 13.4 us  [the longest x1 10 us: body(): across = lax.ppermute(onward, 'grp', swap)]
  transfers between devices with their start and end apart: 6 -> 8, of which waited for: 1 -> 2; matrix products, arithmetic and copies ran while one was open for 2% -> 0% of each run, Pallas kernels for 1% -> 2%
where the time goes in v3:
time: 134 us; the launch traced here: 133 us
  blocking collectives  82.1 us (61%)
  starting transfers between devices  26 us (19%)
  waiting for transfers between devices  13.4 us (10%)
  Pallas kernels  7.06 us (5%)
  local copies, waits for them, and re-layouts  3.97 us (3%)
    all_to_all x1, blocking collectives, body(): landed = lax.all_to_all(sent, 'dp', 0, 0, tiled=True)  27.9 us
    all_gather x1, blocking collectives, body(): all_keys = lax.all_gather(chosen, ('x', 'core'), axis=0, tiled=True)  22.9 us
    all_to_all x1, blocking collectives, body(): terms = lax.all_to_all(gradient, 'x', 0, 0, tiled=True)  17.6 us
    all_gather x1, blocking collectives, body(): values = lax.all_gather(values, ('grp', 'zl', 'core'), axis=0)  13.6 us
    ppermute x1, waiting for transfers between devices, body(): across = lax.ppermute(onward, 'grp', swap)  10 us
    pallas_call x7, Pallas kernels, call(): pl.pallas_call(kernel, out_shape=out, in_specs=[SCALARS] * len(scalars) +...  7.06 us
    all_to_all x1, starting transfers between devices, body(): lax.all_to_all(partial.reshape(blocks, rows, HD), ('x', 'core'), 0, 0, ti...  6.46 us
    ppermute x1, starting transfers between devices, body(): got = lax.ppermute(send, 'zl', swap)  5.04 us
  transfers between devices with their start and end apart: 8, of which 2 were waited for; matrix products, arithmetic and copies ran while one was open for 0% of the time, Pallas kernels for 2%

profile of v3, /device:TPU:1, one launch (start us, length us, event | category | flops | bytes accessed | tf_op | source)
XLA Modules:
  0.0 133.4 jit_solution(1657617076625833120)
XLA Ops:
  0.6 0.0 copy-start
  0.6 4.3 %collective-permute-start = (bf16[128,256]{1,0:T(8,128)(2,1)}, bf16[128,256]{1,0:T(8,128)(2,1)S(1)}, u32[]{:S(2)}, u32[]{:S(2)}) collective-permute-start(bf16[128,256]{1,0:T(8,128)(2,1)} %bitcast.18), channel_id=1, source_target_pairs={{0,512},{1,513},{2,514},{3,515},{4,516},{5,517},{6,518},{7,519},{8... | collective-permute-start | bytes 196616 | tf_op jit(solution)/shard_map/ppermute | solution.py:249
  4.9 0.1 stack.27.place
  5.0 0.0 copy-start.8
  5.0 0.0 copy-done
  5.0 0.7 copy-done.8
  5.7 0.0 copy-start.3
  5.7 1.2 copy-done.3
  6.9 0.0 copy-start.4
  6.9 1.0 copy-done.4
  7.9 0.0 copy-start.6
  7.9 1.0 copy-done.6
  8.9 0.0 copy-start.7
  8.9 1.7 %shard_map.94 = (bf16[128,256]{1,0:T(8,128)(2,1)S(1)}, bf16[128,1792]{1,0:T(8,128)(2,1)S(1)}, bf16[256,896]{1,0:T(8,128)(2,1)S(1)}, bf16[256,896]{1,0:T(8,128)(2,1)S(1)}) custom-call(s32[6]{0:T(128)S(1)} %stack.27.place, s32[1,128]{1,0:T(1,128)S(1)} %copy-done.8, bf16[128,1792]{1,0:T(8,128)(2,1)S(1)} %bitcast.24, bf16[128,1792]{1,0:T(8,128)(2,1)S(1)} %bitcast.26, ...), custom_call_target="tpu_custom_call" | custom-call | flops 3000000000 | tf_op jit(solution)/shard_map/pallas_call | solution.py:219
  10.6 0.0 copy-start.5
  10.6 5.0 %collective-permute-start.1 = (bf16[256,896]{1,0:T(8,128)(2,1)S(1)}, bf16[256,896]{1,0:T(8,128)(2,1)S(1)}, u32[]{:S(2)}, u32[]{:S(2)}) collective-permute-start(bf16[256,896]{1,0:T(8,128)(2,1)S(1)} %get-tuple-element.19), channel_id=1, source_target_pairs={{0,16},{16,0},{1,17},{17,1},{2,18},{18,2},{3,19},{19,3},{4,20},{20... | collective-permute-start | bytes 1376264 | tf_op jit(solution)/shard_map/ppermute | solution.py:260
  15.7 2.2 %collective-permute-start.2 = (bf16[128,1792]{1,0:T(8,128)(2,1)S(1)}, bf16[128,1792]{1,0:T(8,128)(2,1)S(1)}, u32[]{:S(2)}, u32[]{:S(2)}) collective-permute-start(bf16[128,1792]{1,0:T(8,128)(2,1)S(1)} %get-tuple-element.21), channel_id=1, source_target_pairs={{0,512},{1,513},{2,514},{3,515},{4,516},{5,517},{6,518},{7,519},{8... | collective-permute-start | bytes 1376264 | tf_op jit(solution)/shard_map/ppermute | solution.py:259
  17.9 0.0 collective-permute-done
  17.9 22.9 %all_gather.9.k = bf16[2048,128]{1,0:T(8,128)(2,1)S(1)} all-gather(bf16[128,128]{1,0:T(8,128)(2,1)S(1)} %slice_select_fusion), channel_id=1, replica_groups=mesh['grp'=2,'dp'=16,'zl'=2,'x'=8,'core'=2] {'x','core'}, dimensions={0}, use_global_device_ids=true | all-gather | bytes 557056 | tf_op jit(solution)/shard_map/all_gather | solution.py:262
  40.9 0.0 collective-permute-done.1.got
  40.9 0.0 collective-permute-done.2.other
  40.9 0.0 copy-done.7
  40.9 0.0 copy-done.5
  40.9 2.6 %shard_map.95 = (bf16[2048,128]{1,0:T(8,128)(2,1)}, f32[128,128]{1,0:T(8,128)S(1)}) custom-call(s32[6]{0:T(128)S(1)} %stack.27.place, bf16[128,1792]{1,0:T(8,128)(2,1)S(1)} %bitcast.25, bf16[128,1792]{1,0:T(8,128)(2,1)S(1)} %bitcast.27, bf16[128,1792]{1,0:T(8,128)(2,1)S(1)} %collective-permute-done.2.other, bf16[2048,128]{1,0:T(8,128)(2,1)S(1)} %all_gather.9.k), custom_call_target="tpu_custom_call" | custom-call | flops 6000000000 | tf_op jit(solution)/shard_map/pallas_call | solution.py:219
  43.6 6.5 %all-to-all-start = ((bf16[16,128,128]{2,1,0:T(8,128)(2,1)}), bf16[16,128,128]{2,1,0:T(8,128)(2,1)S(1)}, u32[]{:S(2)}, u32[]{:S(2)}) async-start(bf16[16,128,128]{2,1,0:T(8,128)(2,1)} %bitcast.10), calls=%async_computation | async-start | bytes 1048576 | tf_op jit(solution)/shard_map/all_to_all | solution.py:284
  50.0 0.1 shard_map.96
  50.1 1.9 %collective-permute-start.4 = (bf16[256,896]{1,0:T(8,128)(2,1)S(1)}, bf16[256,896]{1,0:T(8,128)(2,1)S(1)}, u32[]{:S(2)}, u32[]{:S(2)}) collective-permute-start(bf16[256,896]{1,0:T(8,128)(2,1)S(1)} %get-tuple-element.31), channel_id=1, source_target_pairs={{0,512},{512,0},{1,513},{513,1},{2,514},{514,2},{3,515},{515,3},{4... | collective-permute-start | bytes 1376264 | tf_op jit(solution)/shard_map/ppermute | solution.py:280
  52.0 2.0 %collective-permute-start.5 = (bf16[256,896]{1,0:T(8,128)(2,1)S(1)}, bf16[256,896]{1,0:T(8,128)(2,1)S(1)}, u32[]{:S(2)}, u32[]{:S(2)}) collective-permute-start(bf16[256,896]{1,0:T(8,128)(2,1)S(1)} %get-tuple-element.30.pair), channel_id=1, source_target_pairs={{0,1},{1,0},{2,3},{3,2},{4,5},{5,4},{6,7},{7,6},{8,9},{9,8},{10,11... | collective-permute-start | bytes 1376264 | tf_op jit(solution)/shard_map/ppermute | solution.py:281
  54.1 10.0 %collective-permute-done.4.across = bf16[256,896]{1,0:T(8,128)(2,1)S(1)} collective-permute-done((bf16[256,896]{1,0:T(8,128)(2,1)S(1)}, bf16[256,896]{1,0:T(8,128)(2,1)S(1)}, u32[]{:S(2)}, u32[]{:S(2)}) %collective-permute-start.4) | collective-permute-done | bytes 458784 | tf_op jit(solution)/shard_map/ppermute | solution.py:280
  64.1 2.8 %collective-permute-start.6 = (bf16[256,896]{1,0:T(8,128)(2,1)S(1)}, bf16[256,896]{1,0:T(8,128)(2,1)S(1)}, u32[]{:S(2)}, u32[]{:S(2)}) collective-permute-start(bf16[256,896]{1,0:T(8,128)(2,1)S(1)} %collective-permute-done.4.across), channel_id=1, source_target_pairs={{0,1},{1,0},{2,3},{3,2},{4,5},{5,4},{6,7},{7,6},{8,9},{9,8},{10,11... | collective-permute-start | bytes 1376264 | tf_op jit(solution)/shard_map/ppermute | solution.py:283
  66.9 1.3 collective-permute-start.3
  68.2 3.4 %collective-permute-done.3.got = bf16[128,128]{1,0:T(8,128)(2,1)S(1)} collective-permute-done((bf16[128,128]{1,0:T(8,128)(2,1)S(1)}, bf16[128,128]{1,0:T(8,128)(2,1)S(1)}, u32[]{:S(2)}, u32[]{:S(2)}) %collective-permute-start.3) | collective-permute-done | bytes 32800 | tf_op jit(solution)/shard_map/ppermute | solution.py:282
  71.5 0.0 all-to-all-done.pieces
  71.5 0.7 shard_map.97
  72.2 13.6 %all-gather = bf16[1024,256]{1,0:T(8,128)(2,1)S(1)} all-gather(bf16[128,256]{1,0:T(8,128)(2,1)S(1)} %shard_map.97), channel_id=2, replica_groups=mesh['grp'=2,'dp'=16,'zl'=2,'x'=8,'core'=2] {'grp','zl','core'}, dimensions={0}, use_global_device_ids=true | all-gather | bytes 589824 | tf_op jit(solution)/shard_map/all_gather | solution.py:290
  85.8 0.0 collective-permute-done.5.beside
  85.8 0.0 collective-permute-done.6.corner
  85.8 1.2 shard_map.98
  87.0 17.6 %all_to_all.15.pieces = bf16[8,16,896]{2,1,0:T(8,128)(2,1)S(1)} all-to-all(bf16[8,16,896]{2,1,0:T(8,128)(2,1)S(1)} %shard_map.98), channel_id=1, replica_groups=mesh['grp'=2,'dp'=16,'zl'=2,'x'=8,'core'=2] {'x'}, dimensions={0} | all-to-all | bytes 458752 | tf_op jit(solution)/shard_map/all_to_all | solution.py:298
  104.6 0.0 copy-start.1
  104.6 0.0 copy-start.2
  104.6 0.1 shard_map.99
  104.7 27.9 %all_to_all.16.pieces = f32[16,8,128]{2,1,0:T(8,128)S(1)} all-to-all(f32[16,8,128]{2,1,0:T(8,128)S(1)} %shard_map.99), channel_id=1, replica_groups=mesh['grp'=2,'dp'=16,'zl'=2,'x'=8,'core'=2] {'dp'}, dimensions={0} | all-to-all | bytes 131072 | tf_op jit(solution)/shard_map/all_to_all | solution.py:306
  132.7 0.0 copy-done.1
  132.7 0.0 copy-done.2
  132.7 0.7 shard_map.100
  (1 shorter events, 0.0 us)
Async XLA Ops:
  0.6 4.4 %copy-start = (bf16[1,128,256]{2,1,0:T(8,128)(2,1)S(1)}, bf16[1,128,256]{2,1,0:T(8,128)(2,1)}, u32[]{:S(2)}) copy-start(bf16[1,128,256]{2,1,0:T(8,128)(2,1)} %param.9) | copy-start | bytes 196612
  0.6 17.3 %collective-permute-start = (bf16[128,256]{1,0:T(8,128)(2,1)}, bf16[128,256]{1,0:T(8,128)(2,1)S(1)}, u32[]{:S(2)}, u32[]{:S(2)}) collective-permute-start(bf16[128,256]{1,0:T(8,128)(2,1)} %bitcast.18), channel_id=1, source_target_pairs={{0,512},{1,513},{2,514},{3,515},{4,516},{5,517},{6,518},{7,519},{8... | collective-permute-start | bytes 196616 | tf_op jit(solution)/shard_map/ppermute | solution.py:249
  5.0 0.7 copy-start.8
  5.7 1.2 copy-start.3
  6.9 1.0 copy-start.4
  7.9 1.0 copy-start.6
  8.9 32.0 %copy-start.7 = (bf16[1,128,1792]{2,1,0:T(8,128)(2,1)S(1)}, bf16[1,128,1792]{2,1,0:T(8,128)(2,1)}, u32[]{:S(2)}) copy-start(bf16[1,128,1792]{2,1,0:T(8,128)(2,1)} %param.10) | copy-start | bytes 1376260
  10.6 30.3 %copy-start.5 = (bf16[1,128,1792]{2,1,0:T(8,128)(2,1)S(1)}, bf16[1,128,1792]{2,1,0:T(8,128)(2,1)}, u32[]{:S(2)}) copy-start(bf16[1,128,1792]{2,1,0:T(8,128)(2,1)} %param.8) | copy-start | bytes 1376260
  10.6 30.3 %collective-permute-start.1 = (bf16[256,896]{1,0:T(8,128)(2,1)S(1)}, bf16[256,896]{1,0:T(8,128)(2,1)S(1)}, u32[]{:S(2)}, u32[]{:S(2)}) collective-permute-start(bf16[256,896]{1,0:T(8,128)(2,1)S(1)} %get-tuple-element.19), channel_id=1, source_target_pairs={{0,16},{16,0},{1,17},{17,1},{2,18},{18,2},{3,19},{19,3},{4,20},{20... | collective-permute-start | bytes 1376264 | tf_op jit(solution)/shard_map/ppermute | solution.py:260
  15.7 25.2 %collective-permute-start.2 = (bf16[128,1792]{1,0:T(8,128)(2,1)S(1)}, bf16[128,1792]{1,0:T(8,128)(2,1)S(1)}, u32[]{:S(2)}, u32[]{:S(2)}) collective-permute-start(bf16[128,1792]{1,0:T(8,128)(2,1)S(1)} %get-tuple-element.21), channel_id=1, source_target_pairs={{0,512},{1,513},{2,514},{3,515},{4,516},{5,517},{6,518},{7,519},{8... | collective-permute-start | bytes 1376264 | tf_op jit(solution)/shard_map/ppermute | solution.py:259
  43.6 28.0 %all-to-all-start = ((bf16[16,128,128]{2,1,0:T(8,128)(2,1)}), bf16[16,128,128]{2,1,0:T(8,128)(2,1)S(1)}, u32[]{:S(2)}, u32[]{:S(2)}) async-start(bf16[16,128,128]{2,1,0:T(8,128)(2,1)} %bitcast.10), calls=%async_computation | async-start | bytes 1048576 | tf_op jit(solution)/shard_map/all_to_all | solution.py:284
  50.1 14.0 %collective-permute-start.4 = (bf16[256,896]{1,0:T(8,128)(2,1)S(1)}, bf16[256,896]{1,0:T(8,128)(2,1)S(1)}, u32[]{:S(2)}, u32[]{:S(2)}) collective-permute-start(bf16[256,896]{1,0:T(8,128)(2,1)S(1)} %get-tuple-element.31), channel_id=1, source_target_pairs={{0,512},{512,0},{1,513},{513,1},{2,514},{514,2},{3,515},{515,3},{4... | collective-permute-start | bytes 1376264 | tf_op jit(solution)/shard_map/ppermute | solution.py:280
  52.0 33.8 %collective-permute-start.5 = (bf16[256,896]{1,0:T(8,128)(2,1)S(1)}, bf16[256,896]{1,0:T(8,128)(2,1)S(1)}, u32[]{:S(2)}, u32[]{:S(2)}) collective-permute-start(bf16[256,896]{1,0:T(8,128)(2,1)S(1)} %get-tuple-element.30.pair), channel_id=1, source_target_pairs={{0,1},{1,0},{2,3},{3,2},{4,5},{5,4},{6,7},{7,6},{8,9},{9,8},{10,11... | collective-permute-start | bytes 1376264 | tf_op jit(solution)/shard_map/ppermute | solution.py:281
  64.1 21.7 %collective-permute-start.6 = (bf16[256,896]{1,0:T(8,128)(2,1)S(1)}, bf16[256,896]{1,0:T(8,128)(2,1)S(1)}, u32[]{:S(2)}, u32[]{:S(2)}) collective-permute-start(bf16[256,896]{1,0:T(8,128)(2,1)S(1)} %collective-permute-done.4.across), channel_id=1, source_target_pairs={{0,1},{1,0},{2,3},{3,2},{4,5},{5,4},{6,7},{7,6},{8,9},{9,8},{10,11... | collective-permute-start | bytes 1376264 | tf_op jit(solution)/shard_map/ppermute | solution.py:283
  66.9 4.7 %collective-permute-start.3 = (bf16[128,128]{1,0:T(8,128)(2,1)S(1)}, bf16[128,128]{1,0:T(8,128)(2,1)S(1)}, u32[]{:S(2)}, u32[]{:S(2)}) collective-permute-start(bf16[128,128]{1,0:T(8,128)(2,1)S(1)} %get-tuple-element.29), channel_id=1, source_target_pairs={{512,0},{513,1},{514,2},{515,3},{516,4},{517,5},{518,6},{519,7},{5... | collective-permute-start | bytes 98312 | tf_op jit(solution)/shard_map/ppermute | solution.py:282
  104.6 28.0 %copy-start.1 = (f32[56,16]{0,1:T(8,128)S(1)}, f32[56,16]{0,1:T(8,128)}, u32[]{:S(2)}) copy-start(f32[56,16]{0,1:T(8,128)} %param.12) | copy-start | bytes 10756
  104.6 28.0 %copy-start.2 = (f32[56,16]{0,1:T(8,128)S(1)}, f32[56,16]{0,1:T(8,128)}, u32[]{:S(2)}) copy-start(f32[56,16]{0,1:T(8,128)} %param.13) | copy-start | bytes 10756

commit v4 on v2

--- a/solution.py
+++ b/solution.py
@@ -86,28 +86,28 @@
 
     lax.fori_loop(high + 1, seq // CHUNK, clear, 0)
 
-    def larger(x, top):
-        return jnp.maximum(top, jnp.max(x.reshape(CHUNK // 8, 8, width), axis=0))
-
-    def inner(c, top):
+    def absorb(x, top, total):
+        x = x.reshape(CHUNK // 8, 8, width)
+        larger = jnp.maximum(top, jnp.max(x, axis=0))
+        total = total * jnp.exp2(top - larger) + jnp.sum(jnp.exp2(x - larger), axis=0)
+        return larger, total
+
+    def inner(c, carry):
         x = product(k[chunk_rows(c), :], qs[...], 1) * GAIN
         s[chunk_rows(c), :] = x
-        return larger(x, top)
-
-    top = lax.fori_loop(0, high, inner, jnp.full((8, width), masked_score, jnp.float32))
+        return absorb(x, *carry)
+
+    empty = jnp.full((8, width), masked_score, jnp.float32), jnp.zeros((8, width), jnp.float32)
+    top, total = lax.fori_loop(0, high, inner, empty)
     query_pos = first_row + lanes_of_queries(lax.broadcasted_iota(jnp.int32, (1, rows), 1))
     key_pos = high * CHUNK + lax.broadcasted_iota(jnp.int32, (CHUNK, width), 0)
     x = product(k[chunk_rows(high), :], qs[...], 1) * GAIN
     x = jnp.where(key_pos <= query_pos, x, masked_score)
     s[chunk_rows(high), :] = x
-    top = jnp.max(larger(x, top), axis=0, keepdims=True)
-
-    def weigh(c, total):
-        p = jnp.exp2(s[chunk_rows(c), :] - top)
-        return total + jnp.sum(p.reshape(CHUNK // 8, 8, width), axis=0)
-
-    total = lax.fori_loop(0, high + 1, weigh, jnp.zeros((8, width), jnp.float32))
-    shift = top + jnp.log2(jnp.sum(total, axis=0, keepdims=True))
+    top, total = absorb(x, top, total)
+    most = jnp.max(top, axis=0, keepdims=True)
+    total = jnp.sum(total * jnp.exp2(top - most), axis=0, keepdims=True)
+    shift = most + jnp.log2(total)
 
     def collect(c):
         p = jnp.exp2(s[chunk_rows(c), :] - shift).astype(ds.dtype)
@@ -220,24 +220,14 @@
     place = jnp.stack([group, first_row, first_row // CHUNK, index, core]).astype(jnp.int32)
     q, d, k = queries[0], d_out[0], keys[0]
 
-    down = [(0, 1)]
-    other_k = lax.ppermute(k[:, HD:], "grp", down)
+    down, swap = [(0, 1)], [(0, 1), (1, 0)]
+    other_k = lax.ppermute(k, "grp", down)
     other = lax.ppermute(jnp.concatenate([q[:, heads:], d[:, heads:]], axis=1), "grp", down)
-    short = call(
-        local_kernel,
-        shape((rows, cols), bf16),
-        [place],
-        [doc_start, q, d, k],
-        [pltpu.VMEM((heads, HD), bf16), pltpu.VMEM((heads, HD), bf16)],
-        flops=3 * 10**9,
-    )
     lower, upper = layer_input[0, :, :half], layer_input[0, :, half:]
     mine = jnp.where(group == 0, lower, upper)
     theirs = jnp.where(group == 0, upper, lower)
-    theirs, other_k, short = lax.optimization_barrier((theirs, other_k, short))
-    swap = [(0, 1), (1, 0)]
     across = lax.ppermute(theirs, "grp", swap)
-    chosen = jnp.where(group == 0, k[:, :HD], other_k)
+    chosen = jnp.where(group == 0, k[:, :HD], other_k[:, HD:])
     all_keys = lax.all_gather(chosen, ("x", "core"), axis=0, tiled=True)
     partial, own = call(
         long_kernel,
@@ -251,7 +241,16 @@
         ],
         flops=6 * 10**9,
     )
-    mine, across, own = lax.optimization_barrier((mine, across, own))
+    partial, across = lax.optimization_barrier((partial, across))
+    mine, begin, own = lax.optimization_barrier((mine, doc_start, own))
+    short = call(
+        local_kernel,
+        shape((rows, cols), bf16),
+        [place],
+        [begin, q, d, k],
+        [pltpu.VMEM((heads, HD), bf16), pltpu.VMEM((heads, HD), bf16)],
+        flops=3 * 10**9,
+    )
     beside = lax.ppermute(mine, "core", swap)
     corner = lax.ppermute(across, "core", swap)
     pieces = lax.all_to_all(

time: 123 us -> 118 us (0.959)
  the two profiles are of different devices: /device:TPU:1 before, /device:TPU:16 now
where the time goes in v4:
time: 118 us
  blocking collectives  69.6 us (59%)
  starting transfers between devices  28.4 us (24%)
  waiting for transfers between devices  10.2 us (9%)
  Pallas kernels  6.74 us (6%)
  local copies, waits for them, and re-layouts  1.18 us (1%)
    all_to_all x1, blocking collectives, body(): landed = lax.all_to_all(sent, 'dp', 0, 0, tiled=True)  27 us
    all_to_all x1, blocking collectives, body(): terms = lax.all_to_all(gradient, 'x', 0, 0, tiled=True)  20 us
    all_gather x1, blocking collectives, body(): all_keys = lax.all_gather(chosen, ('x', 'core'), axis=0, tiled=True)  15.7 us
    ppermute x1, starting transfers between devices, body(): across = lax.ppermute(theirs, 'grp', swap)  15 us
    all_to_all x1, waiting for transfers between devices, body(): lax.all_to_all(partial.reshape(blocks, rows, HD), ('x', 'core'), 0, 0, ti...  10.2 us
    all_gather x1, blocking collectives, body(): values = lax.all_gather(values, ('grp', 'core'), axis=0)  6.86 us
    pallas_call x6, Pallas kernels, call(): pl.pallas_call(kernel, out_shape=out, in_specs=[SCALARS] * len(scalars) +...  6.74 us
    all_to_all x1, starting transfers between devices, body(): lax.all_to_all(partial.reshape(blocks, rows, HD), ('x', 'core'), 0, 0, ti...  6.3 us
  transfers between devices with their start and end apart: 6, of which 1 were waited for; matrix products, arithmetic and copies ran while one was open for 2% of the time, Pallas kernels for 4%

profile of v4, /device:TPU:16, one launch (start us, length us, event | category | flops | bytes accessed | tf_op | source)
XLA Modules:
  0.0 117.8 jit_solution(17805863410202967121)
XLA Ops:
  0.6 0.0 copy-start.1
  0.6 1.4 %collective-permute-start.1 = (bf16[128,256]{1,0:T(8,128)(2,1)}, bf16[128,256]{1,0:T(8,128)(2,1)S(1)}, u32[]{:S(2)}, u32[]{:S(2)}) collective-permute-start(bf16[128,256]{1,0:T(8,128)(2,1)} %bitcast.26), channel_id=1, source_target_pairs={{0,512},{1,513},{2,514},{3,515},{4,516},{5,517},{6,518},{7,519},{8... | collective-permute-start | bytes 196616 | tf_op jit(solution)/shard_map/ppermute | solution.py:224
  2.1 0.0 copy-start.6
  2.1 1.0 slice.24
  3.1 0.0 copy-done.1
  3.2 1.3 %collective-permute-start = (bf16[128,1792]{1,0:T(8,128)(2,1)S(1)}, bf16[128,1792]{1,0:T(8,128)(2,1)S(1)}, u32[]{:S(2)}, u32[]{:S(2)}) collective-permute-start(bf16[128,1792]{1,0:T(8,128)(2,1)S(1)} %pad_maximum_fusion), channel_id=1, source_target_pairs={{0,512},{1,513},{2,514},{3,515},{4,516},{5,517},{6,518},{7,519},{8... | collective-permute-start | bytes 1376264 | tf_op jit(solution)/shard_map/ppermute | solution.py:225
  4.5 0.0 copy-done.6
  4.5 0.0 copy-start.2
  4.5 0.8 select_bitcast_fusion
  5.4 0.0 copy-start
  5.4 15.0 %collective-permute-start.2 = (bf16[128,1792]{1,0:T(8,128)(2,1)}, bf16[128,1792]{1,0:T(8,128)(2,1)S(1)}, u32[]{:S(2)}, u32[]{:S(2)}) collective-permute-start(bf16[128,1792]{1,0:T(8,128)(2,1)} %get-tuple-element.23), channel_id=1, source_target_pairs={{0,512},{512,0},{1,513},{513,1},{2,514},{514,2},{3,515},{515,3},{4... | collective-permute-start | bytes 1376264 | tf_op jit(solution)/shard_map/ppermute | solution.py:229
  20.4 0.1 stack.23.place
  20.5 0.0 collective-permute-done.1
  20.5 0.0 copy-done.2
  20.6 15.7 %all_gather.9.k = bf16[2048,128]{1,0:T(8,128)(2,1)S(1)} all-gather(bf16[128,128]{1,0:T(8,128)(2,1)S(1)} %slice_select_fusion), channel_id=1, replica_groups=mesh['grp'=2,'dp'=32,'x'=8,'core'=2] {'x','core'}, dimensions={0}, use_global_device_ids=true | all-gather | bytes 557056 | tf_op jit(solution)/shard_map/all_gather | solution.py:231
  36.3 0.0 collective-permute-done.other
  36.3 0.0 copy-done
  36.3 2.6 %shard_map.94 = (bf16[2048,128]{1,0:T(8,128)(2,1)}, f32[128,128]{1,0:T(8,128)S(1)}) custom-call(s32[5]{0:T(128)S(1)} %stack.23.place, bf16[128,1792]{1,0:T(8,128)(2,1)S(1)} %bitcast.21, bf16[128,1792]{1,0:T(8,128)(2,1)S(1)} %bitcast.24, bf16[128,1792]{1,0:T(8,128)(2,1)S(1)} %collective-permute-done.other, bf16[2048,128]{1,0:T(8,128)(2,1)S(1)} %all_gather.9.k), custom_call_target="tpu_custom_call" | custom-call | flops 6000000000 | tf_op jit(solution)/shard_map/pallas_call | solution.py:194
  38.9 0.0 collective-permute-done.2.across
  38.9 6.3 %all-to-all-start = ((bf16[16,128,128]{2,1,0:T(8,128)(2,1)}), bf16[16,128,128]{2,1,0:T(8,128)(2,1)S(1)}, u32[]{:S(2)}, u32[]{:S(2)}) async-start(bf16[16,128,128]{2,1,0:T(8,128)(2,1)} %bitcast.10), calls=%async_computation | async-start | bytes 1048576 | tf_op jit(solution)/shard_map/all_to_all | solution.py:256
  45.2 0.0 copy-start.5
  45.3 2.3 %collective-permute-start.3 = (bf16[128,1792]{1,0:T(8,128)(2,1)S(1)}, bf16[128,1792]{1,0:T(8,128)(2,1)S(1)}, u32[]{:S(2)}, u32[]{:S(2)}) collective-permute-start(bf16[128,1792]{1,0:T(8,128)(2,1)S(1)} %get-tuple-element.18.mine), channel_id=1, source_target_pairs={{0,1},{1,0},{2,3},{3,2},{4,5},{5,4},{6,7},{7,6},{8,9},{9,8},{10,11... | collective-permute-start | bytes 1376264 | tf_op jit(solution)/shard_map/ppermute | solution.py:254
  47.6 2.0 %collective-permute-start.4 = (bf16[128,1792]{1,0:T(8,128)(2,1)S(1)}, bf16[128,1792]{1,0:T(8,128)(2,1)S(1)}, u32[]{:S(2)}, u32[]{:S(2)}) collective-permute-start(bf16[128,1792]{1,0:T(8,128)(2,1)S(1)} %collective-permute-done.2.across), channel_id=1, source_target_pairs={{0,1},{1,0},{2,3},{3,2},{4,5},{5,4},{6,7},{7,6},{8,9},{9,8},{10,11... | collective-permute-start | bytes 1376264 | tf_op jit(solution)/shard_map/ppermute | solution.py:255
  49.6 0.0 copy-done.5
  49.6 1.5 %shard_map.95.short = bf16[128,256]{1,0:T(8,128)(2,1)S(1)} custom-call(s32[5]{0:T(128)S(1)} %stack.23.place, s32[1,128]{1,0:T(1,128)S(1)} %copy-done.5, bf16[128,1792]{1,0:T(8,128)(2,1)S(1)} %bitcast.22, bf16[128,1792]{1,0:T(8,128)(2,1)S(1)} %bitcast.25, bf16[128,256]{1,0:T(8,128)(2,1)S(1)} %bitcast.28), custom_call_target="tpu_custom_call" | custom-call | flops 3000000000 | tf_op jit(solution)/shard_map/pallas_call | solution.py:194
  51.1 10.2 %all-to-all-done.pieces = bf16[16,128,128]{2,1,0:T(8,128)(2,1)S(1)} async-done(((bf16[16,128,128]{2,1,0:T(8,128)(2,1)}), bf16[16,128,128]{2,1,0:T(8,128)(2,1)S(1)}, u32[]{:S(2)}, u32[]{:S(2)}) %all-to-all-start) | async-done | bytes 524320 | tf_op jit(solution)/shard_map/all_to_all | solution.py:256
  61.3 0.7 shard_map.96
  61.9 6.9 %all-gather = bf16[512,384]{1,0:T(8,128)(2,1)S(1)} all-gather(bf16[128,384]{1,0:T(8,128)(2,1)S(1)} %shard_map.96), channel_id=2, replica_groups=mesh['grp'=2,'dp'=32,'x'=8,'core'=2] {'grp','core'}, dimensions={0}, use_global_device_ids=true | all-gather | bytes 491520 | tf_op jit(solution)/shard_map/all_gather | solution.py:260
  68.8 0.0 collective-permute-done.3.beside
  68.8 0.0 collective-permute-done.4.corner
  68.8 1.1 shard_map.97
  69.9 20.0 %all_to_all.15.pieces = bf16[8,16,1792]{2,1,0:T(8,128)(2,1)S(1)} all-to-all(bf16[8,16,1792]{2,1,0:T(8,128)(2,1)S(1)} %shard_map.97), channel_id=1, replica_groups=mesh['grp'=2,'dp'=32,'x'=8,'core'=2] {'x'}, dimensions={0} | all-to-all | bytes 917504 | tf_op jit(solution)/shard_map/all_to_all | solution.py:268
  89.8 0.0 copy-start.3
  89.8 0.0 copy-start.4
  89.9 0.2 shard_map.98
  90.0 27.0 %all_to_all.16.pieces = f32[32,8,128]{2,1,0:T(8,128)S(1)} all-to-all(f32[32,8,128]{2,1,0:T(8,128)S(1)} %shard_map.98), channel_id=1, replica_groups=mesh['grp'=2,'dp'=32,'x'=8,'core'=2] {'dp'}, dimensions={0} | all-to-all | bytes 262144 | tf_op jit(solution)/shard_map/all_to_all | solution.py:276
  117.0 0.0 copy-done.3
  117.0 0.0 copy-done.4
  117.0 0.7 shard_map.99
  (3 shorter events, 0.1 us)
Async XLA Ops:
  0.6 2.5 %copy-start.1 = (bf16[1,128,1792]{2,1,0:T(8,128)(2,1)S(1)}, bf16[1,128,1792]{2,1,0:T(8,128)(2,1)}, u32[]{:S(2)}) copy-start(bf16[1,128,1792]{2,1,0:T(8,128)(2,1)} %param.10) | copy-start | bytes 1376260
  0.6 19.9 %collective-permute-start.1 = (bf16[128,256]{1,0:T(8,128)(2,1)}, bf16[128,256]{1,0:T(8,128)(2,1)S(1)}, u32[]{:S(2)}, u32[]{:S(2)}) collective-permute-start(bf16[128,256]{1,0:T(8,128)(2,1)} %bitcast.26), channel_id=1, source_target_pairs={{0,512},{1,513},{2,514},{3,515},{4,516},{5,517},{6,518},{7,519},{8... | collective-permute-start | bytes 196616 | tf_op jit(solution)/shard_map/ppermute | solution.py:224
  2.1 2.4 %copy-start.6 = (bf16[1,128,3584]{2,1,0:T(8,128)(2,1)S(1)}, bf16[1,128,3584]{2,1,0:T(8,128)(2,1)}, u32[]{:S(2)}) copy-start(bf16[1,128,3584]{2,1,0:T(8,128)(2,1)} %param.7) | copy-start | bytes 2752516
  3.2 33.1 %collective-permute-start = (bf16[128,1792]{1,0:T(8,128)(2,1)S(1)}, bf16[128,1792]{1,0:T(8,128)(2,1)S(1)}, u32[]{:S(2)}, u32[]{:S(2)}) collective-permute-start(bf16[128,1792]{1,0:T(8,128)(2,1)S(1)} %pad_maximum_fusion), channel_id=1, source_target_pairs={{0,512},{1,513},{2,514},{3,515},{4,516},{5,517},{6,518},{7,519},{8... | collective-permute-start | bytes 1376264 | tf_op jit(solution)/shard_map/ppermute | solution.py:225
  4.5 16.0 %copy-start.2 = (bf16[1,128,256]{2,1,0:T(8,128)(2,1)S(1)}, bf16[1,128,256]{2,1,0:T(8,128)(2,1)}, u32[]{:S(2)}) copy-start(bf16[1,128,256]{2,1,0:T(8,128)(2,1)} %param.9) | copy-start | bytes 196612
  5.4 30.9 %copy-start = (bf16[1,128,1792]{2,1,0:T(8,128)(2,1)S(1)}, bf16[1,128,1792]{2,1,0:T(8,128)(2,1)}, u32[]{:S(2)}) copy-start(bf16[1,128,1792]{2,1,0:T(8,128)(2,1)} %param.8) | copy-start | bytes 1376260
  5.4 33.6 %collective-permute-start.2 = (bf16[128,1792]{1,0:T(8,128)(2,1)}, bf16[128,1792]{1,0:T(8,128)(2,1)S(1)}, u32[]{:S(2)}, u32[]{:S(2)}) collective-permute-start(bf16[128,1792]{1,0:T(8,128)(2,1)} %get-tuple-element.23), channel_id=1, source_target_pairs={{0,512},{512,0},{1,513},{513,1},{2,514},{514,2},{3,515},{515,3},{4... | collective-permute-start | bytes 1376264 | tf_op jit(solution)/shard_map/ppermute | solution.py:229
  38.9 22.3 %all-to-all-start = ((bf16[16,128,128]{2,1,0:T(8,128)(2,1)}), bf16[16,128,128]{2,1,0:T(8,128)(2,1)S(1)}, u32[]{:S(2)}, u32[]{:S(2)}) async-start(bf16[16,128,128]{2,1,0:T(8,128)(2,1)} %bitcast.10), calls=%async_computation | async-start | bytes 1048576 | tf_op jit(solution)/shard_map/all_to_all | solution.py:256
  45.2 4.4 %copy-start.5 = (s32[1,128]{1,0:T(1,128)S(1)}, s32[1,128]{1,0:T(1,128)}, u32[]{:S(2)}) copy-start(s32[1,128]{1,0:T(1,128)} %begin) | copy-start | bytes 1540
  45.3 23.5 %collective-permute-start.3 = (bf16[128,1792]{1,0:T(8,128)(2,1)S(1)}, bf16[128,1792]{1,0:T(8,128)(2,1)S(1)}, u32[]{:S(2)}, u32[]{:S(2)}) collective-permute-start(bf16[128,1792]{1,0:T(8,128)(2,1)S(1)} %get-tuple-element.18.mine), channel_id=1, source_target_pairs={{0,1},{1,0},{2,3},{3,2},{4,5},{5,4},{6,7},{7,6},{8,9},{9,8},{10,11... | collective-permute-start | bytes 1376264 | tf_op jit(solution)/shard_map/ppermute | solution.py:254
  47.6 21.2 %collective-permute-start.4 = (bf16[128,1792]{1,0:T(8,128)(2,1)S(1)}, bf16[128,1792]{1,0:T(8,128)(2,1)S(1)}, u32[]{:S(2)}, u32[]{:S(2)}) collective-permute-start(bf16[128,1792]{1,0:T(8,128)(2,1)S(1)} %collective-permute-done.2.across), channel_id=1, source_target_pairs={{0,1},{1,0},{2,3},{3,2},{4,5},{5,4},{6,7},{7,6},{8,9},{9,8},{10,11... | collective-permute-start | bytes 1376264 | tf_op jit(solution)/shard_map/ppermute | solution.py:255
  89.8 27.2 %copy-start.3 = (f32[56,16]{0,1:T(8,128)S(1)}, f32[56,16]{0,1:T(8,128)}, u32[]{:S(2)}) copy-start(f32[56,16]{0,1:T(8,128)} %param.12) | copy-start | bytes 10756
  89.8 27.2 %copy-start.4 = (f32[56,16]{0,1:T(8,128)S(1)}, f32[56,16]{0,1:T(8,128)}, u32[]{:S(2)}) copy-start(f32[56,16]{0,1:T(8,128)} %param.13) | copy-start | bytes 10756

commit v5 on v4

--- a/solution.py
+++ b/solution.py
@@ -32,13 +32,31 @@
     return jnp.concatenate([row] * GROUP, axis=1)
 
 
-def local_kernel(place, begin, q, d, k, out, qs, ds):
+def by_parity(matrix, share):
+    width = matrix.shape[1]
+    old = lax.broadcasted_iota(jnp.int32, (width, width), 0)
+    new = lax.broadcasted_iota(jnp.int32, (width, width), 1)
+    half = width // 2
+    within = new % half
+    source = (2 * (within // share) + new // half) * share + within % share
+    chosen = jnp.where(old == source, 1.0, 0.0).astype(matrix.dtype)
+    return product(matrix, chosen, 0).astype(matrix.dtype)
+
+
+def join(a, b, parity):
+    half = a.shape[1] // 2
+    part = slice(parity * half, (parity + 1) * half)
+    return jnp.concatenate([a[:, part], b[:, part]], axis=1)
+
+
+def local_kernel(share, place, begin, q, d, k, stay, leave, qs, ds):
     rows = q.shape[0]
     width = GROUP * rows
 
     @pl.when(place[0] == 0)
     def _():
-        out[...] = jnp.zeros(out.shape, out.dtype)
+        stay[...] = jnp.zeros(stay.shape, stay.dtype)
+        leave[...] = jnp.zeros(leave.shape, leave.dtype)
 
     @pl.when(place[0] == 1)
     def _():
@@ -46,6 +64,7 @@
         query_pos = lanes_of_queries(lax.broadcasted_iota(jnp.int32, (1, rows), 1))
         key_pos = lax.broadcasted_iota(jnp.int32, (rows, width), 0)
         visible = (key_pos >= first) & (key_pos <= query_pos)
+        sums = []
         for g in range(KV_HEADS):
             for r in range(GROUP):
                 h = g * GROUP + r
@@ -56,10 +75,13 @@
             top = jnp.max(x, axis=0, keepdims=True)
             shift = top + jnp.log2(jnp.sum(jnp.exp2(x - top), axis=0, keepdims=True))
             p = jnp.exp2(x - shift).astype(ds.dtype)
-            out[:, cols] = product(p, ds[...], 0).astype(out.dtype)
-
-
-def long_kernel(place, q, d, other, k, out, own, qs, ds, s):
+            sums.append(product(p, by_parity(ds[...], share), 0))
+        even, odd = (join(*sums, parity).astype(stay.dtype) for parity in range(2))
+        stay[...] = jnp.where(place[4] == 0, even, odd)
+        leave[...] = jnp.where(place[4] == 0, odd, even)
+
+
+def long_kernel(share, place, q, d, other, k, out, qs, ds, s):
     seq, rows = k.shape[0], q.shape[0]
     width = GROUP * rows
     first_row, high = place[1], place[2]
@@ -76,6 +98,8 @@
             h = GROUP + r
             qs[r * rows : (r + 1) * rows, :] = other[:, r * HD : (r + 1) * HD]
             ds[r * rows : (r + 1) * rows, :] = other[:, h * HD : (h + 1) * HD]
+
+    ds[...] = by_parity(ds[...], share)
 
     def chunk_rows(c):
         return pl.ds(pl.multiple_of(c * CHUNK, CHUNK), CHUNK)
@@ -109,51 +133,45 @@
     total = jnp.sum(total * jnp.exp2(top - most), axis=0, keepdims=True)
     shift = most + jnp.log2(total)
 
-    def collect(c):
+    def collect(c, carry):
         p = jnp.exp2(s[chunk_rows(c), :] - shift).astype(ds.dtype)
         block = product(p, ds[...], 0)
-        out[chunk_rows(c), :] = block.astype(out.dtype)
-        return block
-
-    def inner_collect(c, carry):
-        collect(c)
+        for i in range(0, CHUNK // rows, 2):
+            pair = [block[(i + n) * rows : (i + n + 1) * rows] for n in range(2)]
+            for parity in range(2):
+                at = pl.ds(pl.multiple_of(c * CHUNK + (i + parity) * rows, rows), rows)
+                out[at, :] = join(*pair, parity).astype(out.dtype)
         return carry
 
-    lax.fori_loop(0, high, inner_collect, 0)
-    block = collect(high)
-    for i in range(CHUNK // rows):
-
-        @pl.when(first_row == high * CHUNK + i * rows)
-        def _():
-            own[...] = block[i * rows : (i + 1) * rows]
-
-
-def value_kernel(place, own, pieces, short, out):
-    total = own[...]
-    for i in range(pieces.shape[0]):
-        total = total + jnp.where(place[3] == i, 0.0, pieces[i].astype(jnp.float32))
+    lax.fori_loop(0, high + 1, collect, 0)
+
+
+def value_kernel(pieces, stay, got, out):
+    total = pieces[0].astype(jnp.float32)
+    for i in range(1, pieces.shape[0]):
+        total = total + pieces[i].astype(jnp.float32)
     out[:, :HD] = total.astype(out.dtype)
-    out[:, HD:] = short[...]
+    out[:, HD : 2 * HD] = stay[...]
+    out[:, 2 * HD :] = got[...]
 
 
 def project_kernel(place, values, mine, across, beside, corner, out, turned, vg):
     share = out.shape[1]
     rows = values.shape[1]
     group, core = place[0], place[4]
-    for c in range(2):
-        for g in range(KV_HEADS):
-            heads = slice(g * HD, (g + 1) * HD)
-            part = values[2 * g + c, :, :HD].astype(jnp.float32)
-            turned[c, heads, :] = jnp.transpose(part)
-            part = values[2 + c, :, (1 + g) * HD : (2 + g) * HD].astype(jnp.float32)
-            turned[2 + c, heads, :] = jnp.transpose(part)
+    half = HD // 2
+    for g in range(KV_HEADS):
+        part = jnp.transpose(values[g, :, :HD].astype(jnp.float32))
+        for c in range(2):
+            turned[c, g * half : (g + 1) * half, :] = part[c * half : (c + 1) * half]
+    for n in range(2):
+        part = values[1, :, (1 + n) * HD : (2 + n) * HD].astype(jnp.float32)
+        turned[2 + n] = jnp.transpose(part)
     for j in range(4):
-        g = jnp.where(j % 2 == 0, group, 1 - group)
-        c = jnp.where(j // 2 == 0, core, 1 - core)
-        for i in range(out.shape[0]):
-            chunk = pl.ds(pl.multiple_of((2 * i + core) * share, share), share)
-            block = turned[2 * g + c, chunk, :].astype(vg.dtype)
-            vg[i * share : (i + 1) * share, j * rows : (j + 1) * rows] = block
+        g = group if j % 2 == 0 else 1 - group
+        c = core if j // 2 == 0 else 1 - core
+        block = turned[jnp.where(g == 0, c, 2 + j // 2)]
+        vg[:, j * rows : (j + 1) * rows] = block.astype(vg.dtype)
     for t in range(mine.shape[1] // TILE):
         part = slice(t * TILE, (t + 1) * TILE)
         x = jnp.concatenate(
@@ -229,9 +247,9 @@
     across = lax.ppermute(theirs, "grp", swap)
     chosen = jnp.where(group == 0, k[:, :HD], other_k[:, HD:])
     all_keys = lax.all_gather(chosen, ("x", "core"), axis=0, tiled=True)
-    partial, own = call(
-        long_kernel,
-        (shape((seq, HD), bf16), shape((rows, HD), f32)),
+    partial = call(
+        functools.partial(long_kernel, share),
+        shape((seq, HD), bf16),
         [place],
         [q, d, other, all_keys],
         [
@@ -241,11 +259,11 @@
         ],
         flops=6 * 10**9,
     )
-    partial, across = lax.optimization_barrier((partial, across))
-    mine, begin, own = lax.optimization_barrier((mine, doc_start, own))
-    short = call(
-        local_kernel,
-        shape((rows, cols), bf16),
+    partial, across, mine, begin = lax.optimization_barrier((partial, across, mine, doc_start))
+    square = shape((rows, HD), bf16)
+    stay, leave = call(
+        functools.partial(local_kernel, share),
+        (square, square),
         [place],
         [begin, q, d, k],
         [pltpu.VMEM((heads, HD), bf16), pltpu.VMEM((heads, HD), bf16)],
@@ -253,17 +271,18 @@
     )
     beside = lax.ppermute(mine, "core", swap)
     corner = lax.ppermute(across, "core", swap)
+    got = lax.ppermute(leave, "core", swap)
     pieces = lax.all_to_all(
         partial.reshape(blocks, rows, HD), ("x", "core"), 0, 0, tiled=True
     )
-    values = call(value_kernel, shape((rows, HD + cols), bf16), [place], [own, pieces, short])
-    values = lax.all_gather(values, ("grp", "core"), axis=0)
+    values = call(value_kernel, shape((rows, 3 * HD), bf16), [], [pieces, stay, got])
+    values = lax.all_gather(values, "grp", axis=0)
     gradient = call(
         project_kernel,
         shape((chips, share, half), bf16),
         [place],
         [values, mine, across, beside, corner],
-        [pltpu.VMEM((4, cols, rows), f32), pltpu.VMEM((cols // 2, 4 * rows), bf16)],
+        [pltpu.VMEM((4, cols // 2, rows), f32), pltpu.VMEM((cols // 2, 4 * rows), bf16)],
     )
     terms = lax.all_to_all(gradient, "x", 0, 0, tiled=True)
     sent = call(

time: 118 us -> 116 us (0.983)
  starting transfers between devices: 28.4 us -> 31 us
  waiting for transfers between devices: 10.2 us -> 7.81 us
  blocking collectives: 69.6 us -> 67.7 us
    all_to_all x1, waiting for transfers between devices: 10.2 us -> 6.96 us  [body(): lax.all_to_all(partial.reshape(blocks, rows, HD), ('x', 'core'), 0, 0, ti...]
    ppermute x0 -> x1, starting transfers between devices: none -> 2.31 us  [body(): got = lax.ppermute(leave, 'core', swap)]
    all_gather x1, blocking collectives: 6.86 us -> 5.65 us  [body(): values = lax.all_gather(values, 'grp', axis=0)]
  transfers between devices with their start and end apart: 6 -> 7, of which waited for: 1 -> 2; matrix products, arithmetic and copies ran while one was open for 2% -> 2% of each run, Pallas kernels for 4% -> 4%
where the time goes in v5:
time: 116 us
  blocking collectives  67.7 us (58%)
  starting transfers between devices  31 us (27%)
  waiting for transfers between devices  7.81 us (7%)
  Pallas kernels  6.45 us (6%)
  local copies, waits for them, and re-layouts  1.18 us (1%)
    all_to_all x1, blocking collectives, body(): landed = lax.all_to_all(sent, 'dp', 0, 0, tiled=True)  26.9 us
    all_to_all x1, blocking collectives, body(): terms = lax.all_to_all(gradient, 'x', 0, 0, tiled=True)  19.4 us
    all_gather x1, blocking collectives, body(): all_keys = lax.all_gather(chosen, ('x', 'core'), axis=0, tiled=True)  15.7 us
    ppermute x1, starting transfers between devices, body(): across = lax.ppermute(theirs, 'grp', swap)  15 us
    all_to_all x1, waiting for transfers between devices, body(): lax.all_to_all(partial.reshape(blocks, rows, HD), ('x', 'core'), 0, 0, ti...  6.96 us
    all_to_all x1, starting transfers between devices, body(): lax.all_to_all(partial.reshape(blocks, rows, HD), ('x', 'core'), 0, 0, ti...  6.65 us
    pallas_call x6, Pallas kernels, call(): pl.pallas_call(kernel, out_shape=out, in_specs=[SCALARS] * len(scalars) +...  6.45 us
    all_gather x1, blocking collectives, body(): values = lax.all_gather(values, 'grp', axis=0)  5.65 us
  transfers between devices with their start and end apart: 7, of which 2 were waited for; matrix products, arithmetic and copies ran while one was open for 2% of the time, Pallas kernels for 4%

profile of v5, /device:TPU:16, one launch (start us, length us, event | category | flops | bytes accessed | tf_op | source)
XLA Modules:
  0.0 115.9 jit_solution(15815997186663066544)
XLA Ops:
  0.6 0.0 copy-start.1
  0.6 1.4 %collective-permute-start.1 = (bf16[128,256]{1,0:T(8,128)(2,1)}, bf16[128,256]{1,0:T(8,128)(2,1)S(1)}, u32[]{:S(2)}, u32[]{:S(2)}) collective-permute-start(bf16[128,256]{1,0:T(8,128)(2,1)} %bitcast.26), channel_id=1, source_target_pairs={{0,512},{1,513},{2,514},{3,515},{4,516},{5,517},{6,518},{7,519},{8... | collective-permute-start | bytes 196616 | tf_op jit(solution)/shard_map/ppermute | solution.py:242
  2.1 0.0 copy-start.6
  2.1 1.0 slice.24
  3.1 0.0 copy-done.1
  3.2 1.3 %collective-permute-start = (bf16[128,1792]{1,0:T(8,128)(2,1)S(1)}, bf16[128,1792]{1,0:T(8,128)(2,1)S(1)}, u32[]{:S(2)}, u32[]{:S(2)}) collective-permute-start(bf16[128,1792]{1,0:T(8,128)(2,1)S(1)} %pad_maximum_fusion), channel_id=1, source_target_pairs={{0,512},{1,513},{2,514},{3,515},{4,516},{5,517},{6,518},{7,519},{8... | collective-permute-start | bytes 1376264 | tf_op jit(solution)/shard_map/ppermute | solution.py:243
  4.5 0.0 copy-done.6
  4.5 0.0 copy-start.2
  4.5 0.8 select_bitcast_fusion
  5.4 0.0 copy-start
  5.4 15.0 %collective-permute-start.2 = (bf16[128,1792]{1,0:T(8,128)(2,1)}, bf16[128,1792]{1,0:T(8,128)(2,1)S(1)}, u32[]{:S(2)}, u32[]{:S(2)}) collective-permute-start(bf16[128,1792]{1,0:T(8,128)(2,1)} %get-tuple-element.22), channel_id=1, source_target_pairs={{0,512},{512,0},{1,513},{513,1},{2,514},{514,2},{3,515},{515,3},{4... | collective-permute-start | bytes 1376264 | tf_op jit(solution)/shard_map/ppermute | solution.py:247
  20.4 0.1 stack.23.place
  20.5 0.0 collective-permute-done.1
  20.5 0.0 copy-done.2
  20.5 15.7 %all_gather.9.k = bf16[2048,128]{1,0:T(8,128)(2,1)S(1)} all-gather(bf16[128,128]{1,0:T(8,128)(2,1)S(1)} %slice_select_fusion), channel_id=1, replica_groups=mesh['grp'=2,'dp'=32,'x'=8,'core'=2] {'x','core'}, dimensions={0}, use_global_device_ids=true | all-gather | bytes 557056 | tf_op jit(solution)/shard_map/all_gather | solution.py:249
  36.3 0.0 collective-permute-done.other
  36.3 0.0 copy-done
  36.3 2.9 %shard_map.94 = bf16[2048,128]{1,0:T(8,128)(2,1)} custom-call(s32[5]{0:T(128)S(1)} %stack.23.place, bf16[128,1792]{1,0:T(8,128)(2,1)S(1)} %bitcast.21, bf16[128,1792]{1,0:T(8,128)(2,1)S(1)} %bitcast.24, bf16[128,1792]{1,0:T(8,128)(2,1)S(1)} %collective-permute-done.other, bf16[2048,128]{1,0:T(8,128)(2,1)S(1)} %all_gather.9.k), custom_call_target="tpu_custom_call" | custom-call | flops 6000000000 | tf_op jit(solution)/shard_map/pallas_call | solution.py:212
  39.2 0.0 collective-permute-done.2.across
  39.2 0.0 copy-start.5
  39.2 6.6 %all-to-all-start = ((bf16[16,128,128]{2,1,0:T(8,128)(2,1)}), bf16[16,128,128]{2,1,0:T(8,128)(2,1)S(1)}, u32[]{:S(2)}, u32[]{:S(2)}) async-start(bf16[16,128,128]{2,1,0:T(8,128)(2,1)} %bitcast.10), calls=%async_computation | async-start | bytes 1048576 | tf_op jit(solution)/shard_map/all_to_all | solution.py:275
  45.8 2.3 %collective-permute-start.4 = (bf16[128,1792]{1,0:T(8,128)(2,1)S(1)}, bf16[128,1792]{1,0:T(8,128)(2,1)S(1)}, u32[]{:S(2)}, u32[]{:S(2)}) collective-permute-start(bf16[128,1792]{1,0:T(8,128)(2,1)S(1)} %get-tuple-element.16.mine), channel_id=1, source_target_pairs={{0,1},{1,0},{2,3},{3,2},{4,5},{5,4},{6,7},{7,6},{8,9},{9,8},{10,11... | collective-permute-start | bytes 1376264 | tf_op jit(solution)/shard_map/ppermute | solution.py:272
  48.2 2.0 %collective-permute-start.5 = (bf16[128,1792]{1,0:T(8,128)(2,1)S(1)}, bf16[128,1792]{1,0:T(8,128)(2,1)S(1)}, u32[]{:S(2)}, u32[]{:S(2)}) collective-permute-start(bf16[128,1792]{1,0:T(8,128)(2,1)S(1)} %collective-permute-done.2.across), channel_id=1, source_target_pairs={{0,1},{1,0},{2,3},{3,2},{4,5},{5,4},{6,7},{7,6},{8,9},{9,8},{10,11... | collective-permute-start | bytes 1376264 | tf_op jit(solution)/shard_map/ppermute | solution.py:273
  50.2 0.0 copy-done.5
  50.2 1.6 %shard_map.95 = (bf16[128,128]{1,0:T(8,128)(2,1)S(1)}, bf16[128,128]{1,0:T(8,128)(2,1)S(1)}) custom-call(s32[5]{0:T(128)S(1)} %stack.23.place, s32[1,128]{1,0:T(1,128)S(1)} %copy-done.5, bf16[128,1792]{1,0:T(8,128)(2,1)S(1)} %bitcast.22, bf16[128,1792]{1,0:T(8,128)(2,1)S(1)} %bitcast.25, bf16[128,256]{1,0:T(8,128)(2,1)S(1)} %bitcast.28), custom_call_target="tpu_custom_call" | custom-call | flops 3000000000 | tf_op jit(solution)/shard_map/pallas_call | solution.py:212
  51.8 2.3 %collective-permute-start.3 = (bf16[128,128]{1,0:T(8,128)(2,1)S(1)}, bf16[128,128]{1,0:T(8,128)(2,1)S(1)}, u32[]{:S(2)}, u32[]{:S(2)}) collective-permute-start(bf16[128,128]{1,0:T(8,128)(2,1)S(1)} %get-tuple-element.15), channel_id=1, source_target_pairs={{0,1},{1,0},{2,3},{3,2},{4,5},{5,4},{6,7},{7,6},{8,9},{9,8},{10,11... | collective-permute-start | bytes 98312 | tf_op jit(solution)/shard_map/ppermute | solution.py:274
  54.1 0.8 collective-permute-done.3.got
  54.9 7.0 %all-to-all-done.pieces = bf16[16,128,128]{2,1,0:T(8,128)(2,1)S(1)} async-done(((bf16[16,128,128]{2,1,0:T(8,128)(2,1)}), bf16[16,128,128]{2,1,0:T(8,128)(2,1)S(1)}, u32[]{:S(2)}, u32[]{:S(2)}) %all-to-all-start) | async-done | bytes 524320 | tf_op jit(solution)/shard_map/all_to_all | solution.py:275
  61.9 0.1 shard_map.96
  61.9 5.6 %all-gather = bf16[256,384]{1,0:T(8,128)(2,1)S(1)} all-gather(bf16[128,384]{1,0:T(8,128)(2,1)S(1)} %shard_map.96), channel_id=2, replica_groups=mesh['grp'=2,'dp'=32,'x'=8,'core'=2] {'grp'}, dimensions={0}, use_global_device_ids=true | all-gather | bytes 294912 | tf_op jit(solution)/shard_map/all_gather | solution.py:279
  67.6 0.0 collective-permute-done.4.beside
  67.6 0.0 collective-permute-done.5.corner
  67.6 1.0 shard_map.97
  68.7 19.4 %all_to_all.15.pieces = bf16[8,16,1792]{2,1,0:T(8,128)(2,1)S(1)} all-to-all(bf16[8,16,1792]{2,1,0:T(8,128)(2,1)S(1)} %shard_map.97), channel_id=1, replica_groups=mesh['grp'=2,'dp'=32,'x'=8,'core'=2] {'x'}, dimensions={0} | all-to-all | bytes 917504 | tf_op jit(solution)/shard_map/all_to_all | solution.py:287
  88.1 0.0 copy-start.3
  88.1 0.0 copy-start.4
  88.1 0.2 shard_map.98
  88.3 26.9 %all_to_all.16.pieces = f32[32,8,128]{2,1,0:T(8,128)S(1)} all-to-all(f32[32,8,128]{2,1,0:T(8,128)S(1)} %shard_map.98), channel_id=1, replica_groups=mesh['grp'=2,'dp'=32,'x'=8,'core'=2] {'dp'}, dimensions={0} | all-to-all | bytes 262144 | tf_op jit(solution)/shard_map/all_to_all | solution.py:295
  115.1 0.0 copy-done.3
  115.1 0.0 copy-done.4
  115.1 0.7 shard_map.99
  (3 shorter events, 0.1 us)
Async XLA Ops:
  0.6 2.5 %copy-start.1 = (bf16[1,128,1792]{2,1,0:T(8,128)(2,1)S(1)}, bf16[1,128,1792]{2,1,0:T(8,128)(2,1)}, u32[]{:S(2)}) copy-start(bf16[1,128,1792]{2,1,0:T(8,128)(2,1)} %param.10) | copy-start | bytes 1376260
  0.6 19.9 %collective-permute-start.1 = (bf16[128,256]{1,0:T(8,128)(2,1)}, bf16[128,256]{1,0:T(8,128)(2,1)S(1)}, u32[]{:S(2)}, u32[]{:S(2)}) collective-permute-start(bf16[128,256]{1,0:T(8,128)(2,1)} %bitcast.26), channel_id=1, source_target_pairs={{0,512},{1,513},{2,514},{3,515},{4,516},{5,517},{6,518},{7,519},{8... | collective-permute-start | bytes 196616 | tf_op jit(solution)/shard_map/ppermute | solution.py:242
  2.1 2.4 %copy-start.6 = (bf16[1,128,3584]{2,1,0:T(8,128)(2,1)S(1)}, bf16[1,128,3584]{2,1,0:T(8,128)(2,1)}, u32[]{:S(2)}) copy-start(bf16[1,128,3584]{2,1,0:T(8,128)(2,1)} %param.7) | copy-start | bytes 2752516
  3.2 33.1 %collective-permute-start = (bf16[128,1792]{1,0:T(8,128)(2,1)S(1)}, bf16[128,1792]{1,0:T(8,128)(2,1)S(1)}, u32[]{:S(2)}, u32[]{:S(2)}) collective-permute-start(bf16[128,1792]{1,0:T(8,128)(2,1)S(1)} %pad_maximum_fusion), channel_id=1, source_target_pairs={{0,512},{1,513},{2,514},{3,515},{4,516},{5,517},{6,518},{7,519},{8... | collective-permute-start | bytes 1376264 | tf_op jit(solution)/shard_map/ppermute | solution.py:243
  4.5 16.0 %copy-start.2 = (bf16[1,128,256]{2,1,0:T(8,128)(2,1)S(1)}, bf16[1,128,256]{2,1,0:T(8,128)(2,1)}, u32[]{:S(2)}) copy-start(bf16[1,128,256]{2,1,0:T(8,128)(2,1)} %param.9) | copy-start | bytes 196612
  5.4 30.9 %copy-start = (bf16[1,128,1792]{2,1,0:T(8,128)(2,1)S(1)}, bf16[1,128,1792]{2,1,0:T(8,128)(2,1)}, u32[]{:S(2)}) copy-start(bf16[1,128,1792]{2,1,0:T(8,128)(2,1)} %param.8) | copy-start | bytes 1376260
  5.4 33.8 %collective-permute-start.2 = (bf16[128,1792]{1,0:T(8,128)(2,1)}, bf16[128,1792]{1,0:T(8,128)(2,1)S(1)}, u32[]{:S(2)}, u32[]{:S(2)}) collective-permute-start(bf16[128,1792]{1,0:T(8,128)(2,1)} %get-tuple-element.22), channel_id=1, source_target_pairs={{0,512},{512,0},{1,513},{513,1},{2,514},{514,2},{3,515},{515,3},{4... | collective-permute-start | bytes 1376264 | tf_op jit(solution)/shard_map/ppermute | solution.py:247
  39.2 11.0 %copy-start.5 = (s32[1,128]{1,0:T(1,128)S(1)}, s32[1,128]{1,0:T(1,128)}, u32[]{:S(2)}) copy-start(s32[1,128]{1,0:T(1,128)} %begin) | copy-start | bytes 1540
  39.2 22.7 %all-to-all-start = ((bf16[16,128,128]{2,1,0:T(8,128)(2,1)}), bf16[16,128,128]{2,1,0:T(8,128)(2,1)S(1)}, u32[]{:S(2)}, u32[]{:S(2)}) async-start(bf16[16,128,128]{2,1,0:T(8,128)(2,1)} %bitcast.10), calls=%async_computation | async-start | bytes 1048576 | tf_op jit(solution)/shard_map/all_to_all | solution.py:275
  45.8 21.8 %collective-permute-start.4 = (bf16[128,1792]{1,0:T(8,128)(2,1)S(1)}, bf16[128,1792]{1,0:T(8,128)(2,1)S(1)}, u32[]{:S(2)}, u32[]{:S(2)}) collective-permute-start(bf16[128,1792]{1,0:T(8,128)(2,1)S(1)} %get-tuple-element.16.mine), channel_id=1, source_target_pairs={{0,1},{1,0},{2,3},{3,2},{4,5},{5,4},{6,7},{7,6},{8,9},{9,8},{10,11... | collective-permute-start | bytes 1376264 | tf_op jit(solution)/shard_map/ppermute | solution.py:272
  48.2 19.4 %collective-permute-start.5 = (bf16[128,1792]{1,0:T(8,128)(2,1)S(1)}, bf16[128,1792]{1,0:T(8,128)(2,1)S(1)}, u32[]{:S(2)}, u32[]{:S(2)}) collective-permute-start(bf16[128,1792]{1,0:T(8,128)(2,1)S(1)} %collective-permute-done.2.across), channel_id=1, source_target_pairs={{0,1},{1,0},{2,3},{3,2},{4,5},{5,4},{6,7},{7,6},{8,9},{9,8},{10,11... | collective-permute-start | bytes 1376264 | tf_op jit(solution)/shard_map/ppermute | solution.py:273
  51.8 3.2 %collective-permute-start.3 = (bf16[128,128]{1,0:T(8,128)(2,1)S(1)}, bf16[128,128]{1,0:T(8,128)(2,1)S(1)}, u32[]{:S(2)}, u32[]{:S(2)}) collective-permute-start(bf16[128,128]{1,0:T(8,128)(2,1)S(1)} %get-tuple-element.15), channel_id=1, source_target_pairs={{0,1},{1,0},{2,3},{3,2},{4,5},{5,4},{6,7},{7,6},{8,9},{9,8},{10,11... | collective-permute-start | bytes 98312 | tf_op jit(solution)/shard_map/ppermute | solution.py:274
  88.1 27.0 %copy-start.3 = (f32[56,16]{0,1:T(8,128)S(1)}, f32[56,16]{0,1:T(8,128)}, u32[]{:S(2)}) copy-start(f32[56,16]{0,1:T(8,128)} %param.12) | copy-start | bytes 10756
  88.1 27.0 %copy-start.4 = (f32[56,16]{0,1:T(8,128)S(1)}, f32[56,16]{0,1:T(8,128)}, u32[]{:S(2)}) copy-start(f32[56,16]{0,1:T(8,128)} %param.13) | copy-start | bytes 10756

commit v6 on v5

--- a/solution.py
+++ b/solution.py
@@ -14,7 +14,6 @@
 STEP = 10
 GROUP = 7
 CHUNK = 512
-TILE = 256
 masked_score = -1e30
 GAIN = HD ** (-0.5) * math.log2(math.e)
 WHOLE = pl.BlockSpec(memory_space=pltpu.VMEM)
@@ -156,7 +155,7 @@
 
 
 def project_kernel(place, values, mine, across, beside, corner, out, turned, vg):
-    share = out.shape[1]
+    share = out.shape[2]
     rows = values.shape[1]
     group, core = place[0], place[4]
     half = HD // 2
@@ -172,13 +171,16 @@
         c = core if j // 2 == 0 else 1 - core
         block = turned[jnp.where(g == 0, c, 2 + j // 2)]
         vg[:, j * rows : (j + 1) * rows] = block.astype(vg.dtype)
-    for t in range(mine.shape[1] // TILE):
-        part = slice(t * TILE, (t + 1) * TILE)
+    chips, stripes, _, span = out.shape
+    for t in range(0, stripes, 2):
+        part = slice(t * span, (t + 2) * span)
         x = jnp.concatenate(
             [mine[:, part], across[:, part], beside[:, part], corner[:, part]], axis=0
         )
         block = product(vg[...], x, 0)
-        out[:, :, part] = block.astype(out.dtype).reshape(out.shape[0], share, TILE)
+        for n in range(2):
+            piece = block[:, n * span : (n + 1) * span].astype(out.dtype)
+            out[:, t + n] = piece.reshape(chips, share, span)
 
 
 def fold_kernel(owners, pieces, out, total):
@@ -223,7 +225,7 @@
 def body(layer_input, queries, keys, d_out, doc_start, moment_m, moment_v):
     rows = queries.shape[1]
     chips, cores = lax.axis_size("x"), lax.axis_size("core")
-    owners = lax.axis_size("dp")
+    stripes, owners = lax.axis_size("yh"), lax.axis_size("z")
     blocks = chips * cores
     seq = blocks * rows
     width, cols = layer_input.shape[2], KV_HEADS * HD
@@ -279,22 +281,23 @@
     values = lax.all_gather(values, "grp", axis=0)
     gradient = call(
         project_kernel,
-        shape((chips, share, half), bf16),
+        shape((chips, stripes, share, half // stripes), bf16),
         [place],
         [values, mine, across, beside, corner],
         [pltpu.VMEM((4, cols // 2, rows), f32), pltpu.VMEM((cols // 2, 4 * rows), bf16)],
     )
-    terms = lax.all_to_all(gradient, "x", 0, 0, tiled=True)
+    gradient = gradient.reshape(chips * stripes, share, half // stripes)
+    terms = lax.all_to_all(gradient, ("x", "yh"), 0, 0, tiled=True)
     sent = call(
         functools.partial(fold_kernel, owners),
         shape((owners, 8, 128), f32),
         [],
         [terms],
-        [pltpu.VMEM((share, half), f32)],
-    )
-    landed = lax.all_to_all(sent, "dp", 0, 0, tiled=True)
+        [pltpu.VMEM((share, half // stripes), f32)],
+    )
+    landed = lax.all_to_all(sent, "z", 0, 0, tiled=True)
     result = shape(moment_m.shape[::-1], f32)
-    total_tokens = 2 * owners * seq
+    total_tokens = 2 * stripes * owners * seq
     outs = call(
         functools.partial(adam_kernel, 1.0 / math.sqrt(total_tokens)),
         (result,) * 3,
@@ -305,9 +308,10 @@
 
 
 def solution(mesh):
-    split = mesh.devices.reshape(*mesh.devices.shape[:2], -1, 2)
-    mesh = Mesh(split, ("grp", "dp", "x", "core"))
-    slots, tokens = ("grp", "dp"), ("x", "core")
+    groups, copies, blocks = mesh.devices.shape
+    split = mesh.devices.reshape(groups, 4, copies // 4, blocks // 2, 2)
+    mesh = Mesh(split, ("grp", "yh", "z", "x", "core"))
+    slots, tokens = ("grp", "yh", "z"), ("x", "core")
     wide, flat = P(slots, tokens, None), P(slots, tokens)
     in_specs = (wide, wide, wide, wide, flat, flat, flat)
     return jax.shard_map(

time: 116 us -> 116 us (level)
  the two profiles are of different devices: /device:TPU:16 before, /device:TPU:2 now
where the time goes in v6:
time: 116 us; the launch traced here: 115 us
  blocking collectives  79.1 us (68%)
  starting transfers between devices  20.2 us (17%)
  waiting for transfers between devices  7.4 us (6%)
  Pallas kernels  5.54 us (5%)
  local copies, waits for them, and re-layouts  1.18 us (1%)
    all_gather x1, blocking collectives, body(): all_keys = lax.all_gather(chosen, ('x', 'core'), axis=0, tiled=True)  26.4 us
    all_to_all x1, blocking collectives, body(): terms = lax.all_to_all(gradient, ('x', 'yh'), 0, 0, tiled=True)  25 us
    all_to_all x1, blocking collectives, body(): landed = lax.all_to_all(sent, 'z', 0, 0, tiled=True)  21.9 us
    all_to_all x1, starting transfers between devices, body(): lax.all_to_all(partial.reshape(blocks, rows, HD), ('x', 'core'), 0, 0, ti...  6.74 us
    all_to_all x1, waiting for transfers between devices, body(): lax.all_to_all(partial.reshape(blocks, rows, HD), ('x', 'core'), 0, 0, ti...  6.35 us
    all_gather x1, blocking collectives, body(): values = lax.all_gather(values, 'grp', axis=0)  5.74 us
    pallas_call x6, Pallas kernels, call(): pl.pallas_call(kernel, out_shape=out, in_specs=[SCALARS] * len(scalars) +...  5.54 us
    ppermute x1, starting transfers between devices, body(): other_k = lax.ppermute(k, 'grp', down)  3.73 us
  transfers between devices with their start and end apart: 7, of which 2 were waited for; matrix products, arithmetic and copies ran while one was open for 2% of the time, Pallas kernels for 3%

profile of v6, /device:TPU:2, one launch (start us, length us, event | category | flops | bytes accessed | tf_op | source)
XLA Modules:
  0.0 115.1 jit_solution(9625464589505599331)
XLA Ops:
  0.6 0.0 copy-start.1
  0.6 3.7 %collective-permute-start.1 = (bf16[128,256]{1,0:T(8,128)(2,1)}, bf16[128,256]{1,0:T(8,128)(2,1)S(1)}, u32[]{:S(2)}, u32[]{:S(2)}) collective-permute-start(bf16[128,256]{1,0:T(8,128)(2,1)} %bitcast.28), channel_id=1, source_target_pairs={{0,512},{1,513},{2,514},{3,515},{4,516},{5,517},{6,518},{7,519},{8... | collective-permute-start | bytes 196616 | tf_op jit(solution)/shard_map/ppermute | solution.py:244
  4.4 0.0 copy-start.6
  4.4 1.0 slice.24
  5.4 0.0 copy-done.1
  5.5 1.3 %collective-permute-start = (bf16[128,1792]{1,0:T(8,128)(2,1)S(1)}, bf16[128,1792]{1,0:T(8,128)(2,1)S(1)}, u32[]{:S(2)}, u32[]{:S(2)}) collective-permute-start(bf16[128,1792]{1,0:T(8,128)(2,1)S(1)} %pad_maximum_fusion), channel_id=1, source_target_pairs={{0,512},{1,513},{2,514},{3,515},{4,516},{5,517},{6,518},{7,519},{8... | collective-permute-start | bytes 1376264 | tf_op jit(solution)/shard_map/ppermute | solution.py:245
  6.8 0.0 copy-done.6
  6.9 0.0 copy-start.2
  6.9 0.8 select_bitcast_fusion
  7.7 0.0 copy-start
  7.7 2.0 %collective-permute-start.2 = (bf16[128,1792]{1,0:T(8,128)(2,1)}, bf16[128,1792]{1,0:T(8,128)(2,1)S(1)}, u32[]{:S(2)}, u32[]{:S(2)}) collective-permute-start(bf16[128,1792]{1,0:T(8,128)(2,1)} %get-tuple-element.22), channel_id=1, source_target_pairs={{0,512},{512,0},{1,513},{513,1},{2,514},{514,2},{3,515},{515,3},{4... | collective-permute-start | bytes 1376264 | tf_op jit(solution)/shard_map/ppermute | solution.py:249
  9.8 0.1 stack.23.place
  9.9 0.0 collective-permute-done.1
  9.9 0.0 copy-done.2
  9.9 26.4 %all_gather.9.k = bf16[2048,128]{1,0:T(8,128)(2,1)S(1)} all-gather(bf16[128,128]{1,0:T(8,128)(2,1)S(1)} %slice_select_fusion), channel_id=1, replica_groups=mesh['grp'=2,'yh'=4,'z'=8,'x'=8,'core'=2] {'x','core'}, dimensions={0}, use_global_device_ids=true | all-gather | bytes 557056 | tf_op jit(solution)/shard_map/all_gather | solution.py:251
  36.3 0.0 collective-permute-done.other
  36.3 0.0 copy-done
  36.3 2.9 %shard_map.94 = bf16[2048,128]{1,0:T(8,128)(2,1)} custom-call(s32[5]{0:T(128)S(1)} %stack.23.place, bf16[128,1792]{1,0:T(8,128)(2,1)S(1)} %bitcast.23, bf16[128,1792]{1,0:T(8,128)(2,1)S(1)} %bitcast.26, bf16[128,1792]{1,0:T(8,128)(2,1)S(1)} %collective-permute-done.other, bf16[2048,128]{1,0:T(8,128)(2,1)S(1)} %all_gather.9.k), custom_call_target="tpu_custom_call" | custom-call | flops 6000000000 | tf_op jit(solution)/shard_map/pallas_call | solution.py:214
  39.2 0.0 collective-permute-done.2.across
  39.2 0.0 copy-start.5
  39.2 6.7 %all-to-all-start = ((bf16[16,128,128]{2,1,0:T(8,128)(2,1)}), bf16[16,128,128]{2,1,0:T(8,128)(2,1)S(1)}, u32[]{:S(2)}, u32[]{:S(2)}) async-start(bf16[16,128,128]{2,1,0:T(8,128)(2,1)} %bitcast.10), calls=%async_computation | async-start | bytes 1048576 | tf_op jit(solution)/shard_map/all_to_all | solution.py:277
  46.0 2.0 %collective-permute-start.4 = (bf16[128,1792]{1,0:T(8,128)(2,1)S(1)}, bf16[128,1792]{1,0:T(8,128)(2,1)S(1)}, u32[]{:S(2)}, u32[]{:S(2)}) collective-permute-start(bf16[128,1792]{1,0:T(8,128)(2,1)S(1)} %get-tuple-element.16.mine), channel_id=1, source_target_pairs={{0,1},{1,0},{2,3},{3,2},{4,5},{5,4},{6,7},{7,6},{8,9},{9,8},{10,11... | collective-permute-start | bytes 1376264 | tf_op jit(solution)/shard_map/ppermute | solution.py:274
  48.0 2.3 %collective-permute-start.5 = (bf16[128,1792]{1,0:T(8,128)(2,1)S(1)}, bf16[128,1792]{1,0:T(8,128)(2,1)S(1)}, u32[]{:S(2)}, u32[]{:S(2)}) collective-permute-start(bf16[128,1792]{1,0:T(8,128)(2,1)S(1)} %collective-permute-done.2.across), channel_id=1, source_target_pairs={{0,1},{1,0},{2,3},{3,2},{4,5},{5,4},{6,7},{7,6},{8,9},{9,8},{10,11... | collective-permute-start | bytes 1376264 | tf_op jit(solution)/shard_map/ppermute | solution.py:275
  50.3 0.0 copy-done.5
  50.3 0.6 shard_map.95
  50.9 2.1 %collective-permute-start.3 = (bf16[128,128]{1,0:T(8,128)(2,1)S(1)}, bf16[128,128]{1,0:T(8,128)(2,1)S(1)}, u32[]{:S(2)}, u32[]{:S(2)}) collective-permute-start(bf16[128,128]{1,0:T(8,128)(2,1)S(1)} %get-tuple-element.15), channel_id=1, source_target_pairs={{0,1},{1,0},{2,3},{3,2},{4,5},{5,4},{6,7},{7,6},{8,9},{9,8},{10,11... | collective-permute-start | bytes 98312 | tf_op jit(solution)/shard_map/ppermute | solution.py:276
  52.9 1.0 collective-permute-done.3.got
  54.0 6.3 %all-to-all-done.pieces = bf16[16,128,128]{2,1,0:T(8,128)(2,1)S(1)} async-done(((bf16[16,128,128]{2,1,0:T(8,128)(2,1)}), bf16[16,128,128]{2,1,0:T(8,128)(2,1)S(1)}, u32[]{:S(2)}, u32[]{:S(2)}) %all-to-all-start) | async-done | bytes 524320 | tf_op jit(solution)/shard_map/all_to_all | solution.py:277
  60.3 0.1 shard_map.96
  60.4 5.7 %all-gather = bf16[256,384]{1,0:T(8,128)(2,1)S(1)} all-gather(bf16[128,384]{1,0:T(8,128)(2,1)S(1)} %shard_map.96), channel_id=2, replica_groups=mesh['grp'=2,'yh'=4,'z'=8,'x'=8,'core'=2] {'grp'}, dimensions={0}, use_global_device_ids=true | all-gather | bytes 294912 | tf_op jit(solution)/shard_map/all_gather | solution.py:281
  66.1 0.0 collective-permute-done.4.beside
  66.1 0.0 collective-permute-done.5.corner
  66.1 1.1 shard_map.97
  67.3 25.0 %all_to_all.15.pieces = bf16[32,16,448]{2,1,0:T(8,128)(2,1)S(1)} all-to-all(bf16[32,16,448]{2,1,0:T(8,128)(2,1)S(1)} %bitcast.20), channel_id=1, replica_groups=mesh['grp'=2,'yh'=4,'z'=8,'x'=8,'core'=2] {'x','yh'}, dimensions={0} | all-to-all | bytes 917504 | tf_op jit(solution)/shard_map/all_to_all | solution.py:290
  92.3 0.0 copy-start.3
  92.3 0.0 copy-start.4
  92.3 0.2 shard_map.98
  92.5 21.9 %all_to_all.16.pieces = f32[8,8,128]{2,1,0:T(8,128)S(1)} all-to-all(f32[8,8,128]{2,1,0:T(8,128)S(1)} %shard_map.98), channel_id=1, replica_groups=mesh['grp'=2,'yh'=4,'z'=8,'x'=8,'core'=2] {'z'}, dimensions={0} | all-to-all | bytes 65536 | tf_op jit(solution)/shard_map/all_to_all | solution.py:298
  114.4 0.0 copy-done.3
  114.4 0.0 copy-done.4
  114.4 0.7 shard_map.99
  (3 shorter events, 0.1 us)
Async XLA Ops:
  0.6 4.8 %copy-start.1 = (bf16[1,128,1792]{2,1,0:T(8,128)(2,1)S(1)}, bf16[1,128,1792]{2,1,0:T(8,128)(2,1)}, u32[]{:S(2)}) copy-start(bf16[1,128,1792]{2,1,0:T(8,128)(2,1)} %param.10) | copy-start | bytes 1376260
  0.6 9.2 %collective-permute-start.1 = (bf16[128,256]{1,0:T(8,128)(2,1)}, bf16[128,256]{1,0:T(8,128)(2,1)S(1)}, u32[]{:S(2)}, u32[]{:S(2)}) collective-permute-start(bf16[128,256]{1,0:T(8,128)(2,1)} %bitcast.28), channel_id=1, source_target_pairs={{0,512},{1,513},{2,514},{3,515},{4,516},{5,517},{6,518},{7,519},{8... | collective-permute-start | bytes 196616 | tf_op jit(solution)/shard_map/ppermute | solution.py:244
  4.4 2.5 %copy-start.6 = (bf16[1,128,3584]{2,1,0:T(8,128)(2,1)S(1)}, bf16[1,128,3584]{2,1,0:T(8,128)(2,1)}, u32[]{:S(2)}) copy-start(bf16[1,128,3584]{2,1,0:T(8,128)(2,1)} %param.7) | copy-start | bytes 2752516
  5.5 30.8 %collective-permute-start = (bf16[128,1792]{1,0:T(8,128)(2,1)S(1)}, bf16[128,1792]{1,0:T(8,128)(2,1)S(1)}, u32[]{:S(2)}, u32[]{:S(2)}) collective-permute-start(bf16[128,1792]{1,0:T(8,128)(2,1)S(1)} %pad_maximum_fusion), channel_id=1, source_target_pairs={{0,512},{1,513},{2,514},{3,515},{4,516},{5,517},{6,518},{7,519},{8... | collective-permute-start | bytes 1376264 | tf_op jit(solution)/shard_map/ppermute | solution.py:245
  6.9 3.0 %copy-start.2 = (bf16[1,128,256]{2,1,0:T(8,128)(2,1)S(1)}, bf16[1,128,256]{2,1,0:T(8,128)(2,1)}, u32[]{:S(2)}) copy-start(bf16[1,128,256]{2,1,0:T(8,128)(2,1)} %param.9) | copy-start | bytes 196612
  7.7 28.6 %copy-start = (bf16[1,128,1792]{2,1,0:T(8,128)(2,1)S(1)}, bf16[1,128,1792]{2,1,0:T(8,128)(2,1)}, u32[]{:S(2)}) copy-start(bf16[1,128,1792]{2,1,0:T(8,128)(2,1)} %param.8) | copy-start | bytes 1376260
  7.7 31.5 %collective-permute-start.2 = (bf16[128,1792]{1,0:T(8,128)(2,1)}, bf16[128,1792]{1,0:T(8,128)(2,1)S(1)}, u32[]{:S(2)}, u32[]{:S(2)}) collective-permute-start(bf16[128,1792]{1,0:T(8,128)(2,1)} %get-tuple-element.22), channel_id=1, source_target_pairs={{0,512},{512,0},{1,513},{513,1},{2,514},{514,2},{3,515},{515,3},{4... | collective-permute-start | bytes 1376264 | tf_op jit(solution)/shard_map/ppermute | solution.py:249
  39.2 11.1 %copy-start.5 = (s32[1,128]{1,0:T(1,128)S(1)}, s32[1,128]{1,0:T(1,128)}, u32[]{:S(2)}) copy-start(s32[1,128]{1,0:T(1,128)} %begin) | copy-start | bytes 1540
  39.2 21.1 %all-to-all-start = ((bf16[16,128,128]{2,1,0:T(8,128)(2,1)}), bf16[16,128,128]{2,1,0:T(8,128)(2,1)S(1)}, u32[]{:S(2)}, u32[]{:S(2)}) async-start(bf16[16,128,128]{2,1,0:T(8,128)(2,1)} %bitcast.10), calls=%async_computation | async-start | bytes 1048576 | tf_op jit(solution)/shard_map/all_to_all | solution.py:277
  46.0 20.2 %collective-permute-start.4 = (bf16[128,1792]{1,0:T(8,128)(2,1)S(1)}, bf16[128,1792]{1,0:T(8,128)(2,1)S(1)}, u32[]{:S(2)}, u32[]{:S(2)}) collective-permute-start(bf16[128,1792]{1,0:T(8,128)(2,1)S(1)} %get-tuple-element.16.mine), channel_id=1, source_target_pairs={{0,1},{1,0},{2,3},{3,2},{4,5},{5,4},{6,7},{7,6},{8,9},{9,8},{10,11... | collective-permute-start | bytes 1376264 | tf_op jit(solution)/shard_map/ppermute | solution.py:274
  48.0 18.1 %collective-permute-start.5 = (bf16[128,1792]{1,0:T(8,128)(2,1)S(1)}, bf16[128,1792]{1,0:T(8,128)(2,1)S(1)}, u32[]{:S(2)}, u32[]{:S(2)}) collective-permute-start(bf16[128,1792]{1,0:T(8,128)(2,1)S(1)} %collective-permute-done.2.across), channel_id=1, source_target_pairs={{0,1},{1,0},{2,3},{3,2},{4,5},{5,4},{6,7},{7,6},{8,9},{9,8},{10,11... | collective-permute-start | bytes 1376264 | tf_op jit(solution)/shard_map/ppermute | solution.py:275
  50.9 3.1 %collective-permute-start.3 = (bf16[128,128]{1,0:T(8,128)(2,1)S(1)}, bf16[128,128]{1,0:T(8,128)(2,1)S(1)}, u32[]{:S(2)}, u32[]{:S(2)}) collective-permute-start(bf16[128,128]{1,0:T(8,128)(2,1)S(1)} %get-tuple-element.15), channel_id=1, source_target_pairs={{0,1},{1,0},{2,3},{3,2},{4,5},{5,4},{6,7},{7,6},{8,9},{9,8},{10,11... | collective-permute-start | bytes 98312 | tf_op jit(solution)/shard_map/ppermute | solution.py:276
  92.3 22.1 %copy-start.3 = (f32[56,16]{0,1:T(8,128)S(1)}, f32[56,16]{0,1:T(8,128)}, u32[]{:S(2)}) copy-start(f32[56,16]{0,1:T(8,128)} %param.12) | copy-start | bytes 10756
  92.3 22.1 %copy-start.4 = (f32[56,16]{0,1:T(8,128)S(1)}, f32[56,16]{0,1:T(8,128)}, u32[]{:S(2)}) copy-start(f32[56,16]{0,1:T(8,128)} %param.13) | copy-start | bytes 10756

commit v7 on v6

--- a/solution.py
+++ b/solution.py
@@ -155,7 +155,6 @@
 
 
 def project_kernel(place, values, mine, across, beside, corner, out, turned, vg):
-    share = out.shape[2]
     rows = values.shape[1]
     group, core = place[0], place[4]
     half = HD // 2
@@ -171,7 +170,8 @@
         c = core if j // 2 == 0 else 1 - core
         block = turned[jnp.where(g == 0, c, 2 + j // 2)]
         vg[:, j * rows : (j + 1) * rows] = block.astype(vg.dtype)
-    chips, stripes, _, span = out.shape
+    chips, stripes, depth, span = out.shape
+    span = span // 2
     for t in range(0, stripes, 2):
         part = slice(t * span, (t + 2) * span)
         x = jnp.concatenate(
@@ -179,8 +179,9 @@
         )
         block = product(vg[...], x, 0)
         for n in range(2):
-            piece = block[:, n * span : (n + 1) * span].astype(out.dtype)
-            out[:, t + n] = piece.reshape(chips, share, span)
+            piece = block[:, n * span : (n + 1) * span].reshape(chips, 2, depth, span)
+            piece = jnp.concatenate([piece[:, 0], piece[:, 1]], axis=-1)
+            out[:, t + n] = piece.astype(out.dtype)
 
 
 def fold_kernel(owners, pieces, out, total):
@@ -188,12 +189,12 @@
     for i in range(1, pieces.shape[0]):
         acc = acc + pieces[i].astype(jnp.float32)
     total[...] = acc
-    span = total.shape[1] // owners
+    half = total.shape[1] // 2
+    span = half // owners
     out[...] = jnp.zeros(out.shape, out.dtype)
     for r in range(owners):
-        block = total[:, r * span : (r + 1) * span]
-        out[r, :, :span] = block[:8]
-        out[r, :, 64 : 64 + span] = block[8:]
+        out[r, :, :span] = total[:, r * span : (r + 1) * span]
+        out[r, :, 64 : 64 + span] = total[:, half + r * span : half + (r + 1) * span]
 
 
 def adam_kernel(scale, pieces, m, v, new_m, new_v, update):
@@ -281,19 +282,19 @@
     values = lax.all_gather(values, "grp", axis=0)
     gradient = call(
         project_kernel,
-        shape((chips, stripes, share, half // stripes), bf16),
+        shape((chips, stripes, share // 2, 2 * half // stripes), bf16),
         [place],
         [values, mine, across, beside, corner],
         [pltpu.VMEM((4, cols // 2, rows), f32), pltpu.VMEM((cols // 2, 4 * rows), bf16)],
     )
-    gradient = gradient.reshape(chips * stripes, share, half // stripes)
+    gradient = gradient.reshape(chips * stripes, share // 2, 2 * half // stripes)
     terms = lax.all_to_all(gradient, ("x", "yh"), 0, 0, tiled=True)
     sent = call(
         functools.partial(fold_kernel, owners),
         shape((owners, 8, 128), f32),
         [],
         [terms],
-        [pltpu.VMEM((share, half // stripes), f32)],
+        [pltpu.VMEM((share // 2, 2 * half // stripes), f32)],
     )
     landed = lax.all_to_all(sent, "z", 0, 0, tiled=True)
     result = shape(moment_m.shape[::-1], f32)

time: 116 us -> 114 us (0.983)
  no operation moved by 1% of the time
where the time goes in v7:
time: 114 us
  blocking collectives  78 us (68%)
  starting transfers between devices  20.2 us (18%)
  waiting for transfers between devices  7.4 us (6%)
  Pallas kernels  5.52 us (5%)
  local copies, waits for them, and re-layouts  1.18 us (1%)
    all_gather x1, blocking collectives, body(): all_keys = lax.all_gather(chosen, ('x', 'core'), axis=0, tiled=True)  26.4 us
    all_to_all x1, blocking collectives, body(): terms = lax.all_to_all(gradient, ('x', 'yh'), 0, 0, tiled=True)  23.9 us
    all_to_all x1, blocking collectives, body(): landed = lax.all_to_all(sent, 'z', 0, 0, tiled=True)  21.9 us
    all_to_all x1, starting transfers between devices, body(): lax.all_to_all(partial.reshape(blocks, rows, HD), ('x', 'core'), 0, 0, ti...  6.74 us
    all_to_all x1, waiting for transfers between devices, body(): lax.all_to_all(partial.reshape(blocks, rows, HD), ('x', 'core'), 0, 0, ti...  6.35 us
    all_gather x1, blocking collectives, body(): values = lax.all_gather(values, 'grp', axis=0)  5.74 us
    pallas_call x6, Pallas kernels, call(): pl.pallas_call(kernel, out_shape=out, in_specs=[SCALARS] * len(scalars) +...  5.52 us
    ppermute x1, starting transfers between devices, body(): other_k = lax.ppermute(k, 'grp', down)  3.73 us
  transfers between devices with their start and end apart: 7, of which 2 were waited for; matrix products, arithmetic and copies ran while one was open for 2% of the time, Pallas kernels for 3%

profile of v7, /device:TPU:2, one launch (start us, length us, event | category | flops | bytes accessed | tf_op | source)
XLA Modules:
  0.0 114.0 jit_solution(2499198247926055715)
XLA Ops:
  0.6 0.0 copy-start.1
  0.6 3.7 %collective-permute-start.1 = (bf16[128,256]{1,0:T(8,128)(2,1)}, bf16[128,256]{1,0:T(8,128)(2,1)S(1)}, u32[]{:S(2)}, u32[]{:S(2)}) collective-permute-start(bf16[128,256]{1,0:T(8,128)(2,1)} %bitcast.28), channel_id=1, source_target_pairs={{0,512},{1,513},{2,514},{3,515},{4,516},{5,517},{6,518},{7,519},{8... | collective-permute-start | bytes 196616 | tf_op jit(solution)/shard_map/ppermute | solution.py:245
  4.4 0.0 copy-start.6
  4.4 1.0 slice.24
  5.4 0.0 copy-done.1
  5.5 1.3 %collective-permute-start = (bf16[128,1792]{1,0:T(8,128)(2,1)S(1)}, bf16[128,1792]{1,0:T(8,128)(2,1)S(1)}, u32[]{:S(2)}, u32[]{:S(2)}) collective-permute-start(bf16[128,1792]{1,0:T(8,128)(2,1)S(1)} %pad_maximum_fusion), channel_id=1, source_target_pairs={{0,512},{1,513},{2,514},{3,515},{4,516},{5,517},{6,518},{7,519},{8... | collective-permute-start | bytes 1376264 | tf_op jit(solution)/shard_map/ppermute | solution.py:246
  6.8 0.0 copy-done.6
  6.9 0.0 copy-start.2
  6.9 0.8 select_bitcast_fusion
  7.7 0.0 copy-start
  7.7 2.0 %collective-permute-start.2 = (bf16[128,1792]{1,0:T(8,128)(2,1)}, bf16[128,1792]{1,0:T(8,128)(2,1)S(1)}, u32[]{:S(2)}, u32[]{:S(2)}) collective-permute-start(bf16[128,1792]{1,0:T(8,128)(2,1)} %get-tuple-element.22), channel_id=1, source_target_pairs={{0,512},{512,0},{1,513},{513,1},{2,514},{514,2},{3,515},{515,3},{4... | collective-permute-start | bytes 1376264 | tf_op jit(solution)/shard_map/ppermute | solution.py:250
  9.8 0.1 stack.23.place
  9.9 0.0 collective-permute-done.1
  9.9 0.0 copy-done.2
  9.9 26.4 %all_gather.9.k = bf16[2048,128]{1,0:T(8,128)(2,1)S(1)} all-gather(bf16[128,128]{1,0:T(8,128)(2,1)S(1)} %slice_select_fusion), channel_id=1, replica_groups=mesh['grp'=2,'yh'=4,'z'=8,'x'=8,'core'=2] {'x','core'}, dimensions={0}, use_global_device_ids=true | all-gather | bytes 557056 | tf_op jit(solution)/shard_map/all_gather | solution.py:252
  36.3 0.0 collective-permute-done.other
  36.3 0.0 copy-done
  36.3 2.9 %shard_map.94 = bf16[2048,128]{1,0:T(8,128)(2,1)} custom-call(s32[5]{0:T(128)S(1)} %stack.23.place, bf16[128,1792]{1,0:T(8,128)(2,1)S(1)} %bitcast.23, bf16[128,1792]{1,0:T(8,128)(2,1)S(1)} %bitcast.26, bf16[128,1792]{1,0:T(8,128)(2,1)S(1)} %collective-permute-done.other, bf16[2048,128]{1,0:T(8,128)(2,1)S(1)} %all_gather.9.k), custom_call_target="tpu_custom_call" | custom-call | flops 6000000000 | tf_op jit(solution)/shard_map/pallas_call | solution.py:215
  39.2 0.0 collective-permute-done.2.across
  39.2 0.0 copy-start.5
  39.2 6.7 %all-to-all-start = ((bf16[16,128,128]{2,1,0:T(8,128)(2,1)}), bf16[16,128,128]{2,1,0:T(8,128)(2,1)S(1)}, u32[]{:S(2)}, u32[]{:S(2)}) async-start(bf16[16,128,128]{2,1,0:T(8,128)(2,1)} %bitcast.10), calls=%async_computation | async-start | bytes 1048576 | tf_op jit(solution)/shard_map/all_to_all | solution.py:278
  46.0 2.0 %collective-permute-start.4 = (bf16[128,1792]{1,0:T(8,128)(2,1)S(1)}, bf16[128,1792]{1,0:T(8,128)(2,1)S(1)}, u32[]{:S(2)}, u32[]{:S(2)}) collective-permute-start(bf16[128,1792]{1,0:T(8,128)(2,1)S(1)} %get-tuple-element.16.mine), channel_id=1, source_target_pairs={{0,1},{1,0},{2,3},{3,2},{4,5},{5,4},{6,7},{7,6},{8,9},{9,8},{10,11... | collective-permute-start | bytes 1376264 | tf_op jit(solution)/shard_map/ppermute | solution.py:275
  48.0 2.3 %collective-permute-start.5 = (bf16[128,1792]{1,0:T(8,128)(2,1)S(1)}, bf16[128,1792]{1,0:T(8,128)(2,1)S(1)}, u32[]{:S(2)}, u32[]{:S(2)}) collective-permute-start(bf16[128,1792]{1,0:T(8,128)(2,1)S(1)} %collective-permute-done.2.across), channel_id=1, source_target_pairs={{0,1},{1,0},{2,3},{3,2},{4,5},{5,4},{6,7},{7,6},{8,9},{9,8},{10,11... | collective-permute-start | bytes 1376264 | tf_op jit(solution)/shard_map/ppermute | solution.py:276
  50.3 0.0 copy-done.5
  50.3 0.6 shard_map.95
  50.9 2.1 %collective-permute-start.3 = (bf16[128,128]{1,0:T(8,128)(2,1)S(1)}, bf16[128,128]{1,0:T(8,128)(2,1)S(1)}, u32[]{:S(2)}, u32[]{:S(2)}) collective-permute-start(bf16[128,128]{1,0:T(8,128)(2,1)S(1)} %get-tuple-element.15), channel_id=1, source_target_pairs={{0,1},{1,0},{2,3},{3,2},{4,5},{5,4},{6,7},{7,6},{8,9},{9,8},{10,11... | collective-permute-start | bytes 98312 | tf_op jit(solution)/shard_map/ppermute | solution.py:277
  52.9 1.0 collective-permute-done.3.got
  54.0 6.3 %all-to-all-done.pieces = bf16[16,128,128]{2,1,0:T(8,128)(2,1)S(1)} async-done(((bf16[16,128,128]{2,1,0:T(8,128)(2,1)}), bf16[16,128,128]{2,1,0:T(8,128)(2,1)S(1)}, u32[]{:S(2)}, u32[]{:S(2)}) %all-to-all-start) | async-done | bytes 524320 | tf_op jit(solution)/shard_map/all_to_all | solution.py:278
  60.3 0.1 shard_map.96
  60.4 5.7 %all-gather = bf16[256,384]{1,0:T(8,128)(2,1)S(1)} all-gather(bf16[128,384]{1,0:T(8,128)(2,1)S(1)} %shard_map.96), channel_id=2, replica_groups=mesh['grp'=2,'yh'=4,'z'=8,'x'=8,'core'=2] {'grp'}, dimensions={0}, use_global_device_ids=true | all-gather | bytes 294912 | tf_op jit(solution)/shard_map/all_gather | solution.py:282
  66.1 0.0 collective-permute-done.4.beside
  66.1 0.0 collective-permute-done.5.corner
  66.1 1.1 %shard_map.97 = bf16[8,4,8,896]{3,2,1,0:T(8,128)(2,1)S(1)} custom-call(s32[5]{0:T(128)S(1)} %stack.23.place, bf16[2,128,384]{2,1,0:T(8,128)(2,1)S(1)} %bitcast.21, bf16[128,1792]{1,0:T(8,128)(2,1)S(1)} %get-tuple-element.16.mine, bf16[128,1792]{1,0:T(8,128)(2,1)S(1)} %collective-permute-done.2.across, bf16[128,1792]{1,0:T(8,128)(2,1)S(1)} %collective-permute-done.4.beside, ...), custom_call_target="tpu_custom_call" | custom-call | tf_op jit(solution)/shard_map/pallas_call | solution.py:215
  67.3 23.9 %all_to_all.15.pieces = bf16[32,8,896]{2,1,0:T(8,128)(2,1)S(1)} all-to-all(bf16[32,8,896]{2,1,0:T(8,128)(2,1)S(1)} %bitcast.20), channel_id=1, replica_groups=mesh['grp'=2,'yh'=4,'z'=8,'x'=8,'core'=2] {'x','yh'}, dimensions={0} | all-to-all | bytes 917504 | tf_op jit(solution)/shard_map/all_to_all | solution.py:291
  91.2 0.0 copy-start.3
  91.2 0.0 copy-start.4
  91.2 0.1 shard_map.98
  91.3 21.9 %all_to_all.16.pieces = f32[8,8,128]{2,1,0:T(8,128)S(1)} all-to-all(f32[8,8,128]{2,1,0:T(8,128)S(1)} %shard_map.98), channel_id=1, replica_groups=mesh['grp'=2,'yh'=4,'z'=8,'x'=8,'core'=2] {'z'}, dimensions={0} | all-to-all | bytes 65536 | tf_op jit(solution)/shard_map/all_to_all | solution.py:299
  113.2 0.0 copy-done.3
  113.3 0.0 copy-done.4
  113.3 0.7 shard_map.99
  (3 shorter events, 0.1 us)
Async XLA Ops:
  0.6 4.8 %copy-start.1 = (bf16[1,128,1792]{2,1,0:T(8,128)(2,1)S(1)}, bf16[1,128,1792]{2,1,0:T(8,128)(2,1)}, u32[]{:S(2)}) copy-start(bf16[1,128,1792]{2,1,0:T(8,128)(2,1)} %param.10) | copy-start | bytes 1376260
  0.6 9.2 %collective-permute-start.1 = (bf16[128,256]{1,0:T(8,128)(2,1)}, bf16[128,256]{1,0:T(8,128)(2,1)S(1)}, u32[]{:S(2)}, u32[]{:S(2)}) collective-permute-start(bf16[128,256]{1,0:T(8,128)(2,1)} %bitcast.28), channel_id=1, source_target_pairs={{0,512},{1,513},{2,514},{3,515},{4,516},{5,517},{6,518},{7,519},{8... | collective-permute-start | bytes 196616 | tf_op jit(solution)/shard_map/ppermute | solution.py:245
  4.4 2.5 %copy-start.6 = (bf16[1,128,3584]{2,1,0:T(8,128)(2,1)S(1)}, bf16[1,128,3584]{2,1,0:T(8,128)(2,1)}, u32[]{:S(2)}) copy-start(bf16[1,128,3584]{2,1,0:T(8,128)(2,1)} %param.7) | copy-start | bytes 2752516
  5.5 30.8 %collective-permute-start = (bf16[128,1792]{1,0:T(8,128)(2,1)S(1)}, bf16[128,1792]{1,0:T(8,128)(2,1)S(1)}, u32[]{:S(2)}, u32[]{:S(2)}) collective-permute-start(bf16[128,1792]{1,0:T(8,128)(2,1)S(1)} %pad_maximum_fusion), channel_id=1, source_target_pairs={{0,512},{1,513},{2,514},{3,515},{4,516},{5,517},{6,518},{7,519},{8... | collective-permute-start | bytes 1376264 | tf_op jit(solution)/shard_map/ppermute | solution.py:246
  6.9 3.0 %copy-start.2 = (bf16[1,128,256]{2,1,0:T(8,128)(2,1)S(1)}, bf16[1,128,256]{2,1,0:T(8,128)(2,1)}, u32[]{:S(2)}) copy-start(bf16[1,128,256]{2,1,0:T(8,128)(2,1)} %param.9) | copy-start | bytes 196612
  7.7 28.6 %copy-start = (bf16[1,128,1792]{2,1,0:T(8,128)(2,1)S(1)}, bf16[1,128,1792]{2,1,0:T(8,128)(2,1)}, u32[]{:S(2)}) copy-start(bf16[1,128,1792]{2,1,0:T(8,128)(2,1)} %param.8) | copy-start | bytes 1376260
  7.7 31.5 %collective-permute-start.2 = (bf16[128,1792]{1,0:T(8,128)(2,1)}, bf16[128,1792]{1,0:T(8,128)(2,1)S(1)}, u32[]{:S(2)}, u32[]{:S(2)}) collective-permute-start(bf16[128,1792]{1,0:T(8,128)(2,1)} %get-tuple-element.22), channel_id=1, source_target_pairs={{0,512},{512,0},{1,513},{513,1},{2,514},{514,2},{3,515},{515,3},{4... | collective-permute-start | bytes 1376264 | tf_op jit(solution)/shard_map/ppermute | solution.py:250
  39.2 11.1 %copy-start.5 = (s32[1,128]{1,0:T(1,128)S(1)}, s32[1,128]{1,0:T(1,128)}, u32[]{:S(2)}) copy-start(s32[1,128]{1,0:T(1,128)} %begin) | copy-start | bytes 1540
  39.2 21.1 %all-to-all-start = ((bf16[16,128,128]{2,1,0:T(8,128)(2,1)}), bf16[16,128,128]{2,1,0:T(8,128)(2,1)S(1)}, u32[]{:S(2)}, u32[]{:S(2)}) async-start(bf16[16,128,128]{2,1,0:T(8,128)(2,1)} %bitcast.10), calls=%async_computation | async-start | bytes 1048576 | tf_op jit(solution)/shard_map/all_to_all | solution.py:278
  46.0 20.2 %collective-permute-start.4 = (bf16[128,1792]{1,0:T(8,128)(2,1)S(1)}, bf16[128,1792]{1,0:T(8,128)(2,1)S(1)}, u32[]{:S(2)}, u32[]{:S(2)}) collective-permute-start(bf16[128,1792]{1,0:T(8,128)(2,1)S(1)} %get-tuple-element.16.mine), channel_id=1, source_target_pairs={{0,1},{1,0},{2,3},{3,2},{4,5},{5,4},{6,7},{7,6},{8,9},{9,8},{10,11... | collective-permute-start | bytes 1376264 | tf_op jit(solution)/shard_map/ppermute | solution.py:275
  48.0 18.1 %collective-permute-start.5 = (bf16[128,1792]{1,0:T(8,128)(2,1)S(1)}, bf16[128,1792]{1,0:T(8,128)(2,1)S(1)}, u32[]{:S(2)}, u32[]{:S(2)}) collective-permute-start(bf16[128,1792]{1,0:T(8,128)(2,1)S(1)} %collective-permute-done.2.across), channel_id=1, source_target_pairs={{0,1},{1,0},{2,3},{3,2},{4,5},{5,4},{6,7},{7,6},{8,9},{9,8},{10,11... | collective-permute-start | bytes 1376264 | tf_op jit(solution)/shard_map/ppermute | solution.py:276
  50.9 3.1 %collective-permute-start.3 = (bf16[128,128]{1,0:T(8,128)(2,1)S(1)}, bf16[128,128]{1,0:T(8,128)(2,1)S(1)}, u32[]{:S(2)}, u32[]{:S(2)}) collective-permute-start(bf16[128,128]{1,0:T(8,128)(2,1)S(1)} %get-tuple-element.15), channel_id=1, source_target_pairs={{0,1},{1,0},{2,3},{3,2},{4,5},{5,4},{6,7},{7,6},{8,9},{9,8},{10,11... | collective-permute-start | bytes 98312 | tf_op jit(solution)/shard_map/ppermute | solution.py:277
  91.2 22.1 %copy-start.3 = (f32[56,16]{0,1:T(8,128)S(1)}, f32[56,16]{0,1:T(8,128)}, u32[]{:S(2)}) copy-start(f32[56,16]{0,1:T(8,128)} %param.12) | copy-start | bytes 10756
  91.2 22.1 %copy-start.4 = (f32[56,16]{0,1:T(8,128)S(1)}, f32[56,16]{0,1:T(8,128)}, u32[]{:S(2)}) copy-start(f32[56,16]{0,1:T(8,128)} %param.13) | copy-start | bytes 10756

commit v8 on v7

--- a/solution.py
+++ b/solution.py
@@ -145,16 +145,16 @@
     lax.fori_loop(0, high + 1, collect, 0)
 
 
-def value_kernel(pieces, stay, got, out):
+def value_kernel(pieces, out):
     total = pieces[0].astype(jnp.float32)
     for i in range(1, pieces.shape[0]):
         total = total + pieces[i].astype(jnp.float32)
-    out[:, :HD] = total.astype(out.dtype)
-    out[:, HD : 2 * HD] = stay[...]
-    out[:, 2 * HD :] = got[...]
-
-
-def project_kernel(place, values, mine, across, beside, corner, out, turned, vg):
+    out[...] = total.astype(out.dtype)
+
+
+def project_kernel(
+    place, values, stay, got, near, far, mine, across, beside, corner, out, turned, vg
+):
     rows = values.shape[1]
     group, core = place[0], place[4]
     half = HD // 2
@@ -162,8 +162,8 @@
         part = jnp.transpose(values[g, :, :HD].astype(jnp.float32))
         for c in range(2):
             turned[c, g * half : (g + 1) * half, :] = part[c * half : (c + 1) * half]
-    for n in range(2):
-        part = values[1, :, (1 + n) * HD : (2 + n) * HD].astype(jnp.float32)
+    for n, (here, sent) in enumerate(((stay, near), (got, far))):
+        part = jnp.where(group == 1, here[...].astype(jnp.float32), sent[...].astype(jnp.float32))
         turned[2 + n] = jnp.transpose(part)
     for j in range(4):
         g = group if j % 2 == 0 else 1 - group
@@ -275,16 +275,18 @@
     beside = lax.ppermute(mine, "core", swap)
     corner = lax.ppermute(across, "core", swap)
     got = lax.ppermute(leave, "core", swap)
+    near = lax.ppermute(stay, "grp", [(1, 0)])
+    far = lax.ppermute(leave, ("grp", "core"), [(2, 1), (3, 0)])
     pieces = lax.all_to_all(
         partial.reshape(blocks, rows, HD), ("x", "core"), 0, 0, tiled=True
     )
-    values = call(value_kernel, shape((rows, 3 * HD), bf16), [], [pieces, stay, got])
+    values = call(value_kernel, square, [], [pieces])
     values = lax.all_gather(values, "grp", axis=0)
     gradient = call(
         project_kernel,
         shape((chips, stripes, share // 2, 2 * half // stripes), bf16),
         [place],
-        [values, mine, across, beside, corner],
+        [values, stay, got, near, far, mine, across, beside, corner],
         [pltpu.VMEM((4, cols // 2, rows), f32), pltpu.VMEM((cols // 2, 4 * rows), bf16)],
     )
     gradient = gradient.reshape(chips * stripes, share // 2, 2 * half // stripes)

time: 114 us -> 113 us (level)
  starting transfers between devices: 20.2 us -> 22.8 us
  waiting for transfers between devices: 7.4 us -> 4.8 us
  blocking collectives: 78 us -> 76.4 us
    ppermute x0 -> x2, starting transfers between devices: none -> 2.58 us  [the longest x1 1.29 us: body(): near = lax.ppermute(stay, 'grp', [(1, 0)])]
    all_to_all x1, waiting for transfers between devices: 6.35 us -> 4.78 us  [body(): lax.all_to_all(partial.reshape(blocks, rows, HD), ('x', 'core'), 0, 0, ti...]
    all_gather x1, blocking collectives: 5.74 us -> 4.59 us  [body(): values = lax.all_gather(values, 'grp', axis=0)]
  transfers between devices with their start and end apart: 7 -> 9, of which waited for: 2 -> 1; matrix products, arithmetic and copies ran while one was open for 2% -> 2% of each run, Pallas kernels for 3% -> 3%
where the time goes in v8:
time: 113 us; the launch traced here: 112 us
  blocking collectives  76.4 us (68%)
  starting transfers between devices  22.8 us (20%)
  Pallas kernels  5.53 us (5%)
  waiting for transfers between devices  4.8 us (4%)
  local copies, waits for them, and re-layouts  1.18 us (1%)
    all_gather x1, blocking collectives, body(): all_keys = lax.all_gather(chosen, ('x', 'core'), axis=0, tiled=True)  26.4 us
    all_to_all x1, blocking collectives, body(): terms = lax.all_to_all(gradient, ('x', 'yh'), 0, 0, tiled=True)  24 us
    all_to_all x1, blocking collectives, body(): landed = lax.all_to_all(sent, 'z', 0, 0, tiled=True)  21.4 us
    all_to_all x1, starting transfers between devices, body(): lax.all_to_all(partial.reshape(blocks, rows, HD), ('x', 'core'), 0, 0, ti...  6.74 us
    pallas_call x6, Pallas kernels, call(): pl.pallas_call(kernel, out_shape=out, in_specs=[SCALARS] * len(scalars) +...  5.53 us
    all_to_all x1, waiting for transfers between devices, body(): lax.all_to_all(partial.reshape(blocks, rows, HD), ('x', 'core'), 0, 0, ti...  4.78 us
    all_gather x1, blocking collectives, body(): values = lax.all_gather(values, 'grp', axis=0)  4.59 us
    ppermute x1, starting transfers between devices, body(): other_k = lax.ppermute(k, 'grp', down)  3.73 us
  transfers between devices with their start and end apart: 9, of which 1 were waited for; matrix products, arithmetic and copies ran while one was open for 2% of the time, Pallas kernels for 3%

profile of v8, /device:TPU:2, one launch (start us, length us, event | category | flops | bytes accessed | tf_op | source)
XLA Modules:
  0.0 112.4 jit_solution(8446942074384238694)
XLA Ops:
  0.6 0.0 copy-start.1
  0.6 3.7 %collective-permute-start.1 = (bf16[128,256]{1,0:T(8,128)(2,1)}, bf16[128,256]{1,0:T(8,128)(2,1)S(1)}, u32[]{:S(2)}, u32[]{:S(2)}) collective-permute-start(bf16[128,256]{1,0:T(8,128)(2,1)} %bitcast.28), channel_id=1, source_target_pairs={{0,512},{1,513},{2,514},{3,515},{4,516},{5,517},{6,518},{7,519},{8... | collective-permute-start | bytes 196616 | tf_op jit(solution)/shard_map/ppermute | solution.py:245
  4.4 0.0 copy-start.6
  4.4 1.0 slice.24
  5.4 0.0 copy-done.1
  5.5 1.3 %collective-permute-start = (bf16[128,1792]{1,0:T(8,128)(2,1)S(1)}, bf16[128,1792]{1,0:T(8,128)(2,1)S(1)}, u32[]{:S(2)}, u32[]{:S(2)}) collective-permute-start(bf16[128,1792]{1,0:T(8,128)(2,1)S(1)} %pad_maximum_fusion), channel_id=1, source_target_pairs={{0,512},{1,513},{2,514},{3,515},{4,516},{5,517},{6,518},{7,519},{8... | collective-permute-start | bytes 1376264 | tf_op jit(solution)/shard_map/ppermute | solution.py:246
  6.8 0.0 copy-done.6
  6.9 0.0 copy-start.2
  6.9 0.8 select_bitcast_fusion
  7.7 0.0 copy-start
  7.7 2.0 %collective-permute-start.2 = (bf16[128,1792]{1,0:T(8,128)(2,1)}, bf16[128,1792]{1,0:T(8,128)(2,1)S(1)}, u32[]{:S(2)}, u32[]{:S(2)}) collective-permute-start(bf16[128,1792]{1,0:T(8,128)(2,1)} %get-tuple-element.22), channel_id=1, source_target_pairs={{0,512},{512,0},{1,513},{513,1},{2,514},{514,2},{3,515},{515,3},{4... | collective-permute-start | bytes 1376264 | tf_op jit(solution)/shard_map/ppermute | solution.py:250
  9.8 0.1 stack.23.place
  9.9 0.0 collective-permute-done.1
  9.9 0.0 copy-done.2
  9.9 26.4 %all_gather.9.k = bf16[2048,128]{1,0:T(8,128)(2,1)S(1)} all-gather(bf16[128,128]{1,0:T(8,128)(2,1)S(1)} %slice_select_fusion), channel_id=1, replica_groups=mesh['grp'=2,'yh'=4,'z'=8,'x'=8,'core'=2] {'x','core'}, dimensions={0}, use_global_device_ids=true | all-gather | bytes 557056 | tf_op jit(solution)/shard_map/all_gather | solution.py:252
  36.3 0.0 collective-permute-done.other
  36.3 0.0 copy-done
  36.3 2.9 %shard_map.94 = bf16[2048,128]{1,0:T(8,128)(2,1)} custom-call(s32[5]{0:T(128)S(1)} %stack.23.place, bf16[128,1792]{1,0:T(8,128)(2,1)S(1)} %bitcast.23, bf16[128,1792]{1,0:T(8,128)(2,1)S(1)} %bitcast.26, bf16[128,1792]{1,0:T(8,128)(2,1)S(1)} %collective-permute-done.other, bf16[2048,128]{1,0:T(8,128)(2,1)S(1)} %all_gather.9.k), custom_call_target="tpu_custom_call" | custom-call | flops 6000000000 | tf_op jit(solution)/shard_map/pallas_call | solution.py:215
  39.2 0.0 collective-permute-done.2.across
  39.2 0.0 copy-start.5
  39.2 6.7 %all-to-all-start = ((bf16[16,128,128]{2,1,0:T(8,128)(2,1)}), bf16[16,128,128]{2,1,0:T(8,128)(2,1)S(1)}, u32[]{:S(2)}, u32[]{:S(2)}) async-start(bf16[16,128,128]{2,1,0:T(8,128)(2,1)} %bitcast.10), calls=%async_computation | async-start | bytes 1048576 | tf_op jit(solution)/shard_map/all_to_all | solution.py:280
  46.0 2.0 %collective-permute-start.6 = (bf16[128,1792]{1,0:T(8,128)(2,1)S(1)}, bf16[128,1792]{1,0:T(8,128)(2,1)S(1)}, u32[]{:S(2)}, u32[]{:S(2)}) collective-permute-start(bf16[128,1792]{1,0:T(8,128)(2,1)S(1)} %get-tuple-element.16.mine), channel_id=1, source_target_pairs={{0,1},{1,0},{2,3},{3,2},{4,5},{5,4},{6,7},{7,6},{8,9},{9,8},{10,11... | collective-permute-start | bytes 1376264 | tf_op jit(solution)/shard_map/ppermute | solution.py:275
  48.0 2.3 %collective-permute-start.7 = (bf16[128,1792]{1,0:T(8,128)(2,1)S(1)}, bf16[128,1792]{1,0:T(8,128)(2,1)S(1)}, u32[]{:S(2)}, u32[]{:S(2)}) collective-permute-start(bf16[128,1792]{1,0:T(8,128)(2,1)S(1)} %collective-permute-done.2.across), channel_id=1, source_target_pairs={{0,1},{1,0},{2,3},{3,2},{4,5},{5,4},{6,7},{7,6},{8,9},{9,8},{10,11... | collective-permute-start | bytes 1376264 | tf_op jit(solution)/shard_map/ppermute | solution.py:276
  50.3 0.0 copy-done.5
  50.3 0.6 shard_map.96
  50.9 1.3 %collective-permute-start.4 = (bf16[128,128]{1,0:T(8,128)(2,1)S(1)}, bf16[128,128]{1,0:T(8,128)(2,1)S(1)}, u32[]{:S(2)}, u32[]{:S(2)}) collective-permute-start(bf16[128,128]{1,0:T(8,128)(2,1)S(1)} %get-tuple-element.14.stay), channel_id=1, source_target_pairs={{512,0},{513,1},{514,2},{515,3},{516,4},{517,5},{518,6},{519,7},{5... | collective-permute-start | bytes 98312 | tf_op jit(solution)/shard_map/ppermute | solution.py:278
  52.2 1.3 %collective-permute-start.5 = (bf16[128,128]{1,0:T(8,128)(2,1)S(1)}, bf16[128,128]{1,0:T(8,128)(2,1)S(1)}, u32[]{:S(2)}, u32[]{:S(2)}) collective-permute-start(bf16[128,128]{1,0:T(8,128)(2,1)S(1)} %get-tuple-element.15), channel_id=1, source_target_pairs={{512,1},{513,0},{514,3},{515,2},{516,5},{517,4},{518,7},{519,6},{5... | collective-permute-start | bytes 98312 | tf_op jit(solution)/shard_map/ppermute | solution.py:279
  53.5 2.1 %collective-permute-start.3 = (bf16[128,128]{1,0:T(8,128)(2,1)S(1)}, bf16[128,128]{1,0:T(8,128)(2,1)S(1)}, u32[]{:S(2)}, u32[]{:S(2)}) collective-permute-start(bf16[128,128]{1,0:T(8,128)(2,1)S(1)} %get-tuple-element.15), channel_id=1, source_target_pairs={{0,1},{1,0},{2,3},{3,2},{4,5},{5,4},{6,7},{7,6},{8,9},{9,8},{10,11... | collective-permute-start | bytes 98312 | tf_op jit(solution)/shard_map/ppermute | solution.py:277
  55.6 4.8 %all-to-all-done.pieces = bf16[16,128,128]{2,1,0:T(8,128)(2,1)S(1)} async-done(((bf16[16,128,128]{2,1,0:T(8,128)(2,1)}), bf16[16,128,128]{2,1,0:T(8,128)(2,1)S(1)}, u32[]{:S(2)}, u32[]{:S(2)}) %all-to-all-start) | async-done | bytes 524320 | tf_op jit(solution)/shard_map/all_to_all | solution.py:280
  60.3 0.1 shard_map.95
  60.4 4.6 %all-gather = bf16[256,128]{1,0:T(8,128)(2,1)S(1)} all-gather(bf16[128,128]{1,0:T(8,128)(2,1)S(1)} %shard_map.95), channel_id=2, replica_groups=mesh['grp'=2,'yh'=4,'z'=8,'x'=8,'core'=2] {'grp'}, dimensions={0}, use_global_device_ids=true | all-gather | bytes 98304 | tf_op jit(solution)/shard_map/all_gather | solution.py:284
  65.0 0.0 collective-permute-done.4.near
  65.0 0.0 collective-permute-done.5.far
  65.0 0.0 collective-permute-done.3.got
  65.0 0.0 collective-permute-done.6.beside
  65.0 0.0 collective-permute-done.7.corner
  65.0 1.2 %shard_map.97 = bf16[8,4,8,896]{3,2,1,0:T(8,128)(2,1)S(1)} custom-call(s32[5]{0:T(128)S(1)} %stack.23.place, bf16[2,128,128]{2,1,0:T(8,128)(2,1)S(1)} %bitcast.21, bf16[128,128]{1,0:T(8,128)(2,1)S(1)} %get-tuple-element.14.stay, bf16[128,128]{1,0:T(8,128)(2,1)S(1)} %collective-permute-done.3.got, bf16[128,128]{1,0:T(8,128)(2,1)S(1)} %collective-permute-done.4.near, ...), custom_call_target="tpu_custom_call" | custom-call | tf_op jit(solution)/shard_map/pallas_call | solution.py:215
  66.2 24.0 %all_to_all.15.pieces = bf16[32,8,896]{2,1,0:T(8,128)(2,1)S(1)} all-to-all(bf16[32,8,896]{2,1,0:T(8,128)(2,1)S(1)} %bitcast.20), channel_id=1, replica_groups=mesh['grp'=2,'yh'=4,'z'=8,'x'=8,'core'=2] {'x','yh'}, dimensions={0} | all-to-all | bytes 917504 | tf_op jit(solution)/shard_map/all_to_all | solution.py:293
  90.2 0.0 copy-start.3
  90.2 0.0 copy-start.4
  90.2 0.1 shard_map.98
  90.3 21.4 %all_to_all.16.pieces = f32[8,8,128]{2,1,0:T(8,128)S(1)} all-to-all(f32[8,8,128]{2,1,0:T(8,128)S(1)} %shard_map.98), channel_id=1, replica_groups=mesh['grp'=2,'yh'=4,'z'=8,'x'=8,'core'=2] {'z'}, dimensions={0} | all-to-all | bytes 65536 | tf_op jit(solution)/shard_map/all_to_all | solution.py:301
  111.7 0.0 copy-done.3
  111.7 0.0 copy-done.4
  111.7 0.7 shard_map.99
  (3 shorter events, 0.1 us)
Async XLA Ops:
  0.6 4.8 %copy-start.1 = (bf16[1,128,1792]{2,1,0:T(8,128)(2,1)S(1)}, bf16[1,128,1792]{2,1,0:T(8,128)(2,1)}, u32[]{:S(2)}) copy-start(bf16[1,128,1792]{2,1,0:T(8,128)(2,1)} %param.10) | copy-start | bytes 1376260
  0.6 9.2 %collective-permute-start.1 = (bf16[128,256]{1,0:T(8,128)(2,1)}, bf16[128,256]{1,0:T(8,128)(2,1)S(1)}, u32[]{:S(2)}, u32[]{:S(2)}) collective-permute-start(bf16[128,256]{1,0:T(8,128)(2,1)} %bitcast.28), channel_id=1, source_target_pairs={{0,512},{1,513},{2,514},{3,515},{4,516},{5,517},{6,518},{7,519},{8... | collective-permute-start | bytes 196616 | tf_op jit(solution)/shard_map/ppermute | solution.py:245
  4.4 2.5 %copy-start.6 = (bf16[1,128,3584]{2,1,0:T(8,128)(2,1)S(1)}, bf16[1,128,3584]{2,1,0:T(8,128)(2,1)}, u32[]{:S(2)}) copy-start(bf16[1,128,3584]{2,1,0:T(8,128)(2,1)} %param.7) | copy-start | bytes 2752516
  5.5 30.8 %collective-permute-start = (bf16[128,1792]{1,0:T(8,128)(2,1)S(1)}, bf16[128,1792]{1,0:T(8,128)(2,1)S(1)}, u32[]{:S(2)}, u32[]{:S(2)}) collective-permute-start(bf16[128,1792]{1,0:T(8,128)(2,1)S(1)} %pad_maximum_fusion), channel_id=1, source_target_pairs={{0,512},{1,513},{2,514},{3,515},{4,516},{5,517},{6,518},{7,519},{8... | collective-permute-start | bytes 1376264 | tf_op jit(solution)/shard_map/ppermute | solution.py:246
  6.9 3.0 %copy-start.2 = (bf16[1,128,256]{2,1,0:T(8,128)(2,1)S(1)}, bf16[1,128,256]{2,1,0:T(8,128)(2,1)}, u32[]{:S(2)}) copy-start(bf16[1,128,256]{2,1,0:T(8,128)(2,1)} %param.9) | copy-start | bytes 196612
  7.7 28.6 %copy-start = (bf16[1,128,1792]{2,1,0:T(8,128)(2,1)S(1)}, bf16[1,128,1792]{2,1,0:T(8,128)(2,1)}, u32[]{:S(2)}) copy-start(bf16[1,128,1792]{2,1,0:T(8,128)(2,1)} %param.8) | copy-start | bytes 1376260
  7.7 31.5 %collective-permute-start.2 = (bf16[128,1792]{1,0:T(8,128)(2,1)}, bf16[128,1792]{1,0:T(8,128)(2,1)S(1)}, u32[]{:S(2)}, u32[]{:S(2)}) collective-permute-start(bf16[128,1792]{1,0:T(8,128)(2,1)} %get-tuple-element.22), channel_id=1, source_target_pairs={{0,512},{512,0},{1,513},{513,1},{2,514},{514,2},{3,515},{515,3},{4... | collective-permute-start | bytes 1376264 | tf_op jit(solution)/shard_map/ppermute | solution.py:250
  39.2 11.1 %copy-start.5 = (s32[1,128]{1,0:T(1,128)S(1)}, s32[1,128]{1,0:T(1,128)}, u32[]{:S(2)}) copy-start(s32[1,128]{1,0:T(1,128)} %begin) | copy-start | bytes 1540
  39.2 21.1 %all-to-all-start = ((bf16[16,128,128]{2,1,0:T(8,128)(2,1)}), bf16[16,128,128]{2,1,0:T(8,128)(2,1)S(1)}, u32[]{:S(2)}, u32[]{:S(2)}) async-start(bf16[16,128,128]{2,1,0:T(8,128)(2,1)} %bitcast.10), calls=%async_computation | async-start | bytes 1048576 | tf_op jit(solution)/shard_map/all_to_all | solution.py:280
  46.0 19.0 %collective-permute-start.6 = (bf16[128,1792]{1,0:T(8,128)(2,1)S(1)}, bf16[128,1792]{1,0:T(8,128)(2,1)S(1)}, u32[]{:S(2)}, u32[]{:S(2)}) collective-permute-start(bf16[128,1792]{1,0:T(8,128)(2,1)S(1)} %get-tuple-element.16.mine), channel_id=1, source_target_pairs={{0,1},{1,0},{2,3},{3,2},{4,5},{5,4},{6,7},{7,6},{8,9},{9,8},{10,11... | collective-permute-start | bytes 1376264 | tf_op jit(solution)/shard_map/ppermute | solution.py:275
  48.0 17.0 %collective-permute-start.7 = (bf16[128,1792]{1,0:T(8,128)(2,1)S(1)}, bf16[128,1792]{1,0:T(8,128)(2,1)S(1)}, u32[]{:S(2)}, u32[]{:S(2)}) collective-permute-start(bf16[128,1792]{1,0:T(8,128)(2,1)S(1)} %collective-permute-done.2.across), channel_id=1, source_target_pairs={{0,1},{1,0},{2,3},{3,2},{4,5},{5,4},{6,7},{7,6},{8,9},{9,8},{10,11... | collective-permute-start | bytes 1376264 | tf_op jit(solution)/shard_map/ppermute | solution.py:276
  50.9 14.1 %collective-permute-start.4 = (bf16[128,128]{1,0:T(8,128)(2,1)S(1)}, bf16[128,128]{1,0:T(8,128)(2,1)S(1)}, u32[]{:S(2)}, u32[]{:S(2)}) collective-permute-start(bf16[128,128]{1,0:T(8,128)(2,1)S(1)} %get-tuple-element.14.stay), channel_id=1, source_target_pairs={{512,0},{513,1},{514,2},{515,3},{516,4},{517,5},{518,6},{519,7},{5... | collective-permute-start | bytes 98312 | tf_op jit(solution)/shard_map/ppermute | solution.py:278
  52.2 12.8 %collective-permute-start.5 = (bf16[128,128]{1,0:T(8,128)(2,1)S(1)}, bf16[128,128]{1,0:T(8,128)(2,1)S(1)}, u32[]{:S(2)}, u32[]{:S(2)}) collective-permute-start(bf16[128,128]{1,0:T(8,128)(2,1)S(1)} %get-tuple-element.15), channel_id=1, source_target_pairs={{512,1},{513,0},{514,3},{515,2},{516,5},{517,4},{518,7},{519,6},{5... | collective-permute-start | bytes 98312 | tf_op jit(solution)/shard_map/ppermute | solution.py:279
  53.5 11.5 %collective-permute-start.3 = (bf16[128,128]{1,0:T(8,128)(2,1)S(1)}, bf16[128,128]{1,0:T(8,128)(2,1)S(1)}, u32[]{:S(2)}, u32[]{:S(2)}) collective-permute-start(bf16[128,128]{1,0:T(8,128)(2,1)S(1)} %get-tuple-element.15), channel_id=1, source_target_pairs={{0,1},{1,0},{2,3},{3,2},{4,5},{5,4},{6,7},{7,6},{8,9},{9,8},{10,11... | collective-permute-start | bytes 98312 | tf_op jit(solution)/shard_map/ppermute | solution.py:277
  90.2 21.6 %copy-start.3 = (f32[56,16]{0,1:T(8,128)S(1)}, f32[56,16]{0,1:T(8,128)}, u32[]{:S(2)}) copy-start(f32[56,16]{0,1:T(8,128)} %param.12) | copy-start | bytes 10756
  90.2 21.6 %copy-start.4 = (f32[56,16]{0,1:T(8,128)S(1)}, f32[56,16]{0,1:T(8,128)}, u32[]{:S(2)}) copy-start(f32[56,16]{0,1:T(8,128)} %param.13) | copy-start | bytes 10756

commit v9 on v8

--- a/solution.py
+++ b/solution.py
@@ -103,8 +103,14 @@
     def chunk_rows(c):
         return pl.ds(pl.multiple_of(c * CHUNK, CHUNK), CHUNK)
 
+    def piece_rows(c, parity, n, count):
+        start = parity * (seq // 2) + c * (CHUNK // 2) + n * rows
+        return pl.ds(pl.multiple_of(start, rows), count * rows)
+
     def clear(c, carry):
-        out[chunk_rows(c), :] = jnp.zeros((CHUNK, HD), out.dtype)
+        for parity in range(2):
+            at = piece_rows(c, parity, 0, CHUNK // rows // 2)
+            out[at, :] = jnp.zeros((CHUNK // 2, HD), out.dtype)
         return carry
 
     lax.fori_loop(high + 1, seq // CHUNK, clear, 0)
@@ -138,7 +144,7 @@
         for i in range(0, CHUNK // rows, 2):
             pair = [block[(i + n) * rows : (i + n + 1) * rows] for n in range(2)]
             for parity in range(2):
-                at = pl.ds(pl.multiple_of(c * CHUNK + (i + parity) * rows, rows), rows)
+                at = piece_rows(c, parity, i // 2, 1)
                 out[at, :] = join(*pair, parity).astype(out.dtype)
         return carry
 
@@ -170,7 +176,7 @@
         c = core if j // 2 == 0 else 1 - core
         block = turned[jnp.where(g == 0, c, 2 + j // 2)]
         vg[:, j * rows : (j + 1) * rows] = block.astype(vg.dtype)
-    chips, stripes, depth, span = out.shape
+    stripes, chips, depth, span = out.shape
     span = span // 2
     for t in range(0, stripes, 2):
         part = slice(t * span, (t + 2) * span)
@@ -181,7 +187,7 @@
         for n in range(2):
             piece = block[:, n * span : (n + 1) * span].reshape(chips, 2, depth, span)
             piece = jnp.concatenate([piece[:, 0], piece[:, 1]], axis=-1)
-            out[:, t + n] = piece.astype(out.dtype)
+            out[t + n] = piece.astype(out.dtype)
 
 
 def fold_kernel(owners, pieces, out, total):
@@ -278,19 +284,19 @@
     near = lax.ppermute(stay, "grp", [(1, 0)])
     far = lax.ppermute(leave, ("grp", "core"), [(2, 1), (3, 0)])
     pieces = lax.all_to_all(
-        partial.reshape(blocks, rows, HD), ("x", "core"), 0, 0, tiled=True
+        partial.reshape(blocks, rows, HD), ("core", "x"), 0, 0, tiled=True
     )
     values = call(value_kernel, square, [], [pieces])
     values = lax.all_gather(values, "grp", axis=0)
     gradient = call(
         project_kernel,
-        shape((chips, stripes, share // 2, 2 * half // stripes), bf16),
+        shape((stripes, chips, share // 2, 2 * half // stripes), bf16),
         [place],
         [values, stay, got, near, far, mine, across, beside, corner],
         [pltpu.VMEM((4, cols // 2, rows), f32), pltpu.VMEM((cols // 2, 4 * rows), bf16)],
     )
     gradient = gradient.reshape(chips * stripes, share // 2, 2 * half // stripes)
-    terms = lax.all_to_all(gradient, ("x", "yh"), 0, 0, tiled=True)
+    terms = lax.all_to_all(gradient, ("yh", "x"), 0, 0, tiled=True)
     sent = call(
         functools.partial(fold_kernel, owners),
         shape((owners, 8, 128), f32),

time: 113 us -> 113 us (level)
  the two profiles are of different devices: /device:TPU:2 before, /device:TPU:18 now
where the time goes in v9:
time: 113 us
  blocking collectives  74.5 us (66%)
  starting transfers between devices  23.1 us (20%)
  Pallas kernels  6.52 us (6%)
  waiting for transfers between devices  5.84 us (5%)
  local copies, waits for them, and re-layouts  1.18 us (1%)
    all_gather x1, blocking collectives, body(): all_keys = lax.all_gather(chosen, ('x', 'core'), axis=0, tiled=True)  26.4 us
    all_to_all x1, blocking collectives, body(): landed = lax.all_to_all(sent, 'z', 0, 0, tiled=True)  21.9 us
    all_to_all x1, blocking collectives, body(): terms = lax.all_to_all(gradient, ('yh', 'x'), 0, 0, tiled=True)  21.5 us
    all_to_all x1, starting transfers between devices, body(): lax.all_to_all(partial.reshape(blocks, rows, HD), ('core', 'x'), 0, 0, ti...  6.72 us
    pallas_call x6, Pallas kernels, call(): pl.pallas_call(kernel, out_shape=out, in_specs=[SCALARS] * len(scalars) +...  6.52 us
    all_to_all x1, waiting for transfers between devices, body(): lax.all_to_all(partial.reshape(blocks, rows, HD), ('core', 'x'), 0, 0, ti...  5.82 us
    ppermute x1, starting transfers between devices, body(): across = lax.ppermute(theirs, 'grp', swap)  4.7 us
    all_gather x1, blocking collectives, body(): values = lax.all_gather(values, 'grp', axis=0)  4.59 us
  transfers between devices with their start and end apart: 9, of which 1 were waited for; matrix products, arithmetic and copies ran while one was open for 2% of the time, Pallas kernels for 4%

profile of v9, /device:TPU:18, one launch (start us, length us, event | category | flops | bytes accessed | tf_op | source)
XLA Modules:
  0.0 112.9 jit_solution(10354038374588103738)
XLA Ops:
  0.6 0.0 copy-start.1
  0.6 1.4 %collective-permute-start.1 = (bf16[128,256]{1,0:T(8,128)(2,1)}, bf16[128,256]{1,0:T(8,128)(2,1)S(1)}, u32[]{:S(2)}, u32[]{:S(2)}) collective-permute-start(bf16[128,256]{1,0:T(8,128)(2,1)} %bitcast.28), channel_id=1, source_target_pairs={{0,512},{1,513},{2,514},{3,515},{4,516},{5,517},{6,518},{7,519},{8... | collective-permute-start | bytes 196616 | tf_op jit(solution)/shard_map/ppermute | solution.py:251
  2.1 0.0 copy-start.6
  2.1 1.0 slice.24
  3.1 0.0 copy-done.1
  3.2 1.3 %collective-permute-start = (bf16[128,1792]{1,0:T(8,128)(2,1)S(1)}, bf16[128,1792]{1,0:T(8,128)(2,1)S(1)}, u32[]{:S(2)}, u32[]{:S(2)}) collective-permute-start(bf16[128,1792]{1,0:T(8,128)(2,1)S(1)} %pad_maximum_fusion), channel_id=1, source_target_pairs={{0,512},{1,513},{2,514},{3,515},{4,516},{5,517},{6,518},{7,519},{8... | collective-permute-start | bytes 1376264 | tf_op jit(solution)/shard_map/ppermute | solution.py:252
  4.5 0.0 copy-done.6
  4.5 0.0 copy-start.2
  4.5 0.8 select_bitcast_fusion
  5.4 0.0 copy-start
  5.4 4.7 %collective-permute-start.2 = (bf16[128,1792]{1,0:T(8,128)(2,1)}, bf16[128,1792]{1,0:T(8,128)(2,1)S(1)}, u32[]{:S(2)}, u32[]{:S(2)}) collective-permute-start(bf16[128,1792]{1,0:T(8,128)(2,1)} %get-tuple-element.22), channel_id=1, source_target_pairs={{0,512},{512,0},{1,513},{513,1},{2,514},{514,2},{3,515},{515,3},{4... | collective-permute-start | bytes 1376264 | tf_op jit(solution)/shard_map/ppermute | solution.py:256
  10.1 0.1 stack.23.place
  10.2 0.0 collective-permute-done.1
  10.2 0.0 copy-done.2
  10.2 26.4 %all_gather.9.k = bf16[2048,128]{1,0:T(8,128)(2,1)S(1)} all-gather(bf16[128,128]{1,0:T(8,128)(2,1)S(1)} %slice_select_fusion), channel_id=1, replica_groups=mesh['grp'=2,'yh'=4,'z'=8,'x'=8,'core'=2] {'x','core'}, dimensions={0}, use_global_device_ids=true | all-gather | bytes 557056 | tf_op jit(solution)/shard_map/all_gather | solution.py:258
  36.6 0.0 collective-permute-done.other
  36.7 0.0 copy-done
  36.7 2.9 %shard_map.94 = bf16[2048,128]{1,0:T(8,128)(2,1)} custom-call(s32[5]{0:T(128)S(1)} %stack.23.place, bf16[128,1792]{1,0:T(8,128)(2,1)S(1)} %bitcast.23, bf16[128,1792]{1,0:T(8,128)(2,1)S(1)} %bitcast.26, bf16[128,1792]{1,0:T(8,128)(2,1)S(1)} %collective-permute-done.other, bf16[2048,128]{1,0:T(8,128)(2,1)S(1)} %all_gather.9.k), custom_call_target="tpu_custom_call" | custom-call | flops 6000000000 | tf_op jit(solution)/shard_map/pallas_call | solution.py:221
  39.6 0.0 collective-permute-done.2.across
  39.6 0.0 copy-start.5
  39.6 6.7 %all-to-all-start = ((bf16[16,128,128]{2,1,0:T(8,128)(2,1)}), bf16[16,128,128]{2,1,0:T(8,128)(2,1)S(1)}, u32[]{:S(2)}, u32[]{:S(2)}) async-start(bf16[16,128,128]{2,1,0:T(8,128)(2,1)} %bitcast.10), calls=%async_computation | async-start | bytes 1048576 | tf_op jit(solution)/shard_map/all_to_all | solution.py:286
  46.3 2.0 %collective-permute-start.6 = (bf16[128,1792]{1,0:T(8,128)(2,1)S(1)}, bf16[128,1792]{1,0:T(8,128)(2,1)S(1)}, u32[]{:S(2)}, u32[]{:S(2)}) collective-permute-start(bf16[128,1792]{1,0:T(8,128)(2,1)S(1)} %get-tuple-element.16.mine), channel_id=1, source_target_pairs={{0,1},{1,0},{2,3},{3,2},{4,5},{5,4},{6,7},{7,6},{8,9},{9,8},{10,11... | collective-permute-start | bytes 1376264 | tf_op jit(solution)/shard_map/ppermute | solution.py:281
  48.3 2.3 %collective-permute-start.7 = (bf16[128,1792]{1,0:T(8,128)(2,1)S(1)}, bf16[128,1792]{1,0:T(8,128)(2,1)S(1)}, u32[]{:S(2)}, u32[]{:S(2)}) collective-permute-start(bf16[128,1792]{1,0:T(8,128)(2,1)S(1)} %collective-permute-done.2.across), channel_id=1, source_target_pairs={{0,1},{1,0},{2,3},{3,2},{4,5},{5,4},{6,7},{7,6},{8,9},{9,8},{10,11... | collective-permute-start | bytes 1376264 | tf_op jit(solution)/shard_map/ppermute | solution.py:282
  50.6 0.0 copy-done.5
  50.6 1.6 %shard_map.96 = (bf16[128,128]{1,0:T(8,128)(2,1)S(1)}, bf16[128,128]{1,0:T(8,128)(2,1)S(1)}) custom-call(s32[5]{0:T(128)S(1)} %stack.23.place, s32[1,128]{1,0:T(1,128)S(1)} %copy-done.5, bf16[128,1792]{1,0:T(8,128)(2,1)S(1)} %bitcast.24, bf16[128,1792]{1,0:T(8,128)(2,1)S(1)} %bitcast.27, bf16[128,256]{1,0:T(8,128)(2,1)S(1)} %bitcast.30), custom_call_target="tpu_custom_call" | custom-call | flops 3000000000 | tf_op jit(solution)/shard_map/pallas_call | solution.py:221
  52.2 1.3 %collective-permute-start.4 = (bf16[128,128]{1,0:T(8,128)(2,1)S(1)}, bf16[128,128]{1,0:T(8,128)(2,1)S(1)}, u32[]{:S(2)}, u32[]{:S(2)}) collective-permute-start(bf16[128,128]{1,0:T(8,128)(2,1)S(1)} %get-tuple-element.14.stay), channel_id=1, source_target_pairs={{512,0},{513,1},{514,2},{515,3},{516,4},{517,5},{518,6},{519,7},{5... | collective-permute-start | bytes 98312 | tf_op jit(solution)/shard_map/ppermute | solution.py:284
  53.5 1.3 %collective-permute-start.5 = (bf16[128,128]{1,0:T(8,128)(2,1)S(1)}, bf16[128,128]{1,0:T(8,128)(2,1)S(1)}, u32[]{:S(2)}, u32[]{:S(2)}) collective-permute-start(bf16[128,128]{1,0:T(8,128)(2,1)S(1)} %get-tuple-element.15), channel_id=1, source_target_pairs={{512,1},{513,0},{514,3},{515,2},{516,5},{517,4},{518,7},{519,6},{5... | collective-permute-start | bytes 98312 | tf_op jit(solution)/shard_map/ppermute | solution.py:285
  54.8 2.1 %collective-permute-start.3 = (bf16[128,128]{1,0:T(8,128)(2,1)S(1)}, bf16[128,128]{1,0:T(8,128)(2,1)S(1)}, u32[]{:S(2)}, u32[]{:S(2)}) collective-permute-start(bf16[128,128]{1,0:T(8,128)(2,1)S(1)} %get-tuple-element.15), channel_id=1, source_target_pairs={{0,1},{1,0},{2,3},{3,2},{4,5},{5,4},{6,7},{7,6},{8,9},{9,8},{10,11... | collective-permute-start | bytes 98312 | tf_op jit(solution)/shard_map/ppermute | solution.py:283
  56.9 5.8 %all-to-all-done.pieces = bf16[16,128,128]{2,1,0:T(8,128)(2,1)S(1)} async-done(((bf16[16,128,128]{2,1,0:T(8,128)(2,1)}), bf16[16,128,128]{2,1,0:T(8,128)(2,1)S(1)}, u32[]{:S(2)}, u32[]{:S(2)}) %all-to-all-start) | async-done | bytes 524320 | tf_op jit(solution)/shard_map/all_to_all | solution.py:286
  62.7 0.1 shard_map.95
  62.8 4.6 %all-gather = bf16[256,128]{1,0:T(8,128)(2,1)S(1)} all-gather(bf16[128,128]{1,0:T(8,128)(2,1)S(1)} %shard_map.95), channel_id=2, replica_groups=mesh['grp'=2,'yh'=4,'z'=8,'x'=8,'core'=2] {'grp'}, dimensions={0}, use_global_device_ids=true | all-gather | bytes 98304 | tf_op jit(solution)/shard_map/all_gather | solution.py:290
  67.3 0.0 collective-permute-done.4.near
  67.4 0.0 collective-permute-done.5.far
  67.4 0.0 collective-permute-done.3.got
  67.4 0.0 collective-permute-done.6.beside
  67.4 0.0 collective-permute-done.7.corner
  67.4 1.2 %shard_map.97 = bf16[4,8,8,896]{3,2,1,0:T(8,128)(2,1)S(1)} custom-call(s32[5]{0:T(128)S(1)} %stack.23.place, bf16[2,128,128]{2,1,0:T(8,128)(2,1)S(1)} %bitcast.21, bf16[128,128]{1,0:T(8,128)(2,1)S(1)} %get-tuple-element.14.stay, bf16[128,128]{1,0:T(8,128)(2,1)S(1)} %collective-permute-done.3.got, bf16[128,128]{1,0:T(8,128)(2,1)S(1)} %collective-permute-done.4.near, ...), custom_call_target="tpu_custom_call" | custom-call | tf_op jit(solution)/shard_map/pallas_call | solution.py:221
  68.5 21.5 %all_to_all.15.pieces = bf16[32,8,896]{2,1,0:T(8,128)(2,1)S(1)} all-to-all(bf16[32,8,896]{2,1,0:T(8,128)(2,1)S(1)} %bitcast.20), channel_id=1, replica_groups=mesh['grp'=2,'yh'=4,'z'=8,'x'=8,'core'=2] {'yh','x'}, dimensions={0} | all-to-all | bytes 917504 | tf_op jit(solution)/shard_map/all_to_all | solution.py:299
  90.1 0.0 copy-start.3
  90.1 0.0 copy-start.4
  90.1 0.1 shard_map.98
  90.2 21.9 %all_to_all.16.pieces = f32[8,8,128]{2,1,0:T(8,128)S(1)} all-to-all(f32[8,8,128]{2,1,0:T(8,128)S(1)} %shard_map.98), channel_id=1, replica_groups=mesh['grp'=2,'yh'=4,'z'=8,'x'=8,'core'=2] {'z'}, dimensions={0} | all-to-all | bytes 65536 | tf_op jit(solution)/shard_map/all_to_all | solution.py:307
  112.2 0.0 copy-done.3
  112.2 0.0 copy-done.4
  112.2 0.7 shard_map.99
  (3 shorter events, 0.1 us)
Async XLA Ops:
  0.6 2.5 %copy-start.1 = (bf16[1,128,1792]{2,1,0:T(8,128)(2,1)S(1)}, bf16[1,128,1792]{2,1,0:T(8,128)(2,1)}, u32[]{:S(2)}) copy-start(bf16[1,128,1792]{2,1,0:T(8,128)(2,1)} %param.10) | copy-start | bytes 1376260
  0.6 9.6 %collective-permute-start.1 = (bf16[128,256]{1,0:T(8,128)(2,1)}, bf16[128,256]{1,0:T(8,128)(2,1)S(1)}, u32[]{:S(2)}, u32[]{:S(2)}) collective-permute-start(bf16[128,256]{1,0:T(8,128)(2,1)} %bitcast.28), channel_id=1, source_target_pairs={{0,512},{1,513},{2,514},{3,515},{4,516},{5,517},{6,518},{7,519},{8... | collective-permute-start | bytes 196616 | tf_op jit(solution)/shard_map/ppermute | solution.py:251
  2.1 2.4 %copy-start.6 = (bf16[1,128,3584]{2,1,0:T(8,128)(2,1)S(1)}, bf16[1,128,3584]{2,1,0:T(8,128)(2,1)}, u32[]{:S(2)}) copy-start(bf16[1,128,3584]{2,1,0:T(8,128)(2,1)} %param.7) | copy-start | bytes 2752516
  3.2 33.4 %collective-permute-start = (bf16[128,1792]{1,0:T(8,128)(2,1)S(1)}, bf16[128,1792]{1,0:T(8,128)(2,1)S(1)}, u32[]{:S(2)}, u32[]{:S(2)}) collective-permute-start(bf16[128,1792]{1,0:T(8,128)(2,1)S(1)} %pad_maximum_fusion), channel_id=1, source_target_pairs={{0,512},{1,513},{2,514},{3,515},{4,516},{5,517},{6,518},{7,519},{8... | collective-permute-start | bytes 1376264 | tf_op jit(solution)/shard_map/ppermute | solution.py:252
  4.5 5.7 %copy-start.2 = (bf16[1,128,256]{2,1,0:T(8,128)(2,1)S(1)}, bf16[1,128,256]{2,1,0:T(8,128)(2,1)}, u32[]{:S(2)}) copy-start(bf16[1,128,256]{2,1,0:T(8,128)(2,1)} %param.9) | copy-start | bytes 196612
  5.4 31.3 %copy-start = (bf16[1,128,1792]{2,1,0:T(8,128)(2,1)S(1)}, bf16[1,128,1792]{2,1,0:T(8,128)(2,1)}, u32[]{:S(2)}) copy-start(bf16[1,128,1792]{2,1,0:T(8,128)(2,1)} %param.8) | copy-start | bytes 1376260
  5.4 34.2 %collective-permute-start.2 = (bf16[128,1792]{1,0:T(8,128)(2,1)}, bf16[128,1792]{1,0:T(8,128)(2,1)S(1)}, u32[]{:S(2)}, u32[]{:S(2)}) collective-permute-start(bf16[128,1792]{1,0:T(8,128)(2,1)} %get-tuple-element.22), channel_id=1, source_target_pairs={{0,512},{512,0},{1,513},{513,1},{2,514},{514,2},{3,515},{515,3},{4... | collective-permute-start | bytes 1376264 | tf_op jit(solution)/shard_map/ppermute | solution.py:256
  39.6 11.1 %copy-start.5 = (s32[1,128]{1,0:T(1,128)S(1)}, s32[1,128]{1,0:T(1,128)}, u32[]{:S(2)}) copy-start(s32[1,128]{1,0:T(1,128)} %begin) | copy-start | bytes 1540
  39.6 23.1 %all-to-all-start = ((bf16[16,128,128]{2,1,0:T(8,128)(2,1)}), bf16[16,128,128]{2,1,0:T(8,128)(2,1)S(1)}, u32[]{:S(2)}, u32[]{:S(2)}) async-start(bf16[16,128,128]{2,1,0:T(8,128)(2,1)} %bitcast.10), calls=%async_computation | async-start | bytes 1048576 | tf_op jit(solution)/shard_map/all_to_all | solution.py:286
  46.3 21.1 %collective-permute-start.6 = (bf16[128,1792]{1,0:T(8,128)(2,1)S(1)}, bf16[128,1792]{1,0:T(8,128)(2,1)S(1)}, u32[]{:S(2)}, u32[]{:S(2)}) collective-permute-start(bf16[128,1792]{1,0:T(8,128)(2,1)S(1)} %get-tuple-element.16.mine), channel_id=1, source_target_pairs={{0,1},{1,0},{2,3},{3,2},{4,5},{5,4},{6,7},{7,6},{8,9},{9,8},{10,11... | collective-permute-start | bytes 1376264 | tf_op jit(solution)/shard_map/ppermute | solution.py:281
  48.3 19.0 %collective-permute-start.7 = (bf16[128,1792]{1,0:T(8,128)(2,1)S(1)}, bf16[128,1792]{1,0:T(8,128)(2,1)S(1)}, u32[]{:S(2)}, u32[]{:S(2)}) collective-permute-start(bf16[128,1792]{1,0:T(8,128)(2,1)S(1)} %collective-permute-done.2.across), channel_id=1, source_target_pairs={{0,1},{1,0},{2,3},{3,2},{4,5},{5,4},{6,7},{7,6},{8,9},{9,8},{10,11... | collective-permute-start | bytes 1376264 | tf_op jit(solution)/shard_map/ppermute | solution.py:282
  52.2 15.2 %collective-permute-start.4 = (bf16[128,128]{1,0:T(8,128)(2,1)S(1)}, bf16[128,128]{1,0:T(8,128)(2,1)S(1)}, u32[]{:S(2)}, u32[]{:S(2)}) collective-permute-start(bf16[128,128]{1,0:T(8,128)(2,1)S(1)} %get-tuple-element.14.stay), channel_id=1, source_target_pairs={{512,0},{513,1},{514,2},{515,3},{516,4},{517,5},{518,6},{519,7},{5... | collective-permute-start | bytes 98312 | tf_op jit(solution)/shard_map/ppermute | solution.py:284
  53.5 13.9 %collective-permute-start.5 = (bf16[128,128]{1,0:T(8,128)(2,1)S(1)}, bf16[128,128]{1,0:T(8,128)(2,1)S(1)}, u32[]{:S(2)}, u32[]{:S(2)}) collective-permute-start(bf16[128,128]{1,0:T(8,128)(2,1)S(1)} %get-tuple-element.15), channel_id=1, source_target_pairs={{512,1},{513,0},{514,3},{515,2},{516,5},{517,4},{518,7},{519,6},{5... | collective-permute-start | bytes 98312 | tf_op jit(solution)/shard_map/ppermute | solution.py:285
  54.8 12.6 %collective-permute-start.3 = (bf16[128,128]{1,0:T(8,128)(2,1)S(1)}, bf16[128,128]{1,0:T(8,128)(2,1)S(1)}, u32[]{:S(2)}, u32[]{:S(2)}) collective-permute-start(bf16[128,128]{1,0:T(8,128)(2,1)S(1)} %get-tuple-element.15), channel_id=1, source_target_pairs={{0,1},{1,0},{2,3},{3,2},{4,5},{5,4},{6,7},{7,6},{8,9},{9,8},{10,11... | collective-permute-start | bytes 98312 | tf_op jit(solution)/shard_map/ppermute | solution.py:283
  90.1 22.1 %copy-start.3 = (f32[56,16]{0,1:T(8,128)S(1)}, f32[56,16]{0,1:T(8,128)}, u32[]{:S(2)}) copy-start(f32[56,16]{0,1:T(8,128)} %param.12) | copy-start | bytes 10756
  90.1 22.1 %copy-start.4 = (f32[56,16]{0,1:T(8,128)S(1)}, f32[56,16]{0,1:T(8,128)}, u32[]{:S(2)}) copy-start(f32[56,16]{0,1:T(8,128)} %param.13) | copy-start | bytes 10756

commit v10 on v8

--- a/solution.py
+++ b/solution.py
@@ -170,7 +170,7 @@
         c = core if j // 2 == 0 else 1 - core
         block = turned[jnp.where(g == 0, c, 2 + j // 2)]
         vg[:, j * rows : (j + 1) * rows] = block.astype(vg.dtype)
-    chips, stripes, depth, span = out.shape
+    stripes, chips, depth, span = out.shape
     span = span // 2
     for t in range(0, stripes, 2):
         part = slice(t * span, (t + 2) * span)
@@ -181,7 +181,7 @@
         for n in range(2):
             piece = block[:, n * span : (n + 1) * span].reshape(chips, 2, depth, span)
             piece = jnp.concatenate([piece[:, 0], piece[:, 1]], axis=-1)
-            out[:, t + n] = piece.astype(out.dtype)
+            out[t + n] = piece.astype(out.dtype)
 
 
 def fold_kernel(owners, pieces, out, total):
@@ -284,13 +284,13 @@
     values = lax.all_gather(values, "grp", axis=0)
     gradient = call(
         project_kernel,
-        shape((chips, stripes, share // 2, 2 * half // stripes), bf16),
+        shape((stripes, chips, share // 2, 2 * half // stripes), bf16),
         [place],
         [values, stay, got, near, far, mine, across, beside, corner],
         [pltpu.VMEM((4, cols // 2, rows), f32), pltpu.VMEM((cols // 2, 4 * rows), bf16)],
     )
     gradient = gradient.reshape(chips * stripes, share // 2, 2 * half // stripes)
-    terms = lax.all_to_all(gradient, ("x", "yh"), 0, 0, tiled=True)
+    terms = lax.all_to_all(gradient, ("yh", "x"), 0, 0, tiled=True)
     sent = call(
         functools.partial(fold_kernel, owners),
         shape((owners, 8, 128), f32),

time: 113 us -> 114 us (level)
  no operation moved by 1% of the time
where the time goes in v10:
time: 114 us; the launch traced here: 113 us
  blocking collectives  76.9 us (67%)
  starting transfers between devices  22.8 us (20%)
  Pallas kernels  5.53 us (5%)
  waiting for transfers between devices  4.8 us (4%)
  local copies, waits for them, and re-layouts  1.18 us (1%)
    all_gather x1, blocking collectives, body(): all_keys = lax.all_gather(chosen, ('x', 'core'), axis=0, tiled=True)  26.4 us
    all_to_all x1, blocking collectives, body(): terms = lax.all_to_all(gradient, ('yh', 'x'), 0, 0, tiled=True)  24.5 us
    all_to_all x1, blocking collectives, body(): landed = lax.all_to_all(sent, 'z', 0, 0, tiled=True)  21.4 us
    all_to_all x1, starting transfers between devices, body(): lax.all_to_all(partial.reshape(blocks, rows, HD), ('x', 'core'), 0, 0, ti...  6.74 us
    pallas_call x6, Pallas kernels, call(): pl.pallas_call(kernel, out_shape=out, in_specs=[SCALARS] * len(scalars) +...  5.53 us
    all_to_all x1, waiting for transfers between devices, body(): lax.all_to_all(partial.reshape(blocks, rows, HD), ('x', 'core'), 0, 0, ti...  4.78 us
    all_gather x1, blocking collectives, body(): values = lax.all_gather(values, 'grp', axis=0)  4.59 us
    ppermute x1, starting transfers between devices, body(): other_k = lax.ppermute(k, 'grp', down)  3.73 us
  transfers between devices with their start and end apart: 9, of which 1 were waited for; matrix products, arithmetic and copies ran while one was open for 2% of the time, Pallas kernels for 3%

profile of v10, /device:TPU:2, one launch (start us, length us, event | category | flops | bytes accessed | tf_op | source)
XLA Modules:
  0.0 112.9 jit_solution(6295231637805763392)
XLA Ops:
  0.6 0.0 copy-start.1
  0.6 3.7 %collective-permute-start.1 = (bf16[128,256]{1,0:T(8,128)(2,1)}, bf16[128,256]{1,0:T(8,128)(2,1)S(1)}, u32[]{:S(2)}, u32[]{:S(2)}) collective-permute-start(bf16[128,256]{1,0:T(8,128)(2,1)} %bitcast.28), channel_id=1, source_target_pairs={{0,512},{1,513},{2,514},{3,515},{4,516},{5,517},{6,518},{7,519},{8... | collective-permute-start | bytes 196616 | tf_op jit(solution)/shard_map/ppermute | solution.py:245
  4.4 0.0 copy-start.6
  4.4 1.0 slice.24
  5.4 0.0 copy-done.1
  5.5 1.3 %collective-permute-start = (bf16[128,1792]{1,0:T(8,128)(2,1)S(1)}, bf16[128,1792]{1,0:T(8,128)(2,1)S(1)}, u32[]{:S(2)}, u32[]{:S(2)}) collective-permute-start(bf16[128,1792]{1,0:T(8,128)(2,1)S(1)} %pad_maximum_fusion), channel_id=1, source_target_pairs={{0,512},{1,513},{2,514},{3,515},{4,516},{5,517},{6,518},{7,519},{8... | collective-permute-start | bytes 1376264 | tf_op jit(solution)/shard_map/ppermute | solution.py:246
  6.8 0.0 copy-done.6
  6.9 0.0 copy-start.2
  6.9 0.8 select_bitcast_fusion
  7.7 0.0 copy-start
  7.7 2.0 %collective-permute-start.2 = (bf16[128,1792]{1,0:T(8,128)(2,1)}, bf16[128,1792]{1,0:T(8,128)(2,1)S(1)}, u32[]{:S(2)}, u32[]{:S(2)}) collective-permute-start(bf16[128,1792]{1,0:T(8,128)(2,1)} %get-tuple-element.22), channel_id=1, source_target_pairs={{0,512},{512,0},{1,513},{513,1},{2,514},{514,2},{3,515},{515,3},{4... | collective-permute-start | bytes 1376264 | tf_op jit(solution)/shard_map/ppermute | solution.py:250
  9.8 0.1 stack.23.place
  9.9 0.0 collective-permute-done.1
  9.9 0.0 copy-done.2
  9.9 26.4 %all_gather.9.k = bf16[2048,128]{1,0:T(8,128)(2,1)S(1)} all-gather(bf16[128,128]{1,0:T(8,128)(2,1)S(1)} %slice_select_fusion), channel_id=1, replica_groups=mesh['grp'=2,'yh'=4,'z'=8,'x'=8,'core'=2] {'x','core'}, dimensions={0}, use_global_device_ids=true | all-gather | bytes 557056 | tf_op jit(solution)/shard_map/all_gather | solution.py:252
  36.3 0.0 collective-permute-done.other
  36.3 0.0 copy-done
  36.3 2.9 %shard_map.94 = bf16[2048,128]{1,0:T(8,128)(2,1)} custom-call(s32[5]{0:T(128)S(1)} %stack.23.place, bf16[128,1792]{1,0:T(8,128)(2,1)S(1)} %bitcast.23, bf16[128,1792]{1,0:T(8,128)(2,1)S(1)} %bitcast.26, bf16[128,1792]{1,0:T(8,128)(2,1)S(1)} %collective-permute-done.other, bf16[2048,128]{1,0:T(8,128)(2,1)S(1)} %all_gather.9.k), custom_call_target="tpu_custom_call" | custom-call | flops 6000000000 | tf_op jit(solution)/shard_map/pallas_call | solution.py:215
  39.2 0.0 collective-permute-done.2.across
  39.2 0.0 copy-start.5
  39.2 6.7 %all-to-all-start = ((bf16[16,128,128]{2,1,0:T(8,128)(2,1)}), bf16[16,128,128]{2,1,0:T(8,128)(2,1)S(1)}, u32[]{:S(2)}, u32[]{:S(2)}) async-start(bf16[16,128,128]{2,1,0:T(8,128)(2,1)} %bitcast.10), calls=%async_computation | async-start | bytes 1048576 | tf_op jit(solution)/shard_map/all_to_all | solution.py:280
  46.0 2.0 %collective-permute-start.6 = (bf16[128,1792]{1,0:T(8,128)(2,1)S(1)}, bf16[128,1792]{1,0:T(8,128)(2,1)S(1)}, u32[]{:S(2)}, u32[]{:S(2)}) collective-permute-start(bf16[128,1792]{1,0:T(8,128)(2,1)S(1)} %get-tuple-element.16.mine), channel_id=1, source_target_pairs={{0,1},{1,0},{2,3},{3,2},{4,5},{5,4},{6,7},{7,6},{8,9},{9,8},{10,11... | collective-permute-start | bytes 1376264 | tf_op jit(solution)/shard_map/ppermute | solution.py:275
  48.0 2.3 %collective-permute-start.7 = (bf16[128,1792]{1,0:T(8,128)(2,1)S(1)}, bf16[128,1792]{1,0:T(8,128)(2,1)S(1)}, u32[]{:S(2)}, u32[]{:S(2)}) collective-permute-start(bf16[128,1792]{1,0:T(8,128)(2,1)S(1)} %collective-permute-done.2.across), channel_id=1, source_target_pairs={{0,1},{1,0},{2,3},{3,2},{4,5},{5,4},{6,7},{7,6},{8,9},{9,8},{10,11... | collective-permute-start | bytes 1376264 | tf_op jit(solution)/shard_map/ppermute | solution.py:276
  50.3 0.0 copy-done.5
  50.3 0.6 shard_map.96
  50.9 1.3 %collective-permute-start.4 = (bf16[128,128]{1,0:T(8,128)(2,1)S(1)}, bf16[128,128]{1,0:T(8,128)(2,1)S(1)}, u32[]{:S(2)}, u32[]{:S(2)}) collective-permute-start(bf16[128,128]{1,0:T(8,128)(2,1)S(1)} %get-tuple-element.14.stay), channel_id=1, source_target_pairs={{512,0},{513,1},{514,2},{515,3},{516,4},{517,5},{518,6},{519,7},{5... | collective-permute-start | bytes 98312 | tf_op jit(solution)/shard_map/ppermute | solution.py:278
  52.2 1.3 %collective-permute-start.5 = (bf16[128,128]{1,0:T(8,128)(2,1)S(1)}, bf16[128,128]{1,0:T(8,128)(2,1)S(1)}, u32[]{:S(2)}, u32[]{:S(2)}) collective-permute-start(bf16[128,128]{1,0:T(8,128)(2,1)S(1)} %get-tuple-element.15), channel_id=1, source_target_pairs={{512,1},{513,0},{514,3},{515,2},{516,5},{517,4},{518,7},{519,6},{5... | collective-permute-start | bytes 98312 | tf_op jit(solution)/shard_map/ppermute | solution.py:279
  53.5 2.1 %collective-permute-start.3 = (bf16[128,128]{1,0:T(8,128)(2,1)S(1)}, bf16[128,128]{1,0:T(8,128)(2,1)S(1)}, u32[]{:S(2)}, u32[]{:S(2)}) collective-permute-start(bf16[128,128]{1,0:T(8,128)(2,1)S(1)} %get-tuple-element.15), channel_id=1, source_target_pairs={{0,1},{1,0},{2,3},{3,2},{4,5},{5,4},{6,7},{7,6},{8,9},{9,8},{10,11... | collective-permute-start | bytes 98312 | tf_op jit(solution)/shard_map/ppermute | solution.py:277
  55.6 4.8 %all-to-all-done.pieces = bf16[16,128,128]{2,1,0:T(8,128)(2,1)S(1)} async-done(((bf16[16,128,128]{2,1,0:T(8,128)(2,1)}), bf16[16,128,128]{2,1,0:T(8,128)(2,1)S(1)}, u32[]{:S(2)}, u32[]{:S(2)}) %all-to-all-start) | async-done | bytes 524320 | tf_op jit(solution)/shard_map/all_to_all | solution.py:280
  60.3 0.1 shard_map.95
  60.4 4.6 %all-gather = bf16[256,128]{1,0:T(8,128)(2,1)S(1)} all-gather(bf16[128,128]{1,0:T(8,128)(2,1)S(1)} %shard_map.95), channel_id=2, replica_groups=mesh['grp'=2,'yh'=4,'z'=8,'x'=8,'core'=2] {'grp'}, dimensions={0}, use_global_device_ids=true | all-gather | bytes 98304 | tf_op jit(solution)/shard_map/all_gather | solution.py:284
  65.0 0.0 collective-permute-done.4.near
  65.0 0.0 collective-permute-done.5.far
  65.0 0.0 collective-permute-done.3.got
  65.0 0.0 collective-permute-done.6.beside
  65.0 0.0 collective-permute-done.7.corner
  65.0 1.2 %shard_map.97 = bf16[4,8,8,896]{3,2,1,0:T(8,128)(2,1)S(1)} custom-call(s32[5]{0:T(128)S(1)} %stack.23.place, bf16[2,128,128]{2,1,0:T(8,128)(2,1)S(1)} %bitcast.21, bf16[128,128]{1,0:T(8,128)(2,1)S(1)} %get-tuple-element.14.stay, bf16[128,128]{1,0:T(8,128)(2,1)S(1)} %collective-permute-done.3.got, bf16[128,128]{1,0:T(8,128)(2,1)S(1)} %collective-permute-done.4.near, ...), custom_call_target="tpu_custom_call" | custom-call | tf_op jit(solution)/shard_map/pallas_call | solution.py:215
  66.2 24.5 %all_to_all.15.pieces = bf16[32,8,896]{2,1,0:T(8,128)(2,1)S(1)} all-to-all(bf16[32,8,896]{2,1,0:T(8,128)(2,1)S(1)} %bitcast.20), channel_id=1, replica_groups=mesh['grp'=2,'yh'=4,'z'=8,'x'=8,'core'=2] {'yh','x'}, dimensions={0} | all-to-all | bytes 917504 | tf_op jit(solution)/shard_map/all_to_all | solution.py:293
  90.7 0.0 copy-start.3
  90.7 0.0 copy-start.4
  90.7 0.1 shard_map.98
  90.9 21.4 %all_to_all.16.pieces = f32[8,8,128]{2,1,0:T(8,128)S(1)} all-to-all(f32[8,8,128]{2,1,0:T(8,128)S(1)} %shard_map.98), channel_id=1, replica_groups=mesh['grp'=2,'yh'=4,'z'=8,'x'=8,'core'=2] {'z'}, dimensions={0} | all-to-all | bytes 65536 | tf_op jit(solution)/shard_map/all_to_all | solution.py:301
  112.2 0.0 copy-done.3
  112.2 0.0 copy-done.4
  112.2 0.7 shard_map.99
  (3 shorter events, 0.1 us)
Async XLA Ops:
  0.6 4.8 %copy-start.1 = (bf16[1,128,1792]{2,1,0:T(8,128)(2,1)S(1)}, bf16[1,128,1792]{2,1,0:T(8,128)(2,1)}, u32[]{:S(2)}) copy-start(bf16[1,128,1792]{2,1,0:T(8,128)(2,1)} %param.10) | copy-start | bytes 1376260
  0.6 9.2 %collective-permute-start.1 = (bf16[128,256]{1,0:T(8,128)(2,1)}, bf16[128,256]{1,0:T(8,128)(2,1)S(1)}, u32[]{:S(2)}, u32[]{:S(2)}) collective-permute-start(bf16[128,256]{1,0:T(8,128)(2,1)} %bitcast.28), channel_id=1, source_target_pairs={{0,512},{1,513},{2,514},{3,515},{4,516},{5,517},{6,518},{7,519},{8... | collective-permute-start | bytes 196616 | tf_op jit(solution)/shard_map/ppermute | solution.py:245
  4.4 2.5 %copy-start.6 = (bf16[1,128,3584]{2,1,0:T(8,128)(2,1)S(1)}, bf16[1,128,3584]{2,1,0:T(8,128)(2,1)}, u32[]{:S(2)}) copy-start(bf16[1,128,3584]{2,1,0:T(8,128)(2,1)} %param.7) | copy-start | bytes 2752516
  5.5 30.8 %collective-permute-start = (bf16[128,1792]{1,0:T(8,128)(2,1)S(1)}, bf16[128,1792]{1,0:T(8,128)(2,1)S(1)}, u32[]{:S(2)}, u32[]{:S(2)}) collective-permute-start(bf16[128,1792]{1,0:T(8,128)(2,1)S(1)} %pad_maximum_fusion), channel_id=1, source_target_pairs={{0,512},{1,513},{2,514},{3,515},{4,516},{5,517},{6,518},{7,519},{8... | collective-permute-start | bytes 1376264 | tf_op jit(solution)/shard_map/ppermute | solution.py:246
  6.9 3.0 %copy-start.2 = (bf16[1,128,256]{2,1,0:T(8,128)(2,1)S(1)}, bf16[1,128,256]{2,1,0:T(8,128)(2,1)}, u32[]{:S(2)}) copy-start(bf16[1,128,256]{2,1,0:T(8,128)(2,1)} %param.9) | copy-start | bytes 196612
  7.7 28.6 %copy-start = (bf16[1,128,1792]{2,1,0:T(8,128)(2,1)S(1)}, bf16[1,128,1792]{2,1,0:T(8,128)(2,1)}, u32[]{:S(2)}) copy-start(bf16[1,128,1792]{2,1,0:T(8,128)(2,1)} %param.8) | copy-start | bytes 1376260
  7.7 31.5 %collective-permute-start.2 = (bf16[128,1792]{1,0:T(8,128)(2,1)}, bf16[128,1792]{1,0:T(8,128)(2,1)S(1)}, u32[]{:S(2)}, u32[]{:S(2)}) collective-permute-start(bf16[128,1792]{1,0:T(8,128)(2,1)} %get-tuple-element.22), channel_id=1, source_target_pairs={{0,512},{512,0},{1,513},{513,1},{2,514},{514,2},{3,515},{515,3},{4... | collective-permute-start | bytes 1376264 | tf_op jit(solution)/shard_map/ppermute | solution.py:250
  39.2 11.1 %copy-start.5 = (s32[1,128]{1,0:T(1,128)S(1)}, s32[1,128]{1,0:T(1,128)}, u32[]{:S(2)}) copy-start(s32[1,128]{1,0:T(1,128)} %begin) | copy-start | bytes 1540
  39.2 21.1 %all-to-all-start = ((bf16[16,128,128]{2,1,0:T(8,128)(2,1)}), bf16[16,128,128]{2,1,0:T(8,128)(2,1)S(1)}, u32[]{:S(2)}, u32[]{:S(2)}) async-start(bf16[16,128,128]{2,1,0:T(8,128)(2,1)} %bitcast.10), calls=%async_computation | async-start | bytes 1048576 | tf_op jit(solution)/shard_map/all_to_all | solution.py:280
  46.0 19.0 %collective-permute-start.6 = (bf16[128,1792]{1,0:T(8,128)(2,1)S(1)}, bf16[128,1792]{1,0:T(8,128)(2,1)S(1)}, u32[]{:S(2)}, u32[]{:S(2)}) collective-permute-start(bf16[128,1792]{1,0:T(8,128)(2,1)S(1)} %get-tuple-element.16.mine), channel_id=1, source_target_pairs={{0,1},{1,0},{2,3},{3,2},{4,5},{5,4},{6,7},{7,6},{8,9},{9,8},{10,11... | collective-permute-start | bytes 1376264 | tf_op jit(solution)/shard_map/ppermute | solution.py:275
  48.0 17.0 %collective-permute-start.7 = (bf16[128,1792]{1,0:T(8,128)(2,1)S(1)}, bf16[128,1792]{1,0:T(8,128)(2,1)S(1)}, u32[]{:S(2)}, u32[]{:S(2)}) collective-permute-start(bf16[128,1792]{1,0:T(8,128)(2,1)S(1)} %collective-permute-done.2.across), channel_id=1, source_target_pairs={{0,1},{1,0},{2,3},{3,2},{4,5},{5,4},{6,7},{7,6},{8,9},{9,8},{10,11... | collective-permute-start | bytes 1376264 | tf_op jit(solution)/shard_map/ppermute | solution.py:276
  50.9 14.1 %collective-permute-start.4 = (bf16[128,128]{1,0:T(8,128)(2,1)S(1)}, bf16[128,128]{1,0:T(8,128)(2,1)S(1)}, u32[]{:S(2)}, u32[]{:S(2)}) collective-permute-start(bf16[128,128]{1,0:T(8,128)(2,1)S(1)} %get-tuple-element.14.stay), channel_id=1, source_target_pairs={{512,0},{513,1},{514,2},{515,3},{516,4},{517,5},{518,6},{519,7},{5... | collective-permute-start | bytes 98312 | tf_op jit(solution)/shard_map/ppermute | solution.py:278
  52.2 12.8 %collective-permute-start.5 = (bf16[128,128]{1,0:T(8,128)(2,1)S(1)}, bf16[128,128]{1,0:T(8,128)(2,1)S(1)}, u32[]{:S(2)}, u32[]{:S(2)}) collective-permute-start(bf16[128,128]{1,0:T(8,128)(2,1)S(1)} %get-tuple-element.15), channel_id=1, source_target_pairs={{512,1},{513,0},{514,3},{515,2},{516,5},{517,4},{518,7},{519,6},{5... | collective-permute-start | bytes 98312 | tf_op jit(solution)/shard_map/ppermute | solution.py:279
  53.5 11.5 %collective-permute-start.3 = (bf16[128,128]{1,0:T(8,128)(2,1)S(1)}, bf16[128,128]{1,0:T(8,128)(2,1)S(1)}, u32[]{:S(2)}, u32[]{:S(2)}) collective-permute-start(bf16[128,128]{1,0:T(8,128)(2,1)S(1)} %get-tuple-element.15), channel_id=1, source_target_pairs={{0,1},{1,0},{2,3},{3,2},{4,5},{5,4},{6,7},{7,6},{8,9},{9,8},{10,11... | collective-permute-start | bytes 98312 | tf_op jit(solution)/shard_map/ppermute | solution.py:277
  90.7 21.5 %copy-start.3 = (f32[56,16]{0,1:T(8,128)S(1)}, f32[56,16]{0,1:T(8,128)}, u32[]{:S(2)}) copy-start(f32[56,16]{0,1:T(8,128)} %param.12) | copy-start | bytes 10756
  90.7 21.5 %copy-start.4 = (f32[56,16]{0,1:T(8,128)S(1)}, f32[56,16]{0,1:T(8,128)}, u32[]{:S(2)}) copy-start(f32[56,16]{0,1:T(8,128)} %param.13) | copy-start | bytes 10756

commit v11 on v8

--- a/solution.py
+++ b/solution.py
@@ -249,7 +249,7 @@
     theirs = jnp.where(group == 0, upper, lower)
     across = lax.ppermute(theirs, "grp", swap)
     chosen = jnp.where(group == 0, k[:, :HD], other_k[:, HD:])
-    all_keys = lax.all_gather(chosen, ("x", "core"), axis=0, tiled=True)
+    all_keys = lax.all_gather(chosen, ("x", "core"), axis=0).reshape(seq, HD)
     partial = call(
         functools.partial(long_kernel, share),
         shape((seq, HD), bf16),

time: 113 us -> 113 us (level)
  the two profiles are of different devices: /device:TPU:2 before, /device:TPU:18 now
where the time goes in v11:
time: 113 us; the launch traced here: 112 us
  blocking collectives  76.2 us (67%)
  starting transfers between devices  23.1 us (20%)
  Pallas kernels  6.52 us (6%)
  waiting for transfers between devices  3.82 us (3%)
  local copies, waits for them, and re-layouts  1.18 us (1%)
    all_gather x1, blocking collectives, body(): all_keys = lax.all_gather(chosen, ('x', 'core'), axis=0).reshape(seq, HD)  26.4 us
    all_to_all x1, blocking collectives, body(): terms = lax.all_to_all(gradient, ('x', 'yh'), 0, 0, tiled=True)  23.8 us
    all_to_all x1, blocking collectives, body(): landed = lax.all_to_all(sent, 'z', 0, 0, tiled=True)  21.3 us
    all_to_all x1, starting transfers between devices, body(): lax.all_to_all(partial.reshape(blocks, rows, HD), ('x', 'core'), 0, 0, ti...  6.73 us
    pallas_call x6, Pallas kernels, call(): pl.pallas_call(kernel, out_shape=out, in_specs=[SCALARS] * len(scalars) +...  6.52 us
    ppermute x1, starting transfers between devices, body(): across = lax.ppermute(theirs, 'grp', swap)  4.7 us
    all_gather x1, blocking collectives, body(): values = lax.all_gather(values, 'grp', axis=0)  4.59 us
    all_to_all x1, waiting for transfers between devices, body(): lax.all_to_all(partial.reshape(blocks, rows, HD), ('x', 'core'), 0, 0, ti...  3.8 us
  transfers between devices with their start and end apart: 9, of which 1 were waited for; matrix products, arithmetic and copies ran while one was open for 2% of the time, Pallas kernels for 4%

profile of v11, /device:TPU:18, one launch (start us, length us, event | category | flops | bytes accessed | tf_op | source)
XLA Modules:
  0.0 112.5 jit_solution(8446942074384238694)
XLA Ops:
  0.6 0.0 copy-start.1
  0.6 1.4 %collective-permute-start.1 = (bf16[128,256]{1,0:T(8,128)(2,1)}, bf16[128,256]{1,0:T(8,128)(2,1)S(1)}, u32[]{:S(2)}, u32[]{:S(2)}) collective-permute-start(bf16[128,256]{1,0:T(8,128)(2,1)} %bitcast.28), channel_id=1, source_target_pairs={{0,512},{1,513},{2,514},{3,515},{4,516},{5,517},{6,518},{7,519},{8... | collective-permute-start | bytes 196616 | tf_op jit(solution)/shard_map/ppermute | solution.py:245
  2.1 0.0 copy-start.6
  2.1 1.0 slice.24
  3.1 0.0 copy-done.1
  3.2 1.3 %collective-permute-start = (bf16[128,1792]{1,0:T(8,128)(2,1)S(1)}, bf16[128,1792]{1,0:T(8,128)(2,1)S(1)}, u32[]{:S(2)}, u32[]{:S(2)}) collective-permute-start(bf16[128,1792]{1,0:T(8,128)(2,1)S(1)} %pad_maximum_fusion), channel_id=1, source_target_pairs={{0,512},{1,513},{2,514},{3,515},{4,516},{5,517},{6,518},{7,519},{8... | collective-permute-start | bytes 1376264 | tf_op jit(solution)/shard_map/ppermute | solution.py:246
  4.5 0.0 copy-done.6
  4.5 0.0 copy-start.2
  4.5 0.8 select_bitcast_fusion
  5.4 0.0 copy-start
  5.4 4.7 %collective-permute-start.2 = (bf16[128,1792]{1,0:T(8,128)(2,1)}, bf16[128,1792]{1,0:T(8,128)(2,1)S(1)}, u32[]{:S(2)}, u32[]{:S(2)}) collective-permute-start(bf16[128,1792]{1,0:T(8,128)(2,1)} %get-tuple-element.22), channel_id=1, source_target_pairs={{0,512},{512,0},{1,513},{513,1},{2,514},{514,2},{3,515},{515,3},{4... | collective-permute-start | bytes 1376264 | tf_op jit(solution)/shard_map/ppermute | solution.py:250
  10.1 0.1 stack.23.place
  10.2 0.0 collective-permute-done.1
  10.2 0.0 copy-done.2
  10.2 26.4 %all-gather.k = bf16[2048,128]{1,0:T(8,128)(2,1)S(1)} all-gather(bf16[128,128]{1,0:T(8,128)(2,1)S(1)} %slice_select_fusion), channel_id=2, replica_groups=mesh['grp'=2,'yh'=4,'z'=8,'x'=8,'core'=2] {'x','core'}, dimensions={0}, use_global_device_ids=true | all-gather | bytes 557056 | tf_op jit(solution)/shard_map/all_gather | solution.py:252
  36.6 0.0 collective-permute-done.other
  36.7 0.0 copy-done
  36.7 2.9 %shard_map.94 = bf16[2048,128]{1,0:T(8,128)(2,1)} custom-call(s32[5]{0:T(128)S(1)} %stack.23.place, bf16[128,1792]{1,0:T(8,128)(2,1)S(1)} %bitcast.23, bf16[128,1792]{1,0:T(8,128)(2,1)S(1)} %bitcast.26, bf16[128,1792]{1,0:T(8,128)(2,1)S(1)} %collective-permute-done.other, bf16[2048,128]{1,0:T(8,128)(2,1)S(1)} %all-gather.k), custom_call_target="tpu_custom_call" | custom-call | flops 6000000000 | tf_op jit(solution)/shard_map/pallas_call | solution.py:215
  39.6 0.0 collective-permute-done.2.across
  39.6 0.0 copy-start.5
  39.6 6.7 %all-to-all-start = ((bf16[16,128,128]{2,1,0:T(8,128)(2,1)}), bf16[16,128,128]{2,1,0:T(8,128)(2,1)S(1)}, u32[]{:S(2)}, u32[]{:S(2)}) async-start(bf16[16,128,128]{2,1,0:T(8,128)(2,1)} %bitcast.10), calls=%async_computation | async-start | bytes 1048576 | tf_op jit(solution)/shard_map/all_to_all | solution.py:280
  46.3 2.0 %collective-permute-start.6 = (bf16[128,1792]{1,0:T(8,128)(2,1)S(1)}, bf16[128,1792]{1,0:T(8,128)(2,1)S(1)}, u32[]{:S(2)}, u32[]{:S(2)}) collective-permute-start(bf16[128,1792]{1,0:T(8,128)(2,1)S(1)} %get-tuple-element.16.mine), channel_id=1, source_target_pairs={{0,1},{1,0},{2,3},{3,2},{4,5},{5,4},{6,7},{7,6},{8,9},{9,8},{10,11... | collective-permute-start | bytes 1376264 | tf_op jit(solution)/shard_map/ppermute | solution.py:275
  48.3 2.3 %collective-permute-start.7 = (bf16[128,1792]{1,0:T(8,128)(2,1)S(1)}, bf16[128,1792]{1,0:T(8,128)(2,1)S(1)}, u32[]{:S(2)}, u32[]{:S(2)}) collective-permute-start(bf16[128,1792]{1,0:T(8,128)(2,1)S(1)} %collective-permute-done.2.across), channel_id=1, source_target_pairs={{0,1},{1,0},{2,3},{3,2},{4,5},{5,4},{6,7},{7,6},{8,9},{9,8},{10,11... | collective-permute-start | bytes 1376264 | tf_op jit(solution)/shard_map/ppermute | solution.py:276
  50.6 0.0 copy-done.5
  50.6 1.6 %shard_map.96 = (bf16[128,128]{1,0:T(8,128)(2,1)S(1)}, bf16[128,128]{1,0:T(8,128)(2,1)S(1)}) custom-call(s32[5]{0:T(128)S(1)} %stack.23.place, s32[1,128]{1,0:T(1,128)S(1)} %copy-done.5, bf16[128,1792]{1,0:T(8,128)(2,1)S(1)} %bitcast.24, bf16[128,1792]{1,0:T(8,128)(2,1)S(1)} %bitcast.27, bf16[128,256]{1,0:T(8,128)(2,1)S(1)} %bitcast.30), custom_call_target="tpu_custom_call" | custom-call | flops 3000000000 | tf_op jit(solution)/shard_map/pallas_call | solution.py:215
  52.2 1.3 %collective-permute-start.4 = (bf16[128,128]{1,0:T(8,128)(2,1)S(1)}, bf16[128,128]{1,0:T(8,128)(2,1)S(1)}, u32[]{:S(2)}, u32[]{:S(2)}) collective-permute-start(bf16[128,128]{1,0:T(8,128)(2,1)S(1)} %get-tuple-element.14.stay), channel_id=1, source_target_pairs={{512,0},{513,1},{514,2},{515,3},{516,4},{517,5},{518,6},{519,7},{5... | collective-permute-start | bytes 98312 | tf_op jit(solution)/shard_map/ppermute | solution.py:278
  53.5 1.3 %collective-permute-start.5 = (bf16[128,128]{1,0:T(8,128)(2,1)S(1)}, bf16[128,128]{1,0:T(8,128)(2,1)S(1)}, u32[]{:S(2)}, u32[]{:S(2)}) collective-permute-start(bf16[128,128]{1,0:T(8,128)(2,1)S(1)} %get-tuple-element.15), channel_id=1, source_target_pairs={{512,1},{513,0},{514,3},{515,2},{516,5},{517,4},{518,7},{519,6},{5... | collective-permute-start | bytes 98312 | tf_op jit(solution)/shard_map/ppermute | solution.py:279
  54.8 2.1 %collective-permute-start.3 = (bf16[128,128]{1,0:T(8,128)(2,1)S(1)}, bf16[128,128]{1,0:T(8,128)(2,1)S(1)}, u32[]{:S(2)}, u32[]{:S(2)}) collective-permute-start(bf16[128,128]{1,0:T(8,128)(2,1)S(1)} %get-tuple-element.15), channel_id=1, source_target_pairs={{0,1},{1,0},{2,3},{3,2},{4,5},{5,4},{6,7},{7,6},{8,9},{9,8},{10,11... | collective-permute-start | bytes 98312 | tf_op jit(solution)/shard_map/ppermute | solution.py:277
  56.9 3.8 %all-to-all-done.pieces = bf16[16,128,128]{2,1,0:T(8,128)(2,1)S(1)} async-done(((bf16[16,128,128]{2,1,0:T(8,128)(2,1)}), bf16[16,128,128]{2,1,0:T(8,128)(2,1)S(1)}, u32[]{:S(2)}, u32[]{:S(2)}) %all-to-all-start) | async-done | bytes 524320 | tf_op jit(solution)/shard_map/all_to_all | solution.py:280
  60.7 0.1 shard_map.95
  60.7 4.6 %all-gather.1 = bf16[256,128]{1,0:T(8,128)(2,1)S(1)} all-gather(bf16[128,128]{1,0:T(8,128)(2,1)S(1)} %shard_map.95), channel_id=3, replica_groups=mesh['grp'=2,'yh'=4,'z'=8,'x'=8,'core'=2] {'grp'}, dimensions={0}, use_global_device_ids=true | all-gather | bytes 98304 | tf_op jit(solution)/shard_map/all_gather | solution.py:284
  65.3 0.0 collective-permute-done.4.near
  65.3 0.0 collective-permute-done.5.far
  65.3 0.0 collective-permute-done.3.got
  65.3 0.0 collective-permute-done.6.beside
  65.3 0.0 collective-permute-done.7.corner
  65.4 1.2 %shard_map.97 = bf16[8,4,8,896]{3,2,1,0:T(8,128)(2,1)S(1)} custom-call(s32[5]{0:T(128)S(1)} %stack.23.place, bf16[2,128,128]{2,1,0:T(8,128)(2,1)S(1)} %bitcast.21, bf16[128,128]{1,0:T(8,128)(2,1)S(1)} %get-tuple-element.14.stay, bf16[128,128]{1,0:T(8,128)(2,1)S(1)} %collective-permute-done.3.got, bf16[128,128]{1,0:T(8,128)(2,1)S(1)} %collective-permute-done.4.near, ...), custom_call_target="tpu_custom_call" | custom-call | tf_op jit(solution)/shard_map/pallas_call | solution.py:215
  66.5 23.8 %all_to_all.15.pieces = bf16[32,8,896]{2,1,0:T(8,128)(2,1)S(1)} all-to-all(bf16[32,8,896]{2,1,0:T(8,128)(2,1)S(1)} %bitcast.20), channel_id=1, replica_groups=mesh['grp'=2,'yh'=4,'z'=8,'x'=8,'core'=2] {'x','yh'}, dimensions={0} | all-to-all | bytes 917504 | tf_op jit(solution)/shard_map/all_to_all | solution.py:293
  90.3 0.0 copy-start.3
  90.3 0.0 copy-start.4
  90.3 0.1 shard_map.98
  90.5 21.3 %all_to_all.16.pieces = f32[8,8,128]{2,1,0:T(8,128)S(1)} all-to-all(f32[8,8,128]{2,1,0:T(8,128)S(1)} %shard_map.98), channel_id=1, replica_groups=mesh['grp'=2,'yh'=4,'z'=8,'x'=8,'core'=2] {'z'}, dimensions={0} | all-to-all | bytes 65536 | tf_op jit(solution)/shard_map/all_to_all | solution.py:301
  111.8 0.0 copy-done.3
  111.8 0.0 copy-done.4
  111.8 0.7 shard_map.99
  (3 shorter events, 0.1 us)
Async XLA Ops:
  0.6 2.5 %copy-start.1 = (bf16[1,128,1792]{2,1,0:T(8,128)(2,1)S(1)}, bf16[1,128,1792]{2,1,0:T(8,128)(2,1)}, u32[]{:S(2)}) copy-start(bf16[1,128,1792]{2,1,0:T(8,128)(2,1)} %param.10) | copy-start | bytes 1376260
  0.6 9.6 %collective-permute-start.1 = (bf16[128,256]{1,0:T(8,128)(2,1)}, bf16[128,256]{1,0:T(8,128)(2,1)S(1)}, u32[]{:S(2)}, u32[]{:S(2)}) collective-permute-start(bf16[128,256]{1,0:T(8,128)(2,1)} %bitcast.28), channel_id=1, source_target_pairs={{0,512},{1,513},{2,514},{3,515},{4,516},{5,517},{6,518},{7,519},{8... | collective-permute-start | bytes 196616 | tf_op jit(solution)/shard_map/ppermute | solution.py:245
  2.1 2.4 %copy-start.6 = (bf16[1,128,3584]{2,1,0:T(8,128)(2,1)S(1)}, bf16[1,128,3584]{2,1,0:T(8,128)(2,1)}, u32[]{:S(2)}) copy-start(bf16[1,128,3584]{2,1,0:T(8,128)(2,1)} %param.7) | copy-start | bytes 2752516
  3.2 33.4 %collective-permute-start = (bf16[128,1792]{1,0:T(8,128)(2,1)S(1)}, bf16[128,1792]{1,0:T(8,128)(2,1)S(1)}, u32[]{:S(2)}, u32[]{:S(2)}) collective-permute-start(bf16[128,1792]{1,0:T(8,128)(2,1)S(1)} %pad_maximum_fusion), channel_id=1, source_target_pairs={{0,512},{1,513},{2,514},{3,515},{4,516},{5,517},{6,518},{7,519},{8... | collective-permute-start | bytes 1376264 | tf_op jit(solution)/shard_map/ppermute | solution.py:246
  4.5 5.7 %copy-start.2 = (bf16[1,128,256]{2,1,0:T(8,128)(2,1)S(1)}, bf16[1,128,256]{2,1,0:T(8,128)(2,1)}, u32[]{:S(2)}) copy-start(bf16[1,128,256]{2,1,0:T(8,128)(2,1)} %param.9) | copy-start | bytes 196612
  5.4 31.3 %copy-start = (bf16[1,128,1792]{2,1,0:T(8,128)(2,1)S(1)}, bf16[1,128,1792]{2,1,0:T(8,128)(2,1)}, u32[]{:S(2)}) copy-start(bf16[1,128,1792]{2,1,0:T(8,128)(2,1)} %param.8) | copy-start | bytes 1376260
  5.4 34.2 %collective-permute-start.2 = (bf16[128,1792]{1,0:T(8,128)(2,1)}, bf16[128,1792]{1,0:T(8,128)(2,1)S(1)}, u32[]{:S(2)}, u32[]{:S(2)}) collective-permute-start(bf16[128,1792]{1,0:T(8,128)(2,1)} %get-tuple-element.22), channel_id=1, source_target_pairs={{0,512},{512,0},{1,513},{513,1},{2,514},{514,2},{3,515},{515,3},{4... | collective-permute-start | bytes 1376264 | tf_op jit(solution)/shard_map/ppermute | solution.py:250
  39.6 11.1 %copy-start.5 = (s32[1,128]{1,0:T(1,128)S(1)}, s32[1,128]{1,0:T(1,128)}, u32[]{:S(2)}) copy-start(s32[1,128]{1,0:T(1,128)} %begin) | copy-start | bytes 1540
  39.6 21.1 %all-to-all-start = ((bf16[16,128,128]{2,1,0:T(8,128)(2,1)}), bf16[16,128,128]{2,1,0:T(8,128)(2,1)S(1)}, u32[]{:S(2)}, u32[]{:S(2)}) async-start(bf16[16,128,128]{2,1,0:T(8,128)(2,1)} %bitcast.10), calls=%async_computation | async-start | bytes 1048576 | tf_op jit(solution)/shard_map/all_to_all | solution.py:280
  46.3 19.0 %collective-permute-start.6 = (bf16[128,1792]{1,0:T(8,128)(2,1)S(1)}, bf16[128,1792]{1,0:T(8,128)(2,1)S(1)}, u32[]{:S(2)}, u32[]{:S(2)}) collective-permute-start(bf16[128,1792]{1,0:T(8,128)(2,1)S(1)} %get-tuple-element.16.mine), channel_id=1, source_target_pairs={{0,1},{1,0},{2,3},{3,2},{4,5},{5,4},{6,7},{7,6},{8,9},{9,8},{10,11... | collective-permute-start | bytes 1376264 | tf_op jit(solution)/shard_map/ppermute | solution.py:275
  48.3 17.0 %collective-permute-start.7 = (bf16[128,1792]{1,0:T(8,128)(2,1)S(1)}, bf16[128,1792]{1,0:T(8,128)(2,1)S(1)}, u32[]{:S(2)}, u32[]{:S(2)}) collective-permute-start(bf16[128,1792]{1,0:T(8,128)(2,1)S(1)} %collective-permute-done.2.across), channel_id=1, source_target_pairs={{0,1},{1,0},{2,3},{3,2},{4,5},{5,4},{6,7},{7,6},{8,9},{9,8},{10,11... | collective-permute-start | bytes 1376264 | tf_op jit(solution)/shard_map/ppermute | solution.py:276
  52.2 13.1 %collective-permute-start.4 = (bf16[128,128]{1,0:T(8,128)(2,1)S(1)}, bf16[128,128]{1,0:T(8,128)(2,1)S(1)}, u32[]{:S(2)}, u32[]{:S(2)}) collective-permute-start(bf16[128,128]{1,0:T(8,128)(2,1)S(1)} %get-tuple-element.14.stay), channel_id=1, source_target_pairs={{512,0},{513,1},{514,2},{515,3},{516,4},{517,5},{518,6},{519,7},{5... | collective-permute-start | bytes 98312 | tf_op jit(solution)/shard_map/ppermute | solution.py:278
  53.5 11.8 %collective-permute-start.5 = (bf16[128,128]{1,0:T(8,128)(2,1)S(1)}, bf16[128,128]{1,0:T(8,128)(2,1)S(1)}, u32[]{:S(2)}, u32[]{:S(2)}) collective-permute-start(bf16[128,128]{1,0:T(8,128)(2,1)S(1)} %get-tuple-element.15), channel_id=1, source_target_pairs={{512,1},{513,0},{514,3},{515,2},{516,5},{517,4},{518,7},{519,6},{5... | collective-permute-start | bytes 98312 | tf_op jit(solution)/shard_map/ppermute | solution.py:279
  54.8 10.5 %collective-permute-start.3 = (bf16[128,128]{1,0:T(8,128)(2,1)S(1)}, bf16[128,128]{1,0:T(8,128)(2,1)S(1)}, u32[]{:S(2)}, u32[]{:S(2)}) collective-permute-start(bf16[128,128]{1,0:T(8,128)(2,1)S(1)} %get-tuple-element.15), channel_id=1, source_target_pairs={{0,1},{1,0},{2,3},{3,2},{4,5},{5,4},{6,7},{7,6},{8,9},{9,8},{10,11... | collective-permute-start | bytes 98312 | tf_op jit(solution)/shard_map/ppermute | solution.py:277
  90.3 21.5 %copy-start.3 = (f32[56,16]{0,1:T(8,128)S(1)}, f32[56,16]{0,1:T(8,128)}, u32[]{:S(2)}) copy-start(f32[56,16]{0,1:T(8,128)} %param.12) | copy-start | bytes 10756
  90.3 21.5 %copy-start.4 = (f32[56,16]{0,1:T(8,128)S(1)}, f32[56,16]{0,1:T(8,128)}, u32[]{:S(2)}) copy-start(f32[56,16]{0,1:T(8,128)} %param.13) | copy-start | bytes 10756
